TPU v7x, 32 devices: a whole 2x2x4 slice. The times are simulated.
32 devices in a mesh: section: 4 (over y, core), expert: 8 (over z, x).
Axes of the slice: x: 2, y: 2, z: 4, core: 2. Of those that a mesh axis runs over, the one named last changes fastest.
Arguments:
- tokens: bfloat16 [4, 512, 2560], P('section', 'expert'), may hold values from -6 to 6
- norm_gain: float32 [4, 2560], P('section'), may hold values from 0.25 to 1.75
- w_gate: bfloat16 [4, 8, 2560, 192], P('section', 'expert'), may hold values from -0.125 to 0.125
- w_up: bfloat16 [4, 8, 2560, 192], P('section', 'expert'), may hold values from -0.125 to 0.125
- w_down: bfloat16 [4, 8, 192, 2560], P('section', 'expert'), may hold values from -0.21875 to 0.21875
- routes: int32 [4, 2, 512, 1], P('section', None, 'expert'), may hold values from 0 to 1; in each aligned block of 64 rows (0 to 63, 64 to 127, ..., all dimensions but the last counted through in order) at most 34 rows name the same one
- mix_weights: float32 [4, 2, 512, 1], P('section', None, 'expert'), may hold values from 0.1 to 1
- cotangent: bfloat16 [4, 512, 2560], P('section', 'expert'), may hold values from -6 to 6
Outputs:
- final: bfloat16 [4, 512, 2560], P('section', 'expert')
- input_grads: bfloat16 [4, 512, 2560], P('section', 'expert')
Inputs may be any that keep to these rules, and one draw needn't show every extreme that they name: `routes`: the 1 ids of a token differ. In the rows of one device (aligned blocks of 64 tokens of one layer and step) no id is named by more than 34 tokens, a bound that some block reaches.
All inputs are finite; a program needn't handle non-finite values.
Results may differ from a plain program's by a relative error of at most 0.011.
Values may be sent and summed in bfloat16 or wider, within the bound.
No kernel may reach another device: no remote copies, remote signals or barrier semaphores. Data moves between devices by JAX's collectives and lax.ppermute only.
A program may use at most 64 MiB of HBM per device.

v0:
```python
import functools

import jax
import jax.numpy as jnp
from jax import lax
from jax.experimental import pallas as pl
from jax.experimental.pallas import tpu as pltpu
from jax.sharding import PartitionSpec as P

SPLIT = 4
EPSILON = 1e-06
BF = jnp.bfloat16
F32 = jnp.float32
ROWS = 16
LANES = 128


def dot(left, right, dims=((1,), (0,))):
    return lax.dot_general(left, right, (dims, ((), ())), preferred_element_type=F32)


NT = ((1,), (1,))


def iota(shape, axis):
    return lax.broadcasted_iota(jnp.int32, shape, axis)


class Box:
    def __init__(self, capacity, width):
        self.capacity, self.width = capacity, width
        self.groups, self.extra = capacity // ROWS, capacity % ROWS
        self.cuts = ROWS // self.extra if self.extra else 1
        self.wide = -(-width // (LANES * self.cuts)) * LANES if self.extra else 0
        self.lanes = self.groups * width + self.wide
        self.pieces = -(-width // self.wide) if self.extra else 0

    def group(self, g):
        return pl.ds(g * self.width, self.width)

    def tail(self):
        return pl.ds(self.groups * self.width, self.wide)

    def piece(self, i):
        return i * self.wide, min(self.wide, self.width - i * self.wide)


def shift(value, sections=0, experts=0, flip=0):
    n_sec, n_own = lax.axis_size("section"), lax.axis_size("expert")
    n_exp = n_own // SPLIT
    if sections % n_sec == 0 and experts % n_exp == 0 and flip == 0:
        return value
    pairs = []
    for sec in range(n_sec):
        for own in range(n_own):
            exp, sl = own // SPLIT, own % SPLIT
            to = ((exp + experts) % n_exp) * SPLIT + (sl ^ flip)
            pairs.append((sec * n_own + own, ((sec + sections) % n_sec) * n_own + to))
    return lax.ppermute(value, ("section", "expert"), pairs)


def call(body, outs, *operands, scratch=(), flops=0, after=()):
    moved = sum(a.size * a.dtype.itemsize for a in operands)
    moved += sum(o.size * o.dtype.itemsize for o in outs)
    vmem = pl.BlockSpec(memory_space=pltpu.VMEM)
    read = len(operands)

    def reading(*refs):
        body(*refs[:read], *refs[read + len(after) :])

    return pl.pallas_call(
        reading,
        out_shape=list(outs),
        in_specs=[vmem] * read + [pl.BlockSpec(memory_space=pl.ANY)] * len(after),
        out_specs=[vmem] * len(outs),
        scratch_shapes=list(scratch),
        compiler_params=pltpu.CompilerParams(vmem_limit_bytes=40 * 2**20),
        cost_estimate=pl.CostEstimate(flops=flops, bytes_accessed=moved, transcendentals=0),
    )(*operands, *after)


def column_of(row):
    n = row.shape[1]
    eye = iota((n, n), 0) == iota((n, n), 1)
    return jnp.sum(jnp.where(eye, row, 0.0), axis=1, keepdims=True)


def slots_of(rel, experts, capacity):
    n = rel.shape[1]
    same = jnp.broadcast_to(column_of(rel), (n, n)) == jnp.broadcast_to(rel, (n, n))
    before = iota((n, n), 0) < iota((n, n), 1)
    rank = jnp.sum(jnp.where(same & before, 1.0, 0.0), axis=0, keepdims=True)
    return rel * capacity + rank


def terms(value):
    high = value.astype(BF).astype(F32)
    middle = (value - high).astype(BF).astype(F32)
    return high, middle, value - high - middle


def notes_of(slots, mix, gain, n, width):
    r = iota((ROWS, n), 0)
    left = jnp.where(r == 0, slots, 0.0)
    for at, term in enumerate(terms(mix)):
        left = jnp.where(r == 1 + at, term, left)
    r = iota((ROWS, width), 0)
    wide = jnp.concatenate([left, jnp.zeros((ROWS, width - n), F32)], axis=1)
    for at, term in enumerate(terms(gain)):
        wide = jnp.where(r == 4 + at, term, wide)
    return wide.astype(BF)


def slots_in(notes, n):
    return notes[:, :n].astype(F32)[0:1]


def mix_in(notes, n):
    left = notes[:, :n].astype(F32)
    return column_of(left[1:2] + left[2:3] + left[3:4])


def gain_in(notes):
    wide = notes.astype(F32)
    return wide[4:5] + wide[5:6] + wide[6:7]


def pack_rows(box, slots, values, out_refs):
    n = values.shape[0]
    line = jnp.broadcast_to(slots.astype(jnp.int32), (ROWS, n))
    r = iota((ROWS, n), 0)
    for j, out in enumerate(out_refs):
        first = j * box.capacity
        for g in range(box.groups):
            sel = jnp.where(line == first + g * ROWS + r, 1.0, 0.0).astype(BF)
            out[:, box.group(g)] = dot(sel, values).astype(BF)
        if box.extra:
            total = jnp.zeros((ROWS, box.wide), F32)
            for i in range(box.pieces):
                at, size = box.piece(i)
                hit = (line == first + box.groups * ROWS + r // box.cuts) & (r % box.cuts == i)
                hit &= r // box.cuts < box.extra
                got = dot(jnp.where(hit, 1.0, 0.0).astype(BF), values[:, at : at + size])
                if size < box.wide:
                    got = jnp.concatenate([got, jnp.zeros((ROWS, box.wide - size), F32)], axis=1)
                total = total + got
            out[:, box.tail()] = total.astype(BF)


def pick_rows(box, slots, boxes, n, picked):
    count = len(boxes)
    slots = column_of(slots)
    if box.groups:
        stack = jnp.concatenate(
            [b[:, g * box.width : (g + 1) * box.width] for b in boxes for g in range(box.groups)],
            axis=0,
        )
        tall = count * box.groups * ROWS
        c = iota((n, tall), 1)
        slot = c // (box.groups * ROWS) * box.capacity + c % (box.groups * ROWS)
        sel = jnp.where(slots.astype(jnp.int32) == slot, 1.0, 0.0).astype(BF)
        picked[...] = dot(sel, stack)
    else:
        picked[...] = jnp.zeros(picked.shape, F32)
    if box.extra:
        tails = jnp.concatenate([b[:, box.groups * box.width :] for b in boxes], axis=0)
        c = iota((n, count * ROWS), 1)
        r = c % ROWS
        slot = c // ROWS * box.capacity + box.groups * ROWS + r // box.cuts
        mine = (slots.astype(jnp.int32) == slot) & (r // box.cuts < box.extra)
        for i in range(box.pieces):
            at, size = box.piece(i)
            sel = jnp.where(mine & (r % box.cuts == i), 1.0, 0.0).astype(BF)
            picked[:, at : at + size] += dot(sel, tails[:, :size])


def heights(box, count):
    extra = -(-count * box.extra // ROWS) * ROWS
    return count * box.groups * ROWS, extra


def unpack(box, refs, stack, tails, at=0):
    count = 0
    for ref in refs:
        for p in range(ref.shape[0] // ROWS):
            for g in range(box.groups):
                stack[at : at + ROWS, :] = ref[p * ROWS : (p + 1) * ROWS, box.group(g)]
                at += ROWS
            if box.extra:
                tails[count * ROWS : (count + 1) * ROWS, :] = ref[
                    p * ROWS : (p + 1) * ROWS, box.tail()
                ]
            count += 1
    if box.extra:
        extra = heights(box, count)[1]
        r = iota((extra, count * ROWS), 0)
        c = iota((extra, count * ROWS), 1)
        mine = (r // box.extra == c // ROWS) & (r % box.extra == c % ROWS // box.cuts)
        for i in range(box.pieces):
            start, size = box.piece(i)
            sel = jnp.where(mine & (c % ROWS % box.cuts == i), 1.0, 0.0).astype(BF)
            stack[at : at + extra, start : start + size] = dot(sel, tails[:, :size]).astype(BF)


def repack(box, rows, refs):
    rows = rows.astype(BF)
    at = 0
    count = 0
    for ref in refs:
        for p in range(ref.shape[0] // ROWS):
            for g in range(box.groups):
                ref[p * ROWS : (p + 1) * ROWS, box.group(g)] = rows[at : at + ROWS]
                at += ROWS
            count += 1
    if box.extra:
        extra = heights(box, count)[1]
        r = iota((count * ROWS, extra), 0)
        c = iota((count * ROWS, extra), 1)
        mine = (c // box.extra == r // ROWS) & (c % box.extra == r % ROWS // box.cuts)
        total = jnp.zeros((count * ROWS, box.wide), F32)
        for i in range(box.pieces):
            start, size = box.piece(i)
            sel = jnp.where(mine & (r % ROWS % box.cuts == i), 1.0, 0.0).astype(BF)
            got = dot(sel, rows[at:, start : start + size])
            if size < box.wide:
                pad = jnp.zeros((count * ROWS, box.wide - size), F32)
                got = jnp.concatenate([got, pad], axis=1)
            total = total + got
        total = total.astype(BF)
        count = 0
        for ref in refs:
            tall = ref.shape[0]
            ref[:, box.tail()] = total[count : count + tall]
            count += tall


def inv_rms(wide):
    return lax.rsqrt(jnp.mean(wide * wide, axis=-1, keepdims=True) + EPSILON)


def total_of(refs):
    return sum(ref[...].astype(F32) for ref in refs).astype(BF)


def start_kernel(box, experts, tokens, cot, gain, ids, mix, ahead, notes0, notes1, *boxes):
    n, width = tokens.shape
    mine = lax.axis_index("expert") // SPLIT
    for k, notes in enumerate((notes0, notes1)):
        rel = ids[k : k + 1, :] - mine
        rel = jnp.where(rel < 0, rel + experts, rel).astype(F32)
        slots = slots_of(rel, experts, box.capacity)
        notes[...] = notes_of(slots, mix[k : k + 1, :], gain[...], n, width)
    ahead[:n] = tokens[...]
    ahead[n:] = notes0[...]
    wide = tokens[...].astype(F32)
    normed = (wide * inv_rms(wide) * gain[...]).astype(BF)
    crossing = boxes[2:]
    firsts = [boxes[0]] + [ref.at[:ROWS] for ref in crossing]
    pack_rows(box, slots_in(notes0[...], n), normed, firsts)
    seconds = [boxes[1]] + [ref.at[ROWS:] for ref in crossing]
    pack_rows(box, slots_in(notes1[...], n), cot[...], seconds)


def combine(box, notes, n, own, back, picked):
    sums = [total_of(own)] + [ref[...] for ref in back]
    pick_rows(box, slots_in(notes, n), sums, n, picked)
    return mix_in(notes, n) * picked[...]


def split_refs(refs, experts, outs):
    ins = refs[:-outs]
    return ins[experts - 1 :], ins[: experts - 1], refs[-outs:]


def middle_kernel(box, experts, arrived, cot, notes1, gain, *refs):
    boxes, picked = refs[-1 - experts : -1], refs[-1]
    own, back, (after, behind) = split_refs(refs[: -1 - experts], experts, 2)
    n = cot.shape[0]
    update = combine(box, arrived[n:], n, own, back, picked)
    later = (arrived[:n].astype(F32) + update).astype(BF)
    after[...] = later
    behind[:n] = later
    behind[n : 2 * n] = cot[...]
    behind[2 * n :] = notes1[...]
    wide = later.astype(F32)
    normed = (wide * inv_rms(wide) * gain[...]).astype(BF)
    pack_rows(box, slots_in(notes1[...], n), normed, boxes)


def final_kernel(box, experts, hidden, notes, *refs):
    picked = refs[-1]
    own, back, (out,) = split_refs(refs[:-1], experts, 1)
    n = hidden.shape[0]
    update = combine(box, notes[...], n, own, back, picked)
    out[...] = (hidden[...].astype(F32) + update).astype(BF)


def norm_back(hidden, gain, grad):
    wide = hidden.astype(F32)
    inv = inv_rms(wide)
    scaled = grad * gain
    along = jnp.mean(scaled * wide, axis=-1, keepdims=True)
    return inv * scaled - wide * (inv * inv * inv * along)


def turn_kernel(box, experts, arrived, notes0, *refs):
    boxes, picked = refs[-1 - experts : -1], refs[-1]
    own, back, (out,) = split_refs(refs[: -1 - experts], experts, 1)
    n = out.shape[0]
    notes = arrived[2 * n :]
    d_normed = combine(box, notes, n, own, back, picked)
    change = norm_back(arrived[:n], gain_in(notes), d_normed)
    now = (arrived[n : 2 * n].astype(F32) + change).astype(BF)
    out[...] = now
    pack_rows(box, slots_in(notes0[...], n), now, boxes)


def last_kernel(box, experts, grad, hidden, notes0, gain, *refs):
    picked = refs[-1]
    own, back, (out,) = split_refs(refs[:-1], experts, 1)
    n = hidden.shape[0]
    d_normed = combine(box, notes0[...], n, own, back, picked)
    change = norm_back(hidden[...], gain[...], d_normed)
    out[...] = (grad[...].astype(F32) + change).astype(BF)


def spans(tall):
    return pl.ds(0, 2 * tall), pl.ds(tall, 2 * tall)


def gate_up(rows, pack):
    return dot(rows, pack[: 2 * (pack.shape[0] // 3)], NT)


def parts_of(both):
    units = both.shape[1] // 2
    return both[:, :units], both[:, units:]


def down_rows(both, pack):
    g, u = parts_of(both)
    return dot((jax.nn.silu(g) * u).astype(BF), pack[2 * g.shape[1] :])


def inner_of(rows, pack):
    return dot(rows, pack[2 * (pack.shape[0] // 3) :], NT)


def part_rows(d_inner, both, pack):
    g, u = parts_of(both)
    r = jax.nn.sigmoid(g)
    d_gate = d_inner * u * r * (1.0 + g * (1.0 - r))
    d_up = d_inner * g * r
    return dot(jnp.concatenate([d_gate, d_up], axis=1).astype(BF), pack[: both.shape[1]])


def read_rows(box, rows, stack, tails):
    tall = stack.shape[0] // 3
    for at, ref in enumerate(rows):
        unpack(box, [ref], stack, tails, at * tall)
    return [stack[span, :] for span in spans(tall)]


def write_rows(box, top, bottom, outs):
    tall = top.shape[0] // 2
    for ref, value in zip(outs, (top[:tall], top[tall:] + bottom[:tall], bottom[tall:])):
        repack(box, value, [ref])


def forward_kernel(box, packs, saved, rows, outs, kept, stack, tails):
    sides = read_rows(box, rows, stack, tails)
    total = []
    for side, values in enumerate(sides):
        total.append(0.0)
        for at in (2 * side, 2 * side + 1):
            both = gate_up(values, packs[at])
            kept[at][...] = both
            total[side] = total[side] + down_rows(both, packs[at])
    write_rows(box, *total, outs)


def inner_kernel(box, packs, saved, rows, outs, kept, stack, tails):
    for side, values in enumerate(read_rows(box, rows, stack, tails)):
        for at in (2 * side, 2 * side + 1):
            kept[at][...] = inner_of(values, packs[at])


def gate_back_kernel(box, packs, saved, rows, outs, kept, stack, tails):
    sides = read_rows(box, rows, stack, tails)
    total = []
    for side, values in enumerate(sides):
        total.append(0.0)
        for at in (2 * side, 2 * side + 1):
            both = gate_up(values, packs[at])
            kept[at][...] = both
            total[side] = total[side] + part_rows(saved[at][...], both, packs[at])
    write_rows(box, *total, outs)


def back_kernel(box, packs, saved, rows, outs, kept, stack, tails):
    sides = read_rows(box, rows, stack, tails)
    total = []
    for side, values in enumerate(sides):
        total.append(0.0)
        for at in (2 * side, 2 * side + 1):
            d_inner = inner_of(values, packs[at])
            total[side] = total[side] + part_rows(d_inner, saved[at][...], packs[at])
    write_rows(box, *total, outs)


def down_kernel(box, packs, saved, rows, outs, kept, stack, tails):
    total = []
    for side in range(2):
        at = 2 * side
        total.append(sum(down_rows(saved[i][...], packs[i]) for i in (at, at + 1)))
    write_rows(box, *total, outs)


def expert_call(kernel, box, packs, rows, saved=(), outs=True, kept=0, reads=True, after=(), window=None):
    width = packs[0].shape[1]
    first, size = window or (0, rows[0].shape[0])
    count = size // ROWS
    tall = sum(heights(box, count))
    boxes = jax.ShapeDtypeStruct((count * ROWS, box.lanes), BF)
    results = [boxes] * len(rows) if outs else []
    if kept:
        units = [pack.shape[0] // 3 for pack in packs]
        results += [jax.ShapeDtypeStruct((2 * tall, kept * u), F32) for u in units]
    inputs = list(packs) + list(saved) + (list(rows) if reads else [])
    n_in, n_p, n_s, n_out = len(inputs), len(packs), len(saved), len(rows) if outs else 0

    def body(*refs):
        results_refs = refs[n_in:-2]
        kernel(
            box,
            refs[:n_p],
            refs[n_p : n_p + n_s],
            [ref.at[pl.ds(first, size)] for ref in refs[n_p + n_s : n_in]],
            results_refs[:n_out],
            results_refs[n_out:],
            refs[-2],
            refs[-1],
        )

    scratch = [
        pltpu.VMEM((3 * tall, width), BF),
        pltpu.VMEM((count * ROWS, max(box.wide, LANES)), BF),
    ]
    flops = sum(2 * 2 * tall * pack.size for pack in packs)
    results = call(body, results, *inputs, scratch=scratch, flops=flops, after=after)
    return results[:n_out], results[n_out:]


def local(tokens, norm_gain, w_gate, w_up, w_down, routes, mix_weights, cotangent):
    experts = lax.axis_size("expert") // SPLIT
    n, width = tokens.shape[1:]
    capacity = n // experts + max(1, n // (16 * experts))
    box = Box(capacity, width)
    gain = norm_gain
    gate_w, up_w, down_w = w_gate[0, 0].T, w_up[0, 0].T, w_down[0, 0]
    boxed = jax.ShapeDtypeStruct((ROWS, box.lanes), BF)
    picked = pltpu.VMEM((n, width), F32)
    bind = functools.partial

    def joined(arrays):
        return arrays[0] if len(arrays) == 1 else jnp.concatenate(arrays, axis=0)

    fence = lax.optimization_barrier

    def crossing_of(boxes):
        return joined([shift(boxes[j - 1], experts=j) for j in range(1, experts)])

    def around(boxes):
        return [shift(boxes, flip=2), boxes, shift(boxes, flip=1)]

    def add(*values):
        return sum(v.astype(F32) for v in values).astype(BF)

    def sums(parts):
        return add(parts[1], shift(parts[0], flip=2), shift(parts[2], flip=1))

    def home(total, sections):
        return [
            shift(total[(j - 1) * ROWS : j * ROWS], sections=sections, experts=-j)
            for j in range(1, experts)
        ]

    def own_home(parts, sections):
        return [
            shift(parts[0], sections=sections, flip=2),
            shift(parts[2], sections=sections, flip=1),
            shift(parts[1], sections=sections),
        ]

    def give_back(cross, own, sections, others=()):
        total = sums(cross)
        back = home(total, sections)
        own, _, others = fence((own, total, others))
        return back + own_home(own, sections), others

    units = w_gate.shape[3]
    cut = -(-units * 7 // 12 // ROWS) * ROWS
    top = jnp.concatenate([gate_w[:cut], up_w[:cut], down_w[:cut]], axis=0)
    bottom = jnp.concatenate([gate_w[cut:], up_w[cut:], down_w[cut:]], axis=0)
    packs = [top, shift(top, flip=1), bottom, shift(bottom, flip=2)]

    def rows_of(count):
        return jax.ShapeDtypeStruct((count, width), BF)

    both = jax.ShapeDtypeStruct((2 * ROWS, box.lanes), BF)
    ahead, notes0, notes1, own_tok, own_cot, *crossing = call(
        bind(start_kernel, box, experts),
        [rows_of(n + ROWS), rows_of(ROWS), rows_of(ROWS), boxed, boxed] + [both] * (experts - 1),
        tokens[0],
        cotangent[0],
        gain,
        routes[0, :, :, 0],
        mix_weights[0, :, :, 0],
        after=[top, bottom],
    )
    crossed = [shift(crossing[j - 1], experts=j) for j in range(1, experts)]
    own0 = around(own_tok)
    packs, crossed, own0 = fence((packs, crossed, own0))
    cross0 = around(joined([c[:ROWS] for c in crossed]))
    cots = joined([own_cot] + [c[ROWS:] for c in crossed])
    cross0, cots = fence((cross0, cots))
    cots = around(cots)

    cross_out, cross_kept0 = expert_call(forward_kernel, box, packs, cross0, kept=2)
    own_out, own_kept0 = expert_call(
        forward_kernel, box, packs, own0, kept=2, after=cross_out[:1]
    )
    cross_out, ahead = fence((cross_out, ahead))
    arrived0 = shift(ahead, sections=1)
    got, cots = give_back(cross_out, own_out, 1, cots)
    h1, behind, own1, *boxes1 = call(
        bind(middle_kernel, box, experts),
        [rows_of(n), rows_of(2 * n + ROWS)] + [boxed] * experts,
        arrived0,
        cotangent[0],
        notes1,
        gain,
        *got,
        scratch=[picked],
    )
    arrived1 = shift(behind, sections=-1)
    cross1, own_z, own_x, arrived1 = fence(
        (crossing_of(boxes1), shift(own1, flip=2), shift(own1, flip=1), arrived1)
    )
    cross1, own1 = around(cross1), [own_z, own1, own_x]
    inner = bind(expert_call, inner_kernel, box, packs, cots, outs=False, kept=1)
    own_di = inner(window=(0, ROWS))[1]
    cross_di = inner(window=(ROWS, (experts - 1) * ROWS))[1]

    gate_back = bind(expert_call, gate_back_kernel, box, packs, kept=2)
    own_grad, own_kept1 = gate_back(own1, own_di)
    cross_grad, cross_kept1 = gate_back(cross1, cross_di, after=own_grad[:1])
    down = bind(expert_call, down_kernel, box, packs, reads=False)
    cross_fin = down(cross1, cross_kept1)[0]
    got, _ = give_back(cross_grad, own_grad, -1)
    got[: experts - 1], fin_sums = fence((got[: experts - 1], sums(cross_fin)))
    fin_back = home(fin_sums, 0)
    own_fin = down(own1, own_kept1)[0]
    g1, own_g, *boxes_g = call(
        bind(turn_kernel, box, experts),
        [rows_of(n)] + [boxed] * experts,
        arrived1,
        notes0,
        *got,
        scratch=[picked],
    )

    cross_g, own_z, own_x = fence(
        (crossing_of(boxes_g), shift(own_g, flip=2), shift(own_g, flip=1))
    )
    cross_g, own_g = around(cross_g), [own_z, own_g, own_x]
    back = bind(expert_call, back_kernel, box, packs)
    fin = fin_back + own_home(own_fin, 0)
    own_grad = back(own_g, own_kept0, after=fin)[0]
    cross_grad = back(cross_g, cross_kept0, after=own_grad[:1])[0]
    got = home(sums(cross_grad), 0) + own_home(own_grad, 0)
    (g0,) = call(
        bind(last_kernel, box, experts),
        [rows_of(n)],
        g1,
        tokens[0],
        notes0,
        gain,
        *got,
        scratch=[picked],
    )
    (final,) = call(
        bind(final_kernel, box, experts),
        [rows_of(n)],
        h1,
        notes1,
        *fin,
        scratch=[picked],
    )
    return (final[None], g0[None])


def solution(mesh):
    in_specs = (
        P("section", "expert", None),
        P("section", None),
        P("section", "expert", None, None),
        P("section", "expert", None, None),
        P("section", "expert", None, None),
        P("section", None, "expert", None),
        P("section", None, "expert", None),
        P("section", "expert", None),
    )
    out_specs = (P("section", "expert", None), P("section", "expert", None))
    return jax.shard_map(local, mesh=mesh, in_specs=in_specs, out_specs=out_specs, check_vma=False)
```

profile of v0, /device:TPU:0, one launch (start us, length us, event | category | flops | bytes accessed | tf_op | source)
XLA Modules:
  0.0 169.6 jit_solution(4038925555077362182)
XLA Ops:
  0.6 1.2 slice.40
  1.8 1.1 slice.41
  3.1 3.0 %collective-permute-start = (bf16[336,2560]{1,0:T(8,128)(2,1)S(1)}, bf16[336,2560]{1,0:T(8,128)(2,1)S(1)}, u32[]{:S(2)}, u32[]{:S(2)}) collective-permute-start(bf16[336,2560]{1,0:T(8,128)(2,1)S(1)} %pad_maximum_fusion.refs_5_.refs_0_), channel_id=1, source_target_pairs={{0,1},{1,0},{2,3},{3,2},{4,5},{5,4},{6,7},{7,6},{8,9},{9,8},{10,11... | collective-permute-start | bytes 5160968 | tf_op jit(solution)/shard_map/ppermute | solution.py:59
  6.1 1.0 slice.42
  7.2 1.1 slice.43
  8.4 1.6 collective-permute-start.1
  10.9 2.6 %collective-permute-start.2 = (bf16[32,5504]{1,0:T(8,128)(2,1)S(1)}, bf16[32,5504]{1,0:T(8,128)(2,1)S(1)}, u32[]{:S(2)}, u32[]{:S(2)}) collective-permute-start(bf16[32,5504]{1,0:T(8,128)(2,1)S(1)} %get-tuple-element.97), channel_id=1, source_target_pairs={{0,4},{1,5},{2,6},{3,7},{4,0},{5,1},{6,2},{7,3},{8,12},{9,13},{10,... | collective-permute-start | bytes 1056776 | tf_op jit(solution)/shard_map/ppermute | solution.py:59
  14.5 32.9 %collective-permute-done.4.refs_6_ = bf16[16,5504]{1,0:T(8,128)(2,1)S(1)} collective-permute-done((bf16[16,5504]{1,0:T(8,128)(2,1)S(1)}, bf16[16,5504]{1,0:T(8,128)(2,1)S(1)}, u32[]{:S(2)}, u32[]{:S(2)}) %collective-permute-start.4) | collective-permute-done | bytes 176160 | tf_op jit(solution)/shard_map/ppermute | solution.py:59
  49.3 1.6 collective-permute-start.5
  50.9 2.9 %collective-permute-done.6.refs_6_ = bf16[16,5504]{1,0:T(8,128)(2,1)S(1)} collective-permute-done((bf16[16,5504]{1,0:T(8,128)(2,1)S(1)}, bf16[16,5504]{1,0:T(8,128)(2,1)S(1)}, u32[]{:S(2)}, u32[]{:S(2)}) %collective-permute-start.6) | collective-permute-done | bytes 176160 | tf_op jit(solution)/shard_map/ppermute | solution.py:59
  54.8 2.5 %shard_map.96 = (bf16[16,5504]{1,0:T(8,128)(2,1)S(1)}, bf16[16,5504]{1,0:T(8,128)(2,1)S(1)}, bf16[16,5504]{1,0:T(8,128)(2,1)S(1)}, f32[96,224]{1,0:T(8,128)S(1)}...) custom-call(bf16[336,2560]{1,0:T(8,128)(2,1)S(1)} %pad_maximum_fusion.refs_5_.refs_0_, ...), custom_call_target="tpu_custom_call" | custom-call | flops 566231040 | bytes 7249920 | tf_op jit(solution)/shard_map/pallas_call | solution.py:71
  57.2 1.6 collective-permute-start.8
  58.9 1.1 collective-permute-start.9
  61.3 2.5 %shard_map.97 = (bf16[16,5504]{1,0:T(8,128)(2,1)S(1)}, bf16[16,5504]{1,0:T(8,128)(2,1)S(1)}, bf16[16,5504]{1,0:T(8,128)(2,1)S(1)}, f32[96,224]{1,0:T(8,128)S(1)}...) custom-call(bf16[336,2560]{1,0:T(8,128)(2,1)S(1)} %pad_maximum_fusion.refs_5_.refs_0_, ...), custom_call_target="tpu_custom_call" | custom-call | flops 566231040 | bytes 7249920 | tf_op jit(solution)/shard_map/pallas_call | solution.py:71
  64.5 1.7 %collective-permute-done.9 = bf16[16,5504]{1,0:T(8,128)(2,1)S(1)} collective-permute-done((bf16[16,5504]{1,0:T(8,128)(2,1)S(1)}, bf16[16,5504]{1,0:T(8,128)(2,1)S(1)}, u32[]{:S(2)}, u32[]{:S(2)}) %collective-permute-start.9) | collective-permute-done | bytes 176160 | tf_op jit(solution)/shard_map/ppermute | solution.py:59
  66.3 1.5 collective-permute-start.10
  67.8 2.5 %collective-permute-done.12.refs_6_ = bf16[32,5504]{1,0:T(8,128)(2,1)S(1)} collective-permute-done((bf16[32,5504]{1,0:T(8,128)(2,1)S(1)}, bf16[32,5504]{1,0:T(8,128)(2,1)S(1)}, u32[]{:S(2)}, u32[]{:S(2)}) %collective-permute-start.12) | collective-permute-done | bytes 352288 | tf_op jit(solution)/shard_map/ppermute | solution.py:59
  70.3 1.9 %collective-permute-start.14 = (bf16[16,5504]{1,0:T(8,128)(2,1)S(1)}, bf16[16,5504]{1,0:T(8,128)(2,1)S(1)}, u32[]{:S(2)}, u32[]{:S(2)}) collective-permute-start(bf16[16,5504]{1,0:T(8,128)(2,1)S(1)} %get-tuple-element.125), channel_id=1, source_target_pairs={{0,9},{1,8},{2,11},{3,10},{4,13},{5,12},{6,15},{7,14},{8,17},{9,16... | collective-permute-start | bytes 528392 | tf_op jit(solution)/shard_map/ppermute | solution.py:59
  72.3 6.4 %collective-permute-done.10.refs_4_ = bf16[16,5504]{1,0:T(8,128)(2,1)S(1)} collective-permute-done((bf16[16,5504]{1,0:T(8,128)(2,1)S(1)}, bf16[16,5504]{1,0:T(8,128)(2,1)S(1)}, u32[]{:S(2)}, u32[]{:S(2)}) %collective-permute-start.10) | collective-permute-done | bytes 176160 | tf_op jit(solution)/shard_map/ppermute | solution.py:59
  78.7 1.2 collective-permute-done.13.refs_5_
  79.8 1.1 collective-permute-done.15.refs_7_
  81.9 1.9 %collective-permute-start.16 = (bf16[16,5504]{1,0:T(8,128)(2,1)S(1)}, bf16[16,5504]{1,0:T(8,128)(2,1)S(1)}, u32[]{:S(2)}, u32[]{:S(2)}) collective-permute-start(bf16[16,5504]{1,0:T(8,128)(2,1)S(1)} %get-tuple-element.135), channel_id=1, source_target_pairs={{0,4},{1,5},{2,6},{3,7},{4,0},{5,1},{6,2},{7,3},{8,12},{9,13},{10,... | collective-permute-start | bytes 528392 | tf_op jit(solution)/shard_map/ppermute | solution.py:59
  84.4 2.5 %collective-permute-start.17 = (bf16[16,5504]{1,0:T(8,128)(2,1)S(1)}, bf16[16,5504]{1,0:T(8,128)(2,1)S(1)}, u32[]{:S(2)}, u32[]{:S(2)}) collective-permute-start(bf16[16,5504]{1,0:T(8,128)(2,1)S(1)} %get-tuple-element.136.refs_9_), channel_id=1, source_target_pairs={{0,2},{1,3},{2,0},{3,1},{4,6},{5,7},{6,4},{7,5},{8,10},{9,11},{10,... | collective-permute-start | bytes 528392 | tf_op jit(solution)/shard_map/ppermute | solution.py:59
  86.9 6.7 %collective-permute-done.16.refs_9_ = bf16[16,5504]{1,0:T(8,128)(2,1)S(1)} collective-permute-done((bf16[16,5504]{1,0:T(8,128)(2,1)S(1)}, bf16[16,5504]{1,0:T(8,128)(2,1)S(1)}, u32[]{:S(2)}, u32[]{:S(2)}) %collective-permute-start.16) | collective-permute-done | bytes 176160 | tf_op jit(solution)/shard_map/ppermute | solution.py:59
  97.1 2.6 %shard_map.101 = (bf16[16,5504]{1,0:T(8,128)(2,1)S(1)}, bf16[16,5504]{1,0:T(8,128)(2,1)S(1)}, bf16[16,5504]{1,0:T(8,128)(2,1)S(1)}, f32[96,224]{1,0:T(8,128)S(1)...) custom-call(bf16[336,2560]{1,0:T(8,128)(2,1)S(1)} %pad_maximum_fusion.refs_5_.refs_0_, ...), custom_call_target="tpu_custom_call" | custom-call | flops 566231040 | bytes 7397376 | tf_op jit(solution)/shard_map/pallas_call | solution.py:71
  100.8 2.6 %shard_map.102 = (bf16[16,5504]{1,0:T(8,128)(2,1)S(1)}, bf16[16,5504]{1,0:T(8,128)(2,1)S(1)}, bf16[16,5504]{1,0:T(8,128)(2,1)S(1)}, f32[96,224]{1,0:T(8,128)S(1)...) custom-call(bf16[336,2560]{1,0:T(8,128)(2,1)S(1)} %pad_maximum_fusion.refs_5_.refs_0_, ...), custom_call_target="tpu_custom_call" | custom-call | flops 566231040 | bytes 7397376 | tf_op jit(solution)/shard_map/pallas_call | solution.py:71
  103.4 1.0 collective-permute-start.22
  106.3 1.1 collective-permute-start.25
  108.4 2.2 %collective-permute-done.22 = bf16[16,5504]{1,0:T(8,128)(2,1)S(1)} collective-permute-done((bf16[16,5504]{1,0:T(8,128)(2,1)S(1)}, bf16[16,5504]{1,0:T(8,128)(2,1)S(1)}, u32[]{:S(2)}, u32[]{:S(2)}) %collective-permute-start.22) | collective-permute-done | bytes 176160 | tf_op jit(solution)/shard_map/ppermute | solution.py:59
  111.3 4.5 %collective-permute-start.30 = (bf16[16,5504]{1,0:T(8,128)(2,1)S(1)}, bf16[16,5504]{1,0:T(8,128)(2,1)S(1)}, u32[]{:S(2)}, u32[]{:S(2)}) collective-permute-start(bf16[16,5504]{1,0:T(8,128)(2,1)S(1)} %get-tuple-element.169.refs_11_), channel_id=1, source_target_pairs={{0,26},{1,27},{2,24},{3,25},{4,30},{5,31},{6,28},{7,29},{8,2},{9,3... | collective-permute-start | bytes 528392 | tf_op jit(solution)/shard_map/ppermute | solution.py:59
  116.3 6.3 %collective-permute-done.24.refs_2_ = bf16[16,5504]{1,0:T(8,128)(2,1)S(1)} collective-permute-done((bf16[16,5504]{1,0:T(8,128)(2,1)S(1)}, bf16[16,5504]{1,0:T(8,128)(2,1)S(1)}, u32[]{:S(2)}, u32[]{:S(2)}) %collective-permute-start.24) | collective-permute-done | bytes 176160 | tf_op jit(solution)/shard_map/ppermute | solution.py:59
  122.5 2.3 %collective-permute-done.32.refs_5_ = bf16[16,5504]{1,0:T(8,128)(2,1)S(1)} collective-permute-done((bf16[16,5504]{1,0:T(8,128)(2,1)S(1)}, bf16[16,5504]{1,0:T(8,128)(2,1)S(1)}, u32[]{:S(2)}, u32[]{:S(2)}) %collective-permute-start.32) | collective-permute-done | bytes 176160 | tf_op jit(solution)/shard_map/ppermute | solution.py:59
  125.8 1.1 collective-permute-start.35
  127.0 1.4 collective-permute-start.34
  130.9 5.8 %collective-permute-done.33.refs_9_ = bf16[16,5504]{1,0:T(8,128)(2,1)S(1)} collective-permute-done((bf16[16,5504]{1,0:T(8,128)(2,1)S(1)}, bf16[16,5504]{1,0:T(8,128)(2,1)S(1)}, u32[]{:S(2)}, u32[]{:S(2)}) %collective-permute-start.33) | collective-permute-done | bytes 176160 | tf_op jit(solution)/shard_map/ppermute | solution.py:59
  136.7 1.4 collective-permute-done.34.refs_8_
  139.0 1.4 collective-permute-start.36
  140.4 1.6 collective-permute-done.28.refs_3_.refs_12_
  142.1 5.8 %collective-permute-done.27.refs_2_.refs_11_ = bf16[16,5504]{1,0:T(8,128)(2,1)S(1)} collective-permute-done((bf16[16,5504]{1,0:T(8,128)(2,1)S(1)}, bf16[16,5504]{1,0:T(8,128)(2,1)S(1)}, u32[]{:S(2)}, u32[]{:S(2)}) %collective-permute-start.27) | collective-permute-done | bytes 176160 | tf_op jit(solution)/shard_map/ppermute | solution.py:59
  147.9 2.0 %shard_map.107 = (bf16[16,5504]{1,0:T(8,128)(2,1)S(1)}, bf16[16,5504]{1,0:T(8,128)(2,1)S(1)}, bf16[16,5504]{1,0:T(8,128)(2,1)S(1)}) custom-call(bf16[336,2560]{1,0:T(8,128)(2,1)S(1)} %pad_maximum_fusion.refs_5_.refs_0_, bf16[336,2560]{1,0:T(8,128)(2,1)S(1)} %collective-permute-done.refs_1_, bf16[240,2560]{1,0:T(8,128)(2,1)S(1)} %pad_maximum_fusion.1.refs_6_.refs_2_, ...), custom_call_target="tpu_custom_call" | custom-call | flops 566231040 | bytes 7249920 | tf_op jit(solution)/shard_map/pallas_call | solution.py:71
  149.9 2.0 %shard_map.108 = (bf16[16,5504]{1,0:T(8,128)(2,1)S(1)}, bf16[16,5504]{1,0:T(8,128)(2,1)S(1)}, bf16[16,5504]{1,0:T(8,128)(2,1)S(1)}) custom-call(bf16[336,2560]{1,0:T(8,128)(2,1)S(1)} %pad_maximum_fusion.refs_5_.refs_0_, bf16[336,2560]{1,0:T(8,128)(2,1)S(1)} %collective-permute-done.refs_1_, bf16[240,2560]{1,0:T(8,128)(2,1)S(1)} %pad_maximum_fusion.1.refs_6_.refs_2_, ...), custom_call_target="tpu_custom_call" | custom-call | flops 566231040 | bytes 7249920 | tf_op jit(solution)/shard_map/pallas_call | solution.py:71
  153.0 2.0 %collective-permute-start.41 = (bf16[16,5504]{1,0:T(8,128)(2,1)S(1)}, bf16[16,5504]{1,0:T(8,128)(2,1)S(1)}, u32[]{:S(2)}, u32[]{:S(2)}) collective-permute-start(bf16[16,5504]{1,0:T(8,128)(2,1)S(1)} %get-tuple-element.186.refs_11_), channel_id=1, source_target_pairs={{0,2},{1,3},{2,0},{3,1},{4,6},{5,7},{6,4},{7,5},{8,10},{9,11},{10,... | collective-permute-start | bytes 528392 | tf_op jit(solution)/shard_map/ppermute | solution.py:59
  154.9 1.1 collective-permute-start.42
  156.0 3.3 %collective-permute-done.38 = bf16[16,5504]{1,0:T(8,128)(2,1)S(1)} collective-permute-done((bf16[16,5504]{1,0:T(8,128)(2,1)S(1)}, bf16[16,5504]{1,0:T(8,128)(2,1)S(1)}, u32[]{:S(2)}, u32[]{:S(2)}) %collective-permute-start.38) | collective-permute-done | bytes 176160 | tf_op jit(solution)/shard_map/ppermute | solution.py:59
  159.5 2.2 %collective-permute-start.40 = (bf16[16,5504]{1,0:T(8,128)(2,1)S(1)}, bf16[16,5504]{1,0:T(8,128)(2,1)S(1)}, u32[]{:S(2)}, u32[]{:S(2)}) collective-permute-start(bf16[16,5504]{1,0:T(8,128)(2,1)S(1)} %add_convert_fusion), channel_id=1, source_target_pairs={{0,4},{1,5},{2,6},{3,7},{4,0},{5,1},{6,2},{7,3},{8,12},{9,13},{10,... | collective-permute-start | bytes 528392 | tf_op jit(solution)/shard_map/ppermute | solution.py:59
  161.7 1.1 shard_map.105
  162.8 5.5 %collective-permute-done.40.refs_4_ = bf16[16,5504]{1,0:T(8,128)(2,1)S(1)} collective-permute-done((bf16[16,5504]{1,0:T(8,128)(2,1)S(1)}, bf16[16,5504]{1,0:T(8,128)(2,1)S(1)}, u32[]{:S(2)}, u32[]{:S(2)}) %collective-permute-start.40) | collective-permute-done | bytes 176160 | tf_op jit(solution)/shard_map/ppermute | solution.py:59
  168.3 1.3 shard_map.109
  (79 shorter events, 22.9 us)
Async XLA Ops:
  3.1 45.2 %collective-permute-start = (bf16[336,2560]{1,0:T(8,128)(2,1)S(1)}, bf16[336,2560]{1,0:T(8,128)(2,1)S(1)}, u32[]{:S(2)}, u32[]{:S(2)}) collective-permute-start(bf16[336,2560]{1,0:T(8,128)(2,1)S(1)} %pad_maximum_fusion.refs_5_.refs_0_), channel_id=1, source_target_pairs={{0,1},{1,0},{2,3},{3,2},{4,5},{5,4},{6,7},{7,6},{8,9},{9,8},{10,11... | collective-permute-start | bytes 5160968 | tf_op jit(solution)/shard_map/ppermute | solution.py:59
  7.2 2.9 %copy-start = (bf16[1,64,2560]{2,1,0:T(8,128)(2,1)S(1)}, bf16[1,64,2560]{2,1,0:T(8,128)(2,1)}, u32[]{:S(2)}) copy-start(bf16[1,64,2560]{2,1,0:T(8,128)(2,1)} %param.15) | copy-start | bytes 983044
  7.2 2.9 %copy-start.1 = (bf16[1,64,2560]{2,1,0:T(8,128)(2,1)S(1)}, bf16[1,64,2560]{2,1,0:T(8,128)(2,1)}, u32[]{:S(2)}) copy-start(bf16[1,64,2560]{2,1,0:T(8,128)(2,1)} %param.8) | copy-start | bytes 983044
  7.2 2.9 %copy-start.2 = (f32[1,2560]{1,0:T(1,128)S(1)}, f32[1,2560]{1,0:T(1,128)}, u32[]{:S(2)}) copy-start(f32[1,2560]{1,0:T(1,128)} %refs_3_.3) | copy-start | bytes 30724
  7.2 2.9 %copy-start.3 = (s32[1,2,64,1]{2,3,1,0:T(1,128)S(1)}, s32[1,2,64,1]{2,3,1,0:T(1,128)}, u32[]{:S(2)}) copy-start(s32[1,2,64,1]{2,3,1,0:T(1,128)} %param.13) | copy-start | bytes 1540
  7.2 2.8 %copy-start.4 = (f32[1,2,64,1]{2,3,1,0:T(1,128)S(1)}, f32[1,2,64,1]{2,3,1,0:T(1,128)}, u32[]{:S(2)}) copy-start(f32[1,2,64,1]{2,3,1,0:T(1,128)} %param.14) | copy-start | bytes 1540
  8.4 39.9 %collective-permute-start.1 = (bf16[240,2560]{1,0:T(8,128)(2,1)S(1)}, bf16[240,2560]{1,0:T(8,128)(2,1)S(1)}, u32[]{:S(2)}, u32[]{:S(2)}) collective-permute-start(bf16[240,2560]{1,0:T(8,128)(2,1)S(1)} %pad_maximum_fusion.1.refs_6_.refs_2_), channel_id=1, source_target_pairs={{0,2},{1,3},{2,0},{3,1},{4,6},{5,7},{6,4},{7,5},{8,10},{9,11},{10,... | collective-permute-start | bytes 3686408 | tf_op jit(solution)/shard_map/ppermute | solution.py:59
  10.9 37.3 %collective-permute-start.2 = (bf16[32,5504]{1,0:T(8,128)(2,1)S(1)}, bf16[32,5504]{1,0:T(8,128)(2,1)S(1)}, u32[]{:S(2)}, u32[]{:S(2)}) collective-permute-start(bf16[32,5504]{1,0:T(8,128)(2,1)S(1)} %get-tuple-element.97), channel_id=1, source_target_pairs={{0,4},{1,5},{2,6},{3,7},{4,0},{5,1},{6,2},{7,3},{8,12},{9,13},{10,... | collective-permute-start | bytes 1056776 | tf_op jit(solution)/shard_map/ppermute | solution.py:59
  13.6 33.9 %collective-permute-start.4 = (bf16[16,5504]{1,0:T(8,128)(2,1)S(1)}, bf16[16,5504]{1,0:T(8,128)(2,1)S(1)}, u32[]{:S(2)}, u32[]{:S(2)}) collective-permute-start(bf16[16,5504]{1,0:T(8,128)(2,1)S(1)} %get-tuple-element.118.refs_5_), channel_id=1, source_target_pairs={{0,1},{1,0},{2,3},{3,2},{4,5},{5,4},{6,7},{7,6},{8,9},{9,8},{10,11... | collective-permute-start | bytes 528392 | tf_op jit(solution)/shard_map/ppermute | solution.py:59
  14.1 34.2 %collective-permute-start.3 = (bf16[16,5504]{1,0:T(8,128)(2,1)S(1)}, bf16[16,5504]{1,0:T(8,128)(2,1)S(1)}, u32[]{:S(2)}, u32[]{:S(2)}) collective-permute-start(bf16[16,5504]{1,0:T(8,128)(2,1)S(1)} %get-tuple-element.118.refs_5_), channel_id=1, source_target_pairs={{0,2},{1,3},{2,0},{3,1},{4,6},{5,7},{6,4},{7,5},{8,10},{9,11},{10,... | collective-permute-start | bytes 528392 | tf_op jit(solution)/shard_map/ppermute | solution.py:59
  48.3 5.5 %collective-permute-start.6 = (bf16[16,5504]{1,0:T(8,128)(2,1)S(1)}, bf16[16,5504]{1,0:T(8,128)(2,1)S(1)}, u32[]{:S(2)}, u32[]{:S(2)}) collective-permute-start(bf16[16,5504]{1,0:T(8,128)(2,1)S(1)} %get-tuple-element.106.refs_5_), channel_id=1, source_target_pairs={{0,1},{1,0},{2,3},{3,2},{4,5},{5,4},{6,7},{7,6},{8,9},{9,8},{10,11... | collective-permute-start | bytes 528392 | tf_op jit(solution)/shard_map/ppermute | solution.py:59
  49.3 5.5 %collective-permute-start.5 = (bf16[16,5504]{1,0:T(8,128)(2,1)S(1)}, bf16[16,5504]{1,0:T(8,128)(2,1)S(1)}, u32[]{:S(2)}, u32[]{:S(2)}) collective-permute-start(bf16[16,5504]{1,0:T(8,128)(2,1)S(1)} %get-tuple-element.106.refs_5_), channel_id=1, source_target_pairs={{0,2},{1,3},{2,0},{3,1},{4,6},{5,7},{6,4},{7,5},{8,10},{9,11},{10,... | collective-permute-start | bytes 528392 | tf_op jit(solution)/shard_map/ppermute | solution.py:59
  57.2 7.3 %collective-permute-start.8 = (bf16[16,5504]{1,0:T(8,128)(2,1)S(1)}, bf16[16,5504]{1,0:T(8,128)(2,1)S(1)}, u32[]{:S(2)}, u32[]{:S(2)}) collective-permute-start(bf16[16,5504]{1,0:T(8,128)(2,1)S(1)} %get-tuple-element.115.refs_7_), channel_id=1, source_target_pairs={{0,2},{1,3},{2,0},{3,1},{4,6},{5,7},{6,4},{7,5},{8,10},{9,11},{10,... | collective-permute-start | bytes 528392 | tf_op jit(solution)/shard_map/ppermute | solution.py:59
  58.9 7.4 %collective-permute-start.9 = (bf16[16,5504]{1,0:T(8,128)(2,1)S(1)}, bf16[16,5504]{1,0:T(8,128)(2,1)S(1)}, u32[]{:S(2)}, u32[]{:S(2)}) collective-permute-start(bf16[16,5504]{1,0:T(8,128)(2,1)S(1)} %get-tuple-element.116), channel_id=1, source_target_pairs={{0,1},{1,0},{2,3},{3,2},{4,5},{5,4},{6,7},{7,6},{8,9},{9,8},{10,11... | collective-permute-start | bytes 528392 | tf_op jit(solution)/shard_map/ppermute | solution.py:59
  60.0 10.3 %collective-permute-start.12 = (bf16[32,5504]{1,0:T(8,128)(2,1)S(1)}, bf16[32,5504]{1,0:T(8,128)(2,1)S(1)}, u32[]{:S(2)}, u32[]{:S(2)}) collective-permute-start(bf16[32,5504]{1,0:T(8,128)(2,1)S(1)} %pad_maximum_fusion.2.refs_5_), channel_id=1, source_target_pairs={{0,1},{1,0},{2,3},{3,2},{4,5},{5,4},{6,7},{7,6},{8,9},{9,8},{10,11... | collective-permute-start | bytes 1056776 | tf_op jit(solution)/shard_map/ppermute | solution.py:59
  60.9 9.4 %collective-permute-start.11 = (bf16[32,5504]{1,0:T(8,128)(2,1)S(1)}, bf16[32,5504]{1,0:T(8,128)(2,1)S(1)}, u32[]{:S(2)}, u32[]{:S(2)}) collective-permute-start(bf16[32,5504]{1,0:T(8,128)(2,1)S(1)} %pad_maximum_fusion.2.refs_5_), channel_id=1, source_target_pairs={{0,2},{1,3},{2,0},{3,1},{4,6},{5,7},{6,4},{7,5},{8,10},{9,11},{10,... | collective-permute-start | bytes 1056776 | tf_op jit(solution)/shard_map/ppermute | solution.py:59
  61.3 17.3 %collective-permute-start.7 = (bf16[80,2560]{1,0:T(8,128)(2,1)S(1)}, bf16[80,2560]{1,0:T(8,128)(2,1)S(1)}, u32[]{:S(2)}, u32[]{:S(2)}) collective-permute-start(bf16[80,2560]{1,0:T(8,128)(2,1)S(1)} %get-tuple-element.112), channel_id=1, source_target_pairs={{0,8},{1,9},{2,10},{3,11},{4,12},{5,13},{6,14},{7,15},{8,16},{9,17... | collective-permute-start | bytes 1228808 | tf_op jit(solution)/shard_map/ppermute | solution.py:59
  66.3 12.3 %collective-permute-start.10 = (bf16[16,5504]{1,0:T(8,128)(2,1)S(1)}, bf16[16,5504]{1,0:T(8,128)(2,1)S(1)}, u32[]{:S(2)}, u32[]{:S(2)}) collective-permute-start(bf16[16,5504]{1,0:T(8,128)(2,1)S(1)} %add_convert_fusion.3), channel_id=1, source_target_pairs={{0,12},{1,13},{2,14},{3,15},{4,8},{5,9},{6,10},{7,11},{8,20},{9,21... | collective-permute-start | bytes 528392 | tf_op jit(solution)/shard_map/ppermute | solution.py:59
  70.3 9.5 %collective-permute-start.13 = (bf16[16,5504]{1,0:T(8,128)(2,1)S(1)}, bf16[16,5504]{1,0:T(8,128)(2,1)S(1)}, u32[]{:S(2)}, u32[]{:S(2)}) collective-permute-start(bf16[16,5504]{1,0:T(8,128)(2,1)S(1)} %get-tuple-element.124), channel_id=1, source_target_pairs={{0,10},{1,11},{2,8},{3,9},{4,14},{5,15},{6,12},{7,13},{8,18},{9,19... | collective-permute-start | bytes 528392 | tf_op jit(solution)/shard_map/ppermute | solution.py:59
  70.3 9.5 %collective-permute-start.14 = (bf16[16,5504]{1,0:T(8,128)(2,1)S(1)}, bf16[16,5504]{1,0:T(8,128)(2,1)S(1)}, u32[]{:S(2)}, u32[]{:S(2)}) collective-permute-start(bf16[16,5504]{1,0:T(8,128)(2,1)S(1)} %get-tuple-element.125), channel_id=1, source_target_pairs={{0,9},{1,8},{2,11},{3,10},{4,13},{5,12},{6,15},{7,14},{8,17},{9,16... | collective-permute-start | bytes 528392 | tf_op jit(solution)/shard_map/ppermute | solution.py:59
  72.3 8.7 %collective-permute-start.15 = (bf16[16,5504]{1,0:T(8,128)(2,1)S(1)}, bf16[16,5504]{1,0:T(8,128)(2,1)S(1)}, u32[]{:S(2)}, u32[]{:S(2)}) collective-permute-start(bf16[16,5504]{1,0:T(8,128)(2,1)S(1)} %get-tuple-element.126), channel_id=1, source_target_pairs={{0,8},{1,9},{2,10},{3,11},{4,12},{5,13},{6,14},{7,15},{8,16},{9,17... | collective-permute-start | bytes 528392 | tf_op jit(solution)/shard_map/ppermute | solution.py:59
  81.9 12.5 %collective-permute-start.19 = (bf16[144,2560]{1,0:T(8,128)(2,1)S(1)}, bf16[144,2560]{1,0:T(8,128)(2,1)S(1)}, u32[]{:S(2)}, u32[]{:S(2)}) collective-permute-start(bf16[144,2560]{1,0:T(8,128)(2,1)S(1)} %get-tuple-element.137), channel_id=1, source_target_pairs={{0,24},{1,25},{2,26},{3,27},{4,28},{5,29},{6,30},{7,31},{8,0},{9,1... | collective-permute-start | bytes 2211848 | tf_op jit(solution)/shard_map/ppermute | solution.py:59
  81.9 11.7 %collective-permute-start.16 = (bf16[16,5504]{1,0:T(8,128)(2,1)S(1)}, bf16[16,5504]{1,0:T(8,128)(2,1)S(1)}, u32[]{:S(2)}, u32[]{:S(2)}) collective-permute-start(bf16[16,5504]{1,0:T(8,128)(2,1)S(1)} %get-tuple-element.135), channel_id=1, source_target_pairs={{0,4},{1,5},{2,6},{3,7},{4,0},{5,1},{6,2},{7,3},{8,12},{9,13},{10,... | collective-permute-start | bytes 528392 | tf_op jit(solution)/shard_map/ppermute | solution.py:59
  83.8 9.8 %collective-permute-start.18 = (bf16[16,5504]{1,0:T(8,128)(2,1)S(1)}, bf16[16,5504]{1,0:T(8,128)(2,1)S(1)}, u32[]{:S(2)}, u32[]{:S(2)}) collective-permute-start(bf16[16,5504]{1,0:T(8,128)(2,1)S(1)} %get-tuple-element.136.refs_9_), channel_id=1, source_target_pairs={{0,1},{1,0},{2,3},{3,2},{4,5},{5,4},{6,7},{7,6},{8,9},{9,8},{10,11... | collective-permute-start | bytes 528392 | tf_op jit(solution)/shard_map/ppermute | solution.py:59
  84.4 10.0 %collective-permute-start.17 = (bf16[16,5504]{1,0:T(8,128)(2,1)S(1)}, bf16[16,5504]{1,0:T(8,128)(2,1)S(1)}, u32[]{:S(2)}, u32[]{:S(2)}) collective-permute-start(bf16[16,5504]{1,0:T(8,128)(2,1)S(1)} %get-tuple-element.136.refs_9_), channel_id=1, source_target_pairs={{0,2},{1,3},{2,0},{3,1},{4,6},{5,7},{6,4},{7,5},{8,10},{9,11},{10,... | collective-permute-start | bytes 528392 | tf_op jit(solution)/shard_map/ppermute | solution.py:59
  94.3 5.5 %collective-permute-start.21 = (bf16[16,5504]{1,0:T(8,128)(2,1)S(1)}, bf16[16,5504]{1,0:T(8,128)(2,1)S(1)}, u32[]{:S(2)}, u32[]{:S(2)}) collective-permute-start(bf16[16,5504]{1,0:T(8,128)(2,1)S(1)} %collective-permute-done.16.refs_9_), channel_id=1, source_target_pairs={{0,1},{1,0},{2,3},{3,2},{4,5},{5,4},{6,7},{7,6},{8,9},{9,8},{10,11... | collective-permute-start | bytes 528392 | tf_op jit(solution)/shard_map/ppermute | solution.py:59
  95.3 5.5 %collective-permute-start.20 = (bf16[16,5504]{1,0:T(8,128)(2,1)S(1)}, bf16[16,5504]{1,0:T(8,128)(2,1)S(1)}, u32[]{:S(2)}, u32[]{:S(2)}) collective-permute-start(bf16[16,5504]{1,0:T(8,128)(2,1)S(1)} %collective-permute-done.16.refs_9_), channel_id=1, source_target_pairs={{0,2},{1,3},{2,0},{3,1},{4,6},{5,7},{6,4},{7,5},{8,10},{9,11},{10,... | collective-permute-start | bytes 528392 | tf_op jit(solution)/shard_map/ppermute | solution.py:59
  103.4 7.2 %collective-permute-start.22 = (bf16[16,5504]{1,0:T(8,128)(2,1)S(1)}, bf16[16,5504]{1,0:T(8,128)(2,1)S(1)}, u32[]{:S(2)}, u32[]{:S(2)}) collective-permute-start(bf16[16,5504]{1,0:T(8,128)(2,1)S(1)} %get-tuple-element.147), channel_id=1, source_target_pairs={{0,2},{1,3},{2,0},{3,1},{4,6},{5,7},{6,4},{7,5},{8,10},{9,11},{10,... | collective-permute-start | bytes 528392 | tf_op jit(solution)/shard_map/ppermute | solution.py:59
  104.4 6.7 %collective-permute-start.23 = (bf16[16,5504]{1,0:T(8,128)(2,1)S(1)}, bf16[16,5504]{1,0:T(8,128)(2,1)S(1)}, u32[]{:S(2)}, u32[]{:S(2)}) collective-permute-start(bf16[16,5504]{1,0:T(8,128)(2,1)S(1)} %get-tuple-element.148), channel_id=1, source_target_pairs={{0,1},{1,0},{2,3},{3,2},{4,5},{5,4},{6,7},{7,6},{8,9},{9,8},{10,11... | collective-permute-start | bytes 528392 | tf_op jit(solution)/shard_map/ppermute | solution.py:59
  106.3 9.5 %collective-permute-start.25 = (bf16[16,5504]{1,0:T(8,128)(2,1)S(1)}, bf16[16,5504]{1,0:T(8,128)(2,1)S(1)}, u32[]{:S(2)}, u32[]{:S(2)}) collective-permute-start(bf16[16,5504]{1,0:T(8,128)(2,1)S(1)} %get-tuple-element.154), channel_id=1, source_target_pairs={{0,2},{1,3},{2,0},{3,1},{4,6},{5,7},{6,4},{7,5},{8,10},{9,11},{10,... | collective-permute-start | bytes 528392 | tf_op jit(solution)/shard_map/ppermute | solution.py:59
  107.4 8.8 %collective-permute-start.26 = (bf16[16,5504]{1,0:T(8,128)(2,1)S(1)}, bf16[16,5504]{1,0:T(8,128)(2,1)S(1)}, u32[]{:S(2)}, u32[]{:S(2)}) collective-permute-start(bf16[16,5504]{1,0:T(8,128)(2,1)S(1)} %get-tuple-element.155), channel_id=1, source_target_pairs={{0,1},{1,0},{2,3},{3,2},{4,5},{5,4},{6,7},{7,6},{8,9},{9,8},{10,11... | collective-permute-start | bytes 528392 | tf_op jit(solution)/shard_map/ppermute | solution.py:59
  111.3 11.3 %collective-permute-start.24 = (bf16[16,5504]{1,0:T(8,128)(2,1)S(1)}, bf16[16,5504]{1,0:T(8,128)(2,1)S(1)}, u32[]{:S(2)}, u32[]{:S(2)}) collective-permute-start(bf16[16,5504]{1,0:T(8,128)(2,1)S(1)} %add_convert_fusion.2), channel_id=1, source_target_pairs={{0,28},{1,29},{2,30},{3,31},{4,24},{5,25},{6,26},{7,27},{8,4},{9,5... | collective-permute-start | bytes 528392 | tf_op jit(solution)/shard_map/ppermute | solution.py:59
  111.3 11.2 %collective-permute-start.30 = (bf16[16,5504]{1,0:T(8,128)(2,1)S(1)}, bf16[16,5504]{1,0:T(8,128)(2,1)S(1)}, u32[]{:S(2)}, u32[]{:S(2)}) collective-permute-start(bf16[16,5504]{1,0:T(8,128)(2,1)S(1)} %get-tuple-element.169.refs_11_), channel_id=1, source_target_pairs={{0,26},{1,27},{2,24},{3,25},{4,30},{5,31},{6,28},{7,29},{8,2},{9,3... | collective-permute-start | bytes 528392 | tf_op jit(solution)/shard_map/ppermute | solution.py:59
  115.8 6.7 %collective-permute-start.31 = (bf16[16,5504]{1,0:T(8,128)(2,1)S(1)}, bf16[16,5504]{1,0:T(8,128)(2,1)S(1)}, u32[]{:S(2)}, u32[]{:S(2)}) collective-permute-start(bf16[16,5504]{1,0:T(8,128)(2,1)S(1)} %get-tuple-element.170), channel_id=1, source_target_pairs={{0,25},{1,24},{2,27},{3,26},{4,29},{5,28},{6,31},{7,30},{8,1},{9,0... | collective-permute-start | bytes 528392 | tf_op jit(solution)/shard_map/ppermute | solution.py:59
  115.8 9.0 %collective-permute-start.32 = (bf16[16,5504]{1,0:T(8,128)(2,1)S(1)}, bf16[16,5504]{1,0:T(8,128)(2,1)S(1)}, u32[]{:S(2)}, u32[]{:S(2)}) collective-permute-start(bf16[16,5504]{1,0:T(8,128)(2,1)S(1)} %get-tuple-element.171), channel_id=1, source_target_pairs={{0,24},{1,25},{2,26},{3,27},{4,28},{5,29},{6,30},{7,31},{8,0},{9,1... | collective-permute-start | bytes 528392 | tf_op jit(solution)/shard_map/ppermute | solution.py:59
  125.8 10.9 %collective-permute-start.33 = (bf16[16,5504]{1,0:T(8,128)(2,1)S(1)}, bf16[16,5504]{1,0:T(8,128)(2,1)S(1)}, u32[]{:S(2)}, u32[]{:S(2)}) collective-permute-start(bf16[16,5504]{1,0:T(8,128)(2,1)S(1)} %get-tuple-element.177), channel_id=1, source_target_pairs={{0,4},{1,5},{2,6},{3,7},{4,0},{5,1},{6,2},{7,3},{8,12},{9,13},{10,... | collective-permute-start | bytes 528392 | tf_op jit(solution)/shard_map/ppermute | solution.py:59
  125.8 10.8 %collective-permute-start.35 = (bf16[16,5504]{1,0:T(8,128)(2,1)S(1)}, bf16[16,5504]{1,0:T(8,128)(2,1)S(1)}, u32[]{:S(2)}, u32[]{:S(2)}) collective-permute-start(bf16[16,5504]{1,0:T(8,128)(2,1)S(1)} %get-tuple-element.178.refs_9_), channel_id=1, source_target_pairs={{0,1},{1,0},{2,3},{3,2},{4,5},{5,4},{6,7},{7,6},{8,9},{9,8},{10,11... | collective-permute-start | bytes 528392 | tf_op jit(solution)/shard_map/ppermute | solution.py:59
  127.0 11.1 %collective-permute-start.34 = (bf16[16,5504]{1,0:T(8,128)(2,1)S(1)}, bf16[16,5504]{1,0:T(8,128)(2,1)S(1)}, u32[]{:S(2)}, u32[]{:S(2)}) collective-permute-start(bf16[16,5504]{1,0:T(8,128)(2,1)S(1)} %get-tuple-element.178.refs_9_), channel_id=1, source_target_pairs={{0,2},{1,3},{2,0},{3,1},{4,6},{5,7},{6,4},{7,5},{8,10},{9,11},{10,... | collective-permute-start | bytes 528392 | tf_op jit(solution)/shard_map/ppermute | solution.py:59
  129.2 12.9 %collective-permute-start.28 = (bf16[16,5504]{1,0:T(8,128)(2,1)S(1)}, bf16[16,5504]{1,0:T(8,128)(2,1)S(1)}, u32[]{:S(2)}, u32[]{:S(2)}) collective-permute-start(bf16[16,5504]{1,0:T(8,128)(2,1)S(1)} %get-tuple-element.161), channel_id=1, source_target_pairs={{0,2},{1,3},{2,0},{3,1},{4,6},{5,7},{6,4},{7,5},{8,10},{9,11},{10,... | collective-permute-start | bytes 528392 | tf_op jit(solution)/shard_map/ppermute | solution.py:59
  129.9 12.2 %collective-permute-start.29 = (bf16[16,5504]{1,0:T(8,128)(2,1)S(1)}, bf16[16,5504]{1,0:T(8,128)(2,1)S(1)}, u32[]{:S(2)}, u32[]{:S(2)}) collective-permute-start(bf16[16,5504]{1,0:T(8,128)(2,1)S(1)} %get-tuple-element.162), channel_id=1, source_target_pairs={{0,1},{1,0},{2,3},{3,2},{4,5},{5,4},{6,7},{7,6},{8,9},{9,8},{10,11... | collective-permute-start | bytes 528392 | tf_op jit(solution)/shard_map/ppermute | solution.py:59
  136.7 11.2 %collective-permute-start.27 = (bf16[16,5504]{1,0:T(8,128)(2,1)S(1)}, bf16[16,5504]{1,0:T(8,128)(2,1)S(1)}, u32[]{:S(2)}, u32[]{:S(2)}) collective-permute-start(bf16[16,5504]{1,0:T(8,128)(2,1)S(1)} %add_convert_fusion.1), channel_id=1, source_target_pairs={{0,4},{1,5},{2,6},{3,7},{4,0},{5,1},{6,2},{7,3},{8,12},{9,13},{10,... | collective-permute-start | bytes 528392 | tf_op jit(solution)/shard_map/ppermute | solution.py:59
  138.0 11.8 %collective-permute-start.37 = (bf16[16,5504]{1,0:T(8,128)(2,1)S(1)}, bf16[16,5504]{1,0:T(8,128)(2,1)S(1)}, u32[]{:S(2)}, u32[]{:S(2)}) collective-permute-start(bf16[16,5504]{1,0:T(8,128)(2,1)S(1)} %collective-permute-done.33.refs_9_), channel_id=1, source_target_pairs={{0,1},{1,0},{2,3},{3,2},{4,5},{5,4},{6,7},{7,6},{8,9},{9,8},{10,11... | collective-permute-start | bytes 528392 | tf_op jit(solution)/shard_map/ppermute | solution.py:59
  139.0 10.9 %collective-permute-start.36 = (bf16[16,5504]{1,0:T(8,128)(2,1)S(1)}, bf16[16,5504]{1,0:T(8,128)(2,1)S(1)}, u32[]{:S(2)}, u32[]{:S(2)}) collective-permute-start(bf16[16,5504]{1,0:T(8,128)(2,1)S(1)} %collective-permute-done.33.refs_9_), channel_id=1, source_target_pairs={{0,2},{1,3},{2,0},{3,1},{4,6},{5,7},{6,4},{7,5},{8,10},{9,11},{10,... | collective-permute-start | bytes 528392 | tf_op jit(solution)/shard_map/ppermute | solution.py:59
  151.9 7.4 %collective-permute-start.38 = (bf16[16,5504]{1,0:T(8,128)(2,1)S(1)}, bf16[16,5504]{1,0:T(8,128)(2,1)S(1)}, u32[]{:S(2)}, u32[]{:S(2)}) collective-permute-start(bf16[16,5504]{1,0:T(8,128)(2,1)S(1)} %get-tuple-element.188), channel_id=1, source_target_pairs={{0,2},{1,3},{2,0},{3,1},{4,6},{5,7},{6,4},{7,5},{8,10},{9,11},{10,... | collective-permute-start | bytes 528392 | tf_op jit(solution)/shard_map/ppermute | solution.py:59
  152.0 7.4 %collective-permute-start.39 = (bf16[16,5504]{1,0:T(8,128)(2,1)S(1)}, bf16[16,5504]{1,0:T(8,128)(2,1)S(1)}, u32[]{:S(2)}, u32[]{:S(2)}) collective-permute-start(bf16[16,5504]{1,0:T(8,128)(2,1)S(1)} %get-tuple-element.189), channel_id=1, source_target_pairs={{0,1},{1,0},{2,3},{3,2},{4,5},{5,4},{6,7},{7,6},{8,9},{9,8},{10,11... | collective-permute-start | bytes 528392 | tf_op jit(solution)/shard_map/ppermute | solution.py:59
  153.0 9.8 %collective-permute-start.41 = (bf16[16,5504]{1,0:T(8,128)(2,1)S(1)}, bf16[16,5504]{1,0:T(8,128)(2,1)S(1)}, u32[]{:S(2)}, u32[]{:S(2)}) collective-permute-start(bf16[16,5504]{1,0:T(8,128)(2,1)S(1)} %get-tuple-element.186.refs_11_), channel_id=1, source_target_pairs={{0,2},{1,3},{2,0},{3,1},{4,6},{5,7},{6,4},{7,5},{8,10},{9,11},{10,... | collective-permute-start | bytes 528392 | tf_op jit(solution)/shard_map/ppermute | solution.py:59
  154.9 7.9 %collective-permute-start.42 = (bf16[16,5504]{1,0:T(8,128)(2,1)S(1)}, bf16[16,5504]{1,0:T(8,128)(2,1)S(1)}, u32[]{:S(2)}, u32[]{:S(2)}) collective-permute-start(bf16[16,5504]{1,0:T(8,128)(2,1)S(1)} %get-tuple-element.190), channel_id=1, source_target_pairs={{0,1},{1,0},{2,3},{3,2},{4,5},{5,4},{6,7},{7,6},{8,9},{9,8},{10,11... | collective-permute-start | bytes 528392 | tf_op jit(solution)/shard_map/ppermute | solution.py:59
  159.5 8.8 %collective-permute-start.40 = (bf16[16,5504]{1,0:T(8,128)(2,1)S(1)}, bf16[16,5504]{1,0:T(8,128)(2,1)S(1)}, u32[]{:S(2)}, u32[]{:S(2)}) collective-permute-start(bf16[16,5504]{1,0:T(8,128)(2,1)S(1)} %add_convert_fusion), channel_id=1, source_target_pairs={{0,4},{1,5},{2,6},{3,7},{4,0},{5,1},{6,2},{7,3},{8,12},{9,13},{10,... | collective-permute-start | bytes 528392 | tf_op jit(solution)/shard_map/ppermute | solution.py:59
  (1 other events, 2.3 us)
where the time goes:
time: 170 us
  waiting for transfers between devices  94.5 us (56%)
  starting transfers between devices  46.3 us (27%)
  Pallas kernels  22.9 us (13%)
  local copies, waits for them, and re-layouts  4.53 us (3%)
    ppermute x43, waiting for transfers between devices, shift(): return lax.ppermute(value, ('section', 'expert'), pairs)  94.5 us
    ppermute x43, starting transfers between devices, shift(): return lax.ppermute(value, ('section', 'expert'), pairs)  46.3 us
    pallas_call x15, Pallas kernels, call(): pl.pallas_call(reading, out_shape=list(outs), in_specs=[vmem] * read + [p...  22.9 us
  transfers between devices with their start and end apart: 43, of which 25 were waited for; matrix products, arithmetic and copies ran while one was open for 1% of the time, Pallas kernels for 7%

commit v1 on v0

--- a/solution.py
+++ b/solution.py
@@ -576,8 +576,8 @@
     cross_g, own_g = around(cross_g), [own_z, own_g, own_x]
     back = bind(expert_call, back_kernel, box, packs)
     fin = fin_back + own_home(own_fin, 0)
-    own_grad = back(own_g, own_kept0, after=fin)[0]
-    cross_grad = back(cross_g, cross_kept0, after=own_grad[:1])[0]
+    cross_grad = back(cross_g, cross_kept0)[0]
+    own_grad = back(own_g, own_kept0, after=cross_grad[:1] + tuple(fin))[0]
     got = home(sums(cross_grad), 0) + own_home(own_grad, 0)
     (g0,) = call(
         bind(last_kernel, box, experts),

time: 170 us -> 170 us (level)
  starting transfers between devices: 46.3 us -> 43 us
  waiting for transfers between devices: 94.5 us -> 97.7 us
    ppermute x43, waiting for transfers between devices: 94.5 us -> 97.7 us  [shift(): return lax.ppermute(value, ('section', 'expert'), pairs)]
    ppermute x43, starting transfers between devices: 46.3 us -> 43 us  [shift(): return lax.ppermute(value, ('section', 'expert'), pairs)]
  transfers between devices with their start and end apart: 43 -> 43, of which waited for: 25 -> 25; matrix products, arithmetic and copies ran while one was open for 1% -> 2% of each run, Pallas kernels for 7% -> 9%
where the time goes in v1:
time: 170 us
  waiting for transfers between devices  97.7 us (57%)
  starting transfers between devices  43 us (25%)
  Pallas kernels  23 us (14%)
  local copies, waits for them, and re-layouts  4.53 us (3%)
    ppermute x43, waiting for transfers between devices, shift(): return lax.ppermute(value, ('section', 'expert'), pairs)  97.7 us
    ppermute x43, starting transfers between devices, shift(): return lax.ppermute(value, ('section', 'expert'), pairs)  43 us
    pallas_call x15, Pallas kernels, call(): pl.pallas_call(reading, out_shape=list(outs), in_specs=[vmem] * read + [p...  23 us
  transfers between devices with their start and end apart: 43, of which 25 were waited for; matrix products, arithmetic and copies ran while one was open for 2% of the time, Pallas kernels for 9%

profile of v1, /device:TPU:0, one launch (start us, length us, event | category | flops | bytes accessed | tf_op | source)
XLA Modules:
  0.0 169.7 jit_solution(4794412386510556336)
XLA Ops:
  0.6 1.2 slice.40
  1.8 1.1 slice.41
  3.1 3.0 %collective-permute-start = (bf16[336,2560]{1,0:T(8,128)(2,1)S(1)}, bf16[336,2560]{1,0:T(8,128)(2,1)S(1)}, u32[]{:S(2)}, u32[]{:S(2)}) collective-permute-start(bf16[336,2560]{1,0:T(8,128)(2,1)S(1)} %pad_maximum_fusion.refs_5_.refs_0_), channel_id=1, source_target_pairs={{0,1},{1,0},{2,3},{3,2},{4,5},{5,4},{6,7},{7,6},{8,9},{9,8},{10,11... | collective-permute-start | bytes 5160968 | tf_op jit(solution)/shard_map/ppermute | solution.py:59
  6.1 1.0 slice.42
  7.2 1.1 slice.43
  8.4 1.6 collective-permute-start.1
  10.9 2.6 %collective-permute-start.2 = (bf16[32,5504]{1,0:T(8,128)(2,1)S(1)}, bf16[32,5504]{1,0:T(8,128)(2,1)S(1)}, u32[]{:S(2)}, u32[]{:S(2)}) collective-permute-start(bf16[32,5504]{1,0:T(8,128)(2,1)S(1)} %get-tuple-element.97), channel_id=1, source_target_pairs={{0,4},{1,5},{2,6},{3,7},{4,0},{5,1},{6,2},{7,3},{8,12},{9,13},{10,... | collective-permute-start | bytes 1056776 | tf_op jit(solution)/shard_map/ppermute | solution.py:59
  14.5 32.9 %collective-permute-done.4.refs_6_ = bf16[16,5504]{1,0:T(8,128)(2,1)S(1)} collective-permute-done((bf16[16,5504]{1,0:T(8,128)(2,1)S(1)}, bf16[16,5504]{1,0:T(8,128)(2,1)S(1)}, u32[]{:S(2)}, u32[]{:S(2)}) %collective-permute-start.4) | collective-permute-done | bytes 176160 | tf_op jit(solution)/shard_map/ppermute | solution.py:59
  49.3 1.6 collective-permute-start.5
  50.9 2.9 %collective-permute-done.6.refs_6_ = bf16[16,5504]{1,0:T(8,128)(2,1)S(1)} collective-permute-done((bf16[16,5504]{1,0:T(8,128)(2,1)S(1)}, bf16[16,5504]{1,0:T(8,128)(2,1)S(1)}, u32[]{:S(2)}, u32[]{:S(2)}) %collective-permute-start.6) | collective-permute-done | bytes 176160 | tf_op jit(solution)/shard_map/ppermute | solution.py:59
  54.8 2.5 %shard_map.96 = (bf16[16,5504]{1,0:T(8,128)(2,1)S(1)}, bf16[16,5504]{1,0:T(8,128)(2,1)S(1)}, bf16[16,5504]{1,0:T(8,128)(2,1)S(1)}, f32[96,224]{1,0:T(8,128)S(1)}...) custom-call(bf16[336,2560]{1,0:T(8,128)(2,1)S(1)} %pad_maximum_fusion.refs_5_.refs_0_, ...), custom_call_target="tpu_custom_call" | custom-call | flops 566231040 | bytes 7249920 | tf_op jit(solution)/shard_map/pallas_call | solution.py:71
  57.2 1.6 collective-permute-start.8
  58.9 1.1 collective-permute-start.9
  61.3 2.5 %shard_map.97 = (bf16[16,5504]{1,0:T(8,128)(2,1)S(1)}, bf16[16,5504]{1,0:T(8,128)(2,1)S(1)}, bf16[16,5504]{1,0:T(8,128)(2,1)S(1)}, f32[96,224]{1,0:T(8,128)S(1)}...) custom-call(bf16[336,2560]{1,0:T(8,128)(2,1)S(1)} %pad_maximum_fusion.refs_5_.refs_0_, ...), custom_call_target="tpu_custom_call" | custom-call | flops 566231040 | bytes 7249920 | tf_op jit(solution)/shard_map/pallas_call | solution.py:71
  64.5 1.7 %collective-permute-done.9 = bf16[16,5504]{1,0:T(8,128)(2,1)S(1)} collective-permute-done((bf16[16,5504]{1,0:T(8,128)(2,1)S(1)}, bf16[16,5504]{1,0:T(8,128)(2,1)S(1)}, u32[]{:S(2)}, u32[]{:S(2)}) %collective-permute-start.9) | collective-permute-done | bytes 176160 | tf_op jit(solution)/shard_map/ppermute | solution.py:59
  66.3 1.5 collective-permute-start.10
  67.8 2.5 %collective-permute-done.12.refs_6_ = bf16[32,5504]{1,0:T(8,128)(2,1)S(1)} collective-permute-done((bf16[32,5504]{1,0:T(8,128)(2,1)S(1)}, bf16[32,5504]{1,0:T(8,128)(2,1)S(1)}, u32[]{:S(2)}, u32[]{:S(2)}) %collective-permute-start.12) | collective-permute-done | bytes 352288 | tf_op jit(solution)/shard_map/ppermute | solution.py:59
  70.3 1.9 %collective-permute-start.14 = (bf16[16,5504]{1,0:T(8,128)(2,1)S(1)}, bf16[16,5504]{1,0:T(8,128)(2,1)S(1)}, u32[]{:S(2)}, u32[]{:S(2)}) collective-permute-start(bf16[16,5504]{1,0:T(8,128)(2,1)S(1)} %get-tuple-element.125), channel_id=1, source_target_pairs={{0,9},{1,8},{2,11},{3,10},{4,13},{5,12},{6,15},{7,14},{8,17},{9,16... | collective-permute-start | bytes 528392 | tf_op jit(solution)/shard_map/ppermute | solution.py:59
  72.3 6.4 %collective-permute-done.10.refs_4_ = bf16[16,5504]{1,0:T(8,128)(2,1)S(1)} collective-permute-done((bf16[16,5504]{1,0:T(8,128)(2,1)S(1)}, bf16[16,5504]{1,0:T(8,128)(2,1)S(1)}, u32[]{:S(2)}, u32[]{:S(2)}) %collective-permute-start.10) | collective-permute-done | bytes 176160 | tf_op jit(solution)/shard_map/ppermute | solution.py:59
  78.7 1.2 collective-permute-done.13.refs_5_
  79.8 1.1 collective-permute-done.15.refs_7_
  81.9 1.9 %collective-permute-start.16 = (bf16[16,5504]{1,0:T(8,128)(2,1)S(1)}, bf16[16,5504]{1,0:T(8,128)(2,1)S(1)}, u32[]{:S(2)}, u32[]{:S(2)}) collective-permute-start(bf16[16,5504]{1,0:T(8,128)(2,1)S(1)} %get-tuple-element.135), channel_id=1, source_target_pairs={{0,4},{1,5},{2,6},{3,7},{4,0},{5,1},{6,2},{7,3},{8,12},{9,13},{10,... | collective-permute-start | bytes 528392 | tf_op jit(solution)/shard_map/ppermute | solution.py:59
  84.4 2.5 %collective-permute-start.17 = (bf16[16,5504]{1,0:T(8,128)(2,1)S(1)}, bf16[16,5504]{1,0:T(8,128)(2,1)S(1)}, u32[]{:S(2)}, u32[]{:S(2)}) collective-permute-start(bf16[16,5504]{1,0:T(8,128)(2,1)S(1)} %get-tuple-element.136.refs_9_), channel_id=1, source_target_pairs={{0,2},{1,3},{2,0},{3,1},{4,6},{5,7},{6,4},{7,5},{8,10},{9,11},{10,... | collective-permute-start | bytes 528392 | tf_op jit(solution)/shard_map/ppermute | solution.py:59
  86.9 6.7 %collective-permute-done.16.refs_9_ = bf16[16,5504]{1,0:T(8,128)(2,1)S(1)} collective-permute-done((bf16[16,5504]{1,0:T(8,128)(2,1)S(1)}, bf16[16,5504]{1,0:T(8,128)(2,1)S(1)}, u32[]{:S(2)}, u32[]{:S(2)}) %collective-permute-start.16) | collective-permute-done | bytes 176160 | tf_op jit(solution)/shard_map/ppermute | solution.py:59
  94.3 1.0 collective-permute-start.21
  97.1 2.6 %shard_map.101 = (bf16[16,5504]{1,0:T(8,128)(2,1)S(1)}, bf16[16,5504]{1,0:T(8,128)(2,1)S(1)}, bf16[16,5504]{1,0:T(8,128)(2,1)S(1)}, f32[96,224]{1,0:T(8,128)S(1)...) custom-call(bf16[336,2560]{1,0:T(8,128)(2,1)S(1)} %pad_maximum_fusion.refs_5_.refs_0_, ...), custom_call_target="tpu_custom_call" | custom-call | flops 566231040 | bytes 7397376 | tf_op jit(solution)/shard_map/pallas_call | solution.py:71
  100.8 2.6 %shard_map.102 = (bf16[16,5504]{1,0:T(8,128)(2,1)S(1)}, bf16[16,5504]{1,0:T(8,128)(2,1)S(1)}, bf16[16,5504]{1,0:T(8,128)(2,1)S(1)}, f32[96,224]{1,0:T(8,128)S(1)...) custom-call(bf16[336,2560]{1,0:T(8,128)(2,1)S(1)} %pad_maximum_fusion.refs_5_.refs_0_, ...), custom_call_target="tpu_custom_call" | custom-call | flops 566231040 | bytes 7397376 | tf_op jit(solution)/shard_map/pallas_call | solution.py:71
  103.4 1.1 collective-permute-start.22
  106.4 1.1 collective-permute-start.25
  108.4 2.3 %collective-permute-done.22 = bf16[16,5504]{1,0:T(8,128)(2,1)S(1)} collective-permute-done((bf16[16,5504]{1,0:T(8,128)(2,1)S(1)}, bf16[16,5504]{1,0:T(8,128)(2,1)S(1)}, u32[]{:S(2)}, u32[]{:S(2)}) %collective-permute-start.22) | collective-permute-done | bytes 176160 | tf_op jit(solution)/shard_map/ppermute | solution.py:59
  111.4 4.5 %collective-permute-start.30 = (bf16[16,5504]{1,0:T(8,128)(2,1)S(1)}, bf16[16,5504]{1,0:T(8,128)(2,1)S(1)}, u32[]{:S(2)}, u32[]{:S(2)}) collective-permute-start(bf16[16,5504]{1,0:T(8,128)(2,1)S(1)} %get-tuple-element.169.refs_11_), channel_id=1, source_target_pairs={{0,26},{1,27},{2,24},{3,25},{4,30},{5,31},{6,28},{7,29},{8,2},{9,3... | collective-permute-start | bytes 528392 | tf_op jit(solution)/shard_map/ppermute | solution.py:59
  116.3 6.3 %collective-permute-done.24.refs_2_ = bf16[16,5504]{1,0:T(8,128)(2,1)S(1)} collective-permute-done((bf16[16,5504]{1,0:T(8,128)(2,1)S(1)}, bf16[16,5504]{1,0:T(8,128)(2,1)S(1)}, u32[]{:S(2)}, u32[]{:S(2)}) %collective-permute-start.24) | collective-permute-done | bytes 176160 | tf_op jit(solution)/shard_map/ppermute | solution.py:59
  122.6 2.3 %collective-permute-done.32.refs_5_ = bf16[16,5504]{1,0:T(8,128)(2,1)S(1)} collective-permute-done((bf16[16,5504]{1,0:T(8,128)(2,1)S(1)}, bf16[16,5504]{1,0:T(8,128)(2,1)S(1)}, u32[]{:S(2)}, u32[]{:S(2)}) %collective-permute-start.32) | collective-permute-done | bytes 176160 | tf_op jit(solution)/shard_map/ppermute | solution.py:59
  125.9 1.1 collective-permute-start.35
  127.0 1.4 collective-permute-start.34
  128.4 8.3 %collective-permute-done.33.refs_9_ = bf16[16,5504]{1,0:T(8,128)(2,1)S(1)} collective-permute-done((bf16[16,5504]{1,0:T(8,128)(2,1)S(1)}, bf16[16,5504]{1,0:T(8,128)(2,1)S(1)}, u32[]{:S(2)}, u32[]{:S(2)}) %collective-permute-start.33) | collective-permute-done | bytes 176160 | tf_op jit(solution)/shard_map/ppermute | solution.py:59
  136.7 1.1 collective-permute-done.34.refs_8_
  139.6 2.1 %collective-permute-start.28 = (bf16[16,5504]{1,0:T(8,128)(2,1)S(1)}, bf16[16,5504]{1,0:T(8,128)(2,1)S(1)}, u32[]{:S(2)}, u32[]{:S(2)}) collective-permute-start(bf16[16,5504]{1,0:T(8,128)(2,1)S(1)} %get-tuple-element.161), channel_id=1, source_target_pairs={{0,2},{1,3},{2,0},{3,1},{4,6},{5,7},{6,4},{7,5},{8,10},{9,11},{10,... | collective-permute-start | bytes 528392 | tf_op jit(solution)/shard_map/ppermute | solution.py:59
  141.7 1.0 collective-permute-start.29
  143.1 1.4 collective-permute-done.37.refs_10_
  144.6 4.7 %collective-permute-done.36.refs_8_ = bf16[16,5504]{1,0:T(8,128)(2,1)S(1)} collective-permute-done((bf16[16,5504]{1,0:T(8,128)(2,1)S(1)}, bf16[16,5504]{1,0:T(8,128)(2,1)S(1)}, u32[]{:S(2)}, u32[]{:S(2)}) %collective-permute-start.36) | collective-permute-done | bytes 176160 | tf_op jit(solution)/shard_map/ppermute | solution.py:59
  149.3 2.0 %shard_map.107 = (bf16[16,5504]{1,0:T(8,128)(2,1)S(1)}, bf16[16,5504]{1,0:T(8,128)(2,1)S(1)}, bf16[16,5504]{1,0:T(8,128)(2,1)S(1)}) custom-call(bf16[336,2560]{1,0:T(8,128)(2,1)S(1)} %pad_maximum_fusion.refs_5_.refs_0_, bf16[336,2560]{1,0:T(8,128)(2,1)S(1)} %collective-permute-done.refs_1_, bf16[240,2560]{1,0:T(8,128)(2,1)S(1)} %pad_maximum_fusion.1.refs_6_.refs_2_, ...), custom_call_target="tpu_custom_call" | custom-call | flops 566231040 | bytes 7249920 | tf_op jit(solution)/shard_map/pallas_call | solution.py:71
  152.1 1.6 collective-permute-done.28.refs_3_.refs_13_
  153.7 2.0 %shard_map.108 = (bf16[16,5504]{1,0:T(8,128)(2,1)S(1)}, bf16[16,5504]{1,0:T(8,128)(2,1)S(1)}, bf16[16,5504]{1,0:T(8,128)(2,1)S(1)}) custom-call(bf16[336,2560]{1,0:T(8,128)(2,1)S(1)} %pad_maximum_fusion.refs_5_.refs_0_, bf16[336,2560]{1,0:T(8,128)(2,1)S(1)} %collective-permute-done.refs_1_, bf16[240,2560]{1,0:T(8,128)(2,1)S(1)} %pad_maximum_fusion.1.refs_6_.refs_2_, ...), custom_call_target="tpu_custom_call" | custom-call | flops 566231040 | bytes 7249920 | tf_op jit(solution)/shard_map/pallas_call | solution.py:71
  157.5 3.5 %collective-permute-done.38 = bf16[16,5504]{1,0:T(8,128)(2,1)S(1)} collective-permute-done((bf16[16,5504]{1,0:T(8,128)(2,1)S(1)}, bf16[16,5504]{1,0:T(8,128)(2,1)S(1)}, u32[]{:S(2)}, u32[]{:S(2)}) %collective-permute-start.38) | collective-permute-done | bytes 176160 | tf_op jit(solution)/shard_map/ppermute | solution.py:59
  161.1 1.1 shard_map.105
  162.8 5.5 %collective-permute-done.40.refs_4_ = bf16[16,5504]{1,0:T(8,128)(2,1)S(1)} collective-permute-done((bf16[16,5504]{1,0:T(8,128)(2,1)S(1)}, bf16[16,5504]{1,0:T(8,128)(2,1)S(1)}, u32[]{:S(2)}, u32[]{:S(2)}) %collective-permute-start.40) | collective-permute-done | bytes 176160 | tf_op jit(solution)/shard_map/ppermute | solution.py:59
  168.3 1.3 shard_map.109
  (79 shorter events, 22.7 us)
Async XLA Ops:
  3.1 45.2 %collective-permute-start = (bf16[336,2560]{1,0:T(8,128)(2,1)S(1)}, bf16[336,2560]{1,0:T(8,128)(2,1)S(1)}, u32[]{:S(2)}, u32[]{:S(2)}) collective-permute-start(bf16[336,2560]{1,0:T(8,128)(2,1)S(1)} %pad_maximum_fusion.refs_5_.refs_0_), channel_id=1, source_target_pairs={{0,1},{1,0},{2,3},{3,2},{4,5},{5,4},{6,7},{7,6},{8,9},{9,8},{10,11... | collective-permute-start | bytes 5160968 | tf_op jit(solution)/shard_map/ppermute | solution.py:59
  7.2 2.9 %copy-start = (bf16[1,64,2560]{2,1,0:T(8,128)(2,1)S(1)}, bf16[1,64,2560]{2,1,0:T(8,128)(2,1)}, u32[]{:S(2)}) copy-start(bf16[1,64,2560]{2,1,0:T(8,128)(2,1)} %param.15) | copy-start | bytes 983044
  7.2 2.9 %copy-start.1 = (bf16[1,64,2560]{2,1,0:T(8,128)(2,1)S(1)}, bf16[1,64,2560]{2,1,0:T(8,128)(2,1)}, u32[]{:S(2)}) copy-start(bf16[1,64,2560]{2,1,0:T(8,128)(2,1)} %param.8) | copy-start | bytes 983044
  7.2 2.9 %copy-start.2 = (f32[1,2560]{1,0:T(1,128)S(1)}, f32[1,2560]{1,0:T(1,128)}, u32[]{:S(2)}) copy-start(f32[1,2560]{1,0:T(1,128)} %refs_3_.3) | copy-start | bytes 30724
  7.2 2.9 %copy-start.3 = (s32[1,2,64,1]{2,3,1,0:T(1,128)S(1)}, s32[1,2,64,1]{2,3,1,0:T(1,128)}, u32[]{:S(2)}) copy-start(s32[1,2,64,1]{2,3,1,0:T(1,128)} %param.13) | copy-start | bytes 1540
  7.2 2.8 %copy-start.4 = (f32[1,2,64,1]{2,3,1,0:T(1,128)S(1)}, f32[1,2,64,1]{2,3,1,0:T(1,128)}, u32[]{:S(2)}) copy-start(f32[1,2,64,1]{2,3,1,0:T(1,128)} %param.14) | copy-start | bytes 1540
  8.4 39.9 %collective-permute-start.1 = (bf16[240,2560]{1,0:T(8,128)(2,1)S(1)}, bf16[240,2560]{1,0:T(8,128)(2,1)S(1)}, u32[]{:S(2)}, u32[]{:S(2)}) collective-permute-start(bf16[240,2560]{1,0:T(8,128)(2,1)S(1)} %pad_maximum_fusion.1.refs_6_.refs_2_), channel_id=1, source_target_pairs={{0,2},{1,3},{2,0},{3,1},{4,6},{5,7},{6,4},{7,5},{8,10},{9,11},{10,... | collective-permute-start | bytes 3686408 | tf_op jit(solution)/shard_map/ppermute | solution.py:59
  10.9 37.4 %collective-permute-start.2 = (bf16[32,5504]{1,0:T(8,128)(2,1)S(1)}, bf16[32,5504]{1,0:T(8,128)(2,1)S(1)}, u32[]{:S(2)}, u32[]{:S(2)}) collective-permute-start(bf16[32,5504]{1,0:T(8,128)(2,1)S(1)} %get-tuple-element.97), channel_id=1, source_target_pairs={{0,4},{1,5},{2,6},{3,7},{4,0},{5,1},{6,2},{7,3},{8,12},{9,13},{10,... | collective-permute-start | bytes 1056776 | tf_op jit(solution)/shard_map/ppermute | solution.py:59
  13.6 33.9 %collective-permute-start.4 = (bf16[16,5504]{1,0:T(8,128)(2,1)S(1)}, bf16[16,5504]{1,0:T(8,128)(2,1)S(1)}, u32[]{:S(2)}, u32[]{:S(2)}) collective-permute-start(bf16[16,5504]{1,0:T(8,128)(2,1)S(1)} %get-tuple-element.118.refs_5_), channel_id=1, source_target_pairs={{0,1},{1,0},{2,3},{3,2},{4,5},{5,4},{6,7},{7,6},{8,9},{9,8},{10,11... | collective-permute-start | bytes 528392 | tf_op jit(solution)/shard_map/ppermute | solution.py:59
  14.1 34.2 %collective-permute-start.3 = (bf16[16,5504]{1,0:T(8,128)(2,1)S(1)}, bf16[16,5504]{1,0:T(8,128)(2,1)S(1)}, u32[]{:S(2)}, u32[]{:S(2)}) collective-permute-start(bf16[16,5504]{1,0:T(8,128)(2,1)S(1)} %get-tuple-element.118.refs_5_), channel_id=1, source_target_pairs={{0,2},{1,3},{2,0},{3,1},{4,6},{5,7},{6,4},{7,5},{8,10},{9,11},{10,... | collective-permute-start | bytes 528392 | tf_op jit(solution)/shard_map/ppermute | solution.py:59
  48.3 5.5 %collective-permute-start.6 = (bf16[16,5504]{1,0:T(8,128)(2,1)S(1)}, bf16[16,5504]{1,0:T(8,128)(2,1)S(1)}, u32[]{:S(2)}, u32[]{:S(2)}) collective-permute-start(bf16[16,5504]{1,0:T(8,128)(2,1)S(1)} %get-tuple-element.106.refs_5_), channel_id=1, source_target_pairs={{0,1},{1,0},{2,3},{3,2},{4,5},{5,4},{6,7},{7,6},{8,9},{9,8},{10,11... | collective-permute-start | bytes 528392 | tf_op jit(solution)/shard_map/ppermute | solution.py:59
  49.3 5.5 %collective-permute-start.5 = (bf16[16,5504]{1,0:T(8,128)(2,1)S(1)}, bf16[16,5504]{1,0:T(8,128)(2,1)S(1)}, u32[]{:S(2)}, u32[]{:S(2)}) collective-permute-start(bf16[16,5504]{1,0:T(8,128)(2,1)S(1)} %get-tuple-element.106.refs_5_), channel_id=1, source_target_pairs={{0,2},{1,3},{2,0},{3,1},{4,6},{5,7},{6,4},{7,5},{8,10},{9,11},{10,... | collective-permute-start | bytes 528392 | tf_op jit(solution)/shard_map/ppermute | solution.py:59
  57.2 7.3 %collective-permute-start.8 = (bf16[16,5504]{1,0:T(8,128)(2,1)S(1)}, bf16[16,5504]{1,0:T(8,128)(2,1)S(1)}, u32[]{:S(2)}, u32[]{:S(2)}) collective-permute-start(bf16[16,5504]{1,0:T(8,128)(2,1)S(1)} %get-tuple-element.115.refs_7_), channel_id=1, source_target_pairs={{0,2},{1,3},{2,0},{3,1},{4,6},{5,7},{6,4},{7,5},{8,10},{9,11},{10,... | collective-permute-start | bytes 528392 | tf_op jit(solution)/shard_map/ppermute | solution.py:59
  58.9 7.4 %collective-permute-start.9 = (bf16[16,5504]{1,0:T(8,128)(2,1)S(1)}, bf16[16,5504]{1,0:T(8,128)(2,1)S(1)}, u32[]{:S(2)}, u32[]{:S(2)}) collective-permute-start(bf16[16,5504]{1,0:T(8,128)(2,1)S(1)} %get-tuple-element.116), channel_id=1, source_target_pairs={{0,1},{1,0},{2,3},{3,2},{4,5},{5,4},{6,7},{7,6},{8,9},{9,8},{10,11... | collective-permute-start | bytes 528392 | tf_op jit(solution)/shard_map/ppermute | solution.py:59
  60.0 10.3 %collective-permute-start.12 = (bf16[32,5504]{1,0:T(8,128)(2,1)S(1)}, bf16[32,5504]{1,0:T(8,128)(2,1)S(1)}, u32[]{:S(2)}, u32[]{:S(2)}) collective-permute-start(bf16[32,5504]{1,0:T(8,128)(2,1)S(1)} %pad_maximum_fusion.2.refs_5_), channel_id=1, source_target_pairs={{0,1},{1,0},{2,3},{3,2},{4,5},{5,4},{6,7},{7,6},{8,9},{9,8},{10,11... | collective-permute-start | bytes 1056776 | tf_op jit(solution)/shard_map/ppermute | solution.py:59
  60.9 9.4 %collective-permute-start.11 = (bf16[32,5504]{1,0:T(8,128)(2,1)S(1)}, bf16[32,5504]{1,0:T(8,128)(2,1)S(1)}, u32[]{:S(2)}, u32[]{:S(2)}) collective-permute-start(bf16[32,5504]{1,0:T(8,128)(2,1)S(1)} %pad_maximum_fusion.2.refs_5_), channel_id=1, source_target_pairs={{0,2},{1,3},{2,0},{3,1},{4,6},{5,7},{6,4},{7,5},{8,10},{9,11},{10,... | collective-permute-start | bytes 1056776 | tf_op jit(solution)/shard_map/ppermute | solution.py:59
  61.3 17.3 %collective-permute-start.7 = (bf16[80,2560]{1,0:T(8,128)(2,1)S(1)}, bf16[80,2560]{1,0:T(8,128)(2,1)S(1)}, u32[]{:S(2)}, u32[]{:S(2)}) collective-permute-start(bf16[80,2560]{1,0:T(8,128)(2,1)S(1)} %get-tuple-element.112), channel_id=1, source_target_pairs={{0,8},{1,9},{2,10},{3,11},{4,12},{5,13},{6,14},{7,15},{8,16},{9,17... | collective-permute-start | bytes 1228808 | tf_op jit(solution)/shard_map/ppermute | solution.py:59
  66.3 12.3 %collective-permute-start.10 = (bf16[16,5504]{1,0:T(8,128)(2,1)S(1)}, bf16[16,5504]{1,0:T(8,128)(2,1)S(1)}, u32[]{:S(2)}, u32[]{:S(2)}) collective-permute-start(bf16[16,5504]{1,0:T(8,128)(2,1)S(1)} %add_convert_fusion.3), channel_id=1, source_target_pairs={{0,12},{1,13},{2,14},{3,15},{4,8},{5,9},{6,10},{7,11},{8,20},{9,21... | collective-permute-start | bytes 528392 | tf_op jit(solution)/shard_map/ppermute | solution.py:59
  70.3 9.5 %collective-permute-start.13 = (bf16[16,5504]{1,0:T(8,128)(2,1)S(1)}, bf16[16,5504]{1,0:T(8,128)(2,1)S(1)}, u32[]{:S(2)}, u32[]{:S(2)}) collective-permute-start(bf16[16,5504]{1,0:T(8,128)(2,1)S(1)} %get-tuple-element.124), channel_id=1, source_target_pairs={{0,10},{1,11},{2,8},{3,9},{4,14},{5,15},{6,12},{7,13},{8,18},{9,19... | collective-permute-start | bytes 528392 | tf_op jit(solution)/shard_map/ppermute | solution.py:59
  70.3 9.5 %collective-permute-start.14 = (bf16[16,5504]{1,0:T(8,128)(2,1)S(1)}, bf16[16,5504]{1,0:T(8,128)(2,1)S(1)}, u32[]{:S(2)}, u32[]{:S(2)}) collective-permute-start(bf16[16,5504]{1,0:T(8,128)(2,1)S(1)} %get-tuple-element.125), channel_id=1, source_target_pairs={{0,9},{1,8},{2,11},{3,10},{4,13},{5,12},{6,15},{7,14},{8,17},{9,16... | collective-permute-start | bytes 528392 | tf_op jit(solution)/shard_map/ppermute | solution.py:59
  72.3 8.7 %collective-permute-start.15 = (bf16[16,5504]{1,0:T(8,128)(2,1)S(1)}, bf16[16,5504]{1,0:T(8,128)(2,1)S(1)}, u32[]{:S(2)}, u32[]{:S(2)}) collective-permute-start(bf16[16,5504]{1,0:T(8,128)(2,1)S(1)} %get-tuple-element.126), channel_id=1, source_target_pairs={{0,8},{1,9},{2,10},{3,11},{4,12},{5,13},{6,14},{7,15},{8,16},{9,17... | collective-permute-start | bytes 528392 | tf_op jit(solution)/shard_map/ppermute | solution.py:59
  81.9 12.5 %collective-permute-start.19 = (bf16[144,2560]{1,0:T(8,128)(2,1)S(1)}, bf16[144,2560]{1,0:T(8,128)(2,1)S(1)}, u32[]{:S(2)}, u32[]{:S(2)}) collective-permute-start(bf16[144,2560]{1,0:T(8,128)(2,1)S(1)} %get-tuple-element.137), channel_id=1, source_target_pairs={{0,24},{1,25},{2,26},{3,27},{4,28},{5,29},{6,30},{7,31},{8,0},{9,1... | collective-permute-start | bytes 2211848 | tf_op jit(solution)/shard_map/ppermute | solution.py:59
  81.9 11.7 %collective-permute-start.16 = (bf16[16,5504]{1,0:T(8,128)(2,1)S(1)}, bf16[16,5504]{1,0:T(8,128)(2,1)S(1)}, u32[]{:S(2)}, u32[]{:S(2)}) collective-permute-start(bf16[16,5504]{1,0:T(8,128)(2,1)S(1)} %get-tuple-element.135), channel_id=1, source_target_pairs={{0,4},{1,5},{2,6},{3,7},{4,0},{5,1},{6,2},{7,3},{8,12},{9,13},{10,... | collective-permute-start | bytes 528392 | tf_op jit(solution)/shard_map/ppermute | solution.py:59
  83.8 9.7 %collective-permute-start.18 = (bf16[16,5504]{1,0:T(8,128)(2,1)S(1)}, bf16[16,5504]{1,0:T(8,128)(2,1)S(1)}, u32[]{:S(2)}, u32[]{:S(2)}) collective-permute-start(bf16[16,5504]{1,0:T(8,128)(2,1)S(1)} %get-tuple-element.136.refs_9_), channel_id=1, source_target_pairs={{0,1},{1,0},{2,3},{3,2},{4,5},{5,4},{6,7},{7,6},{8,9},{9,8},{10,11... | collective-permute-start | bytes 528392 | tf_op jit(solution)/shard_map/ppermute | solution.py:59
  84.4 10.0 %collective-permute-start.17 = (bf16[16,5504]{1,0:T(8,128)(2,1)S(1)}, bf16[16,5504]{1,0:T(8,128)(2,1)S(1)}, u32[]{:S(2)}, u32[]{:S(2)}) collective-permute-start(bf16[16,5504]{1,0:T(8,128)(2,1)S(1)} %get-tuple-element.136.refs_9_), channel_id=1, source_target_pairs={{0,2},{1,3},{2,0},{3,1},{4,6},{5,7},{6,4},{7,5},{8,10},{9,11},{10,... | collective-permute-start | bytes 528392 | tf_op jit(solution)/shard_map/ppermute | solution.py:59
  94.3 5.5 %collective-permute-start.21 = (bf16[16,5504]{1,0:T(8,128)(2,1)S(1)}, bf16[16,5504]{1,0:T(8,128)(2,1)S(1)}, u32[]{:S(2)}, u32[]{:S(2)}) collective-permute-start(bf16[16,5504]{1,0:T(8,128)(2,1)S(1)} %collective-permute-done.16.refs_9_), channel_id=1, source_target_pairs={{0,1},{1,0},{2,3},{3,2},{4,5},{5,4},{6,7},{7,6},{8,9},{9,8},{10,11... | collective-permute-start | bytes 528392 | tf_op jit(solution)/shard_map/ppermute | solution.py:59
  95.3 5.5 %collective-permute-start.20 = (bf16[16,5504]{1,0:T(8,128)(2,1)S(1)}, bf16[16,5504]{1,0:T(8,128)(2,1)S(1)}, u32[]{:S(2)}, u32[]{:S(2)}) collective-permute-start(bf16[16,5504]{1,0:T(8,128)(2,1)S(1)} %collective-permute-done.16.refs_9_), channel_id=1, source_target_pairs={{0,2},{1,3},{2,0},{3,1},{4,6},{5,7},{6,4},{7,5},{8,10},{9,11},{10,... | collective-permute-start | bytes 528392 | tf_op jit(solution)/shard_map/ppermute | solution.py:59
  103.4 7.2 %collective-permute-start.22 = (bf16[16,5504]{1,0:T(8,128)(2,1)S(1)}, bf16[16,5504]{1,0:T(8,128)(2,1)S(1)}, u32[]{:S(2)}, u32[]{:S(2)}) collective-permute-start(bf16[16,5504]{1,0:T(8,128)(2,1)S(1)} %get-tuple-element.147), channel_id=1, source_target_pairs={{0,2},{1,3},{2,0},{3,1},{4,6},{5,7},{6,4},{7,5},{8,10},{9,11},{10,... | collective-permute-start | bytes 528392 | tf_op jit(solution)/shard_map/ppermute | solution.py:59
  104.5 6.7 %collective-permute-start.23 = (bf16[16,5504]{1,0:T(8,128)(2,1)S(1)}, bf16[16,5504]{1,0:T(8,128)(2,1)S(1)}, u32[]{:S(2)}, u32[]{:S(2)}) collective-permute-start(bf16[16,5504]{1,0:T(8,128)(2,1)S(1)} %get-tuple-element.148), channel_id=1, source_target_pairs={{0,1},{1,0},{2,3},{3,2},{4,5},{5,4},{6,7},{7,6},{8,9},{9,8},{10,11... | collective-permute-start | bytes 528392 | tf_op jit(solution)/shard_map/ppermute | solution.py:59
  106.4 9.5 %collective-permute-start.25 = (bf16[16,5504]{1,0:T(8,128)(2,1)S(1)}, bf16[16,5504]{1,0:T(8,128)(2,1)S(1)}, u32[]{:S(2)}, u32[]{:S(2)}) collective-permute-start(bf16[16,5504]{1,0:T(8,128)(2,1)S(1)} %get-tuple-element.154), channel_id=1, source_target_pairs={{0,2},{1,3},{2,0},{3,1},{4,6},{5,7},{6,4},{7,5},{8,10},{9,11},{10,... | collective-permute-start | bytes 528392 | tf_op jit(solution)/shard_map/ppermute | solution.py:59
  107.4 8.8 %collective-permute-start.26 = (bf16[16,5504]{1,0:T(8,128)(2,1)S(1)}, bf16[16,5504]{1,0:T(8,128)(2,1)S(1)}, u32[]{:S(2)}, u32[]{:S(2)}) collective-permute-start(bf16[16,5504]{1,0:T(8,128)(2,1)S(1)} %get-tuple-element.155), channel_id=1, source_target_pairs={{0,1},{1,0},{2,3},{3,2},{4,5},{5,4},{6,7},{7,6},{8,9},{9,8},{10,11... | collective-permute-start | bytes 528392 | tf_op jit(solution)/shard_map/ppermute | solution.py:59
  111.3 11.3 %collective-permute-start.24 = (bf16[16,5504]{1,0:T(8,128)(2,1)S(1)}, bf16[16,5504]{1,0:T(8,128)(2,1)S(1)}, u32[]{:S(2)}, u32[]{:S(2)}) collective-permute-start(bf16[16,5504]{1,0:T(8,128)(2,1)S(1)} %add_convert_fusion.2), channel_id=1, source_target_pairs={{0,28},{1,29},{2,30},{3,31},{4,24},{5,25},{6,26},{7,27},{8,4},{9,5... | collective-permute-start | bytes 528392 | tf_op jit(solution)/shard_map/ppermute | solution.py:59
  111.4 11.2 %collective-permute-start.30 = (bf16[16,5504]{1,0:T(8,128)(2,1)S(1)}, bf16[16,5504]{1,0:T(8,128)(2,1)S(1)}, u32[]{:S(2)}, u32[]{:S(2)}) collective-permute-start(bf16[16,5504]{1,0:T(8,128)(2,1)S(1)} %get-tuple-element.169.refs_11_), channel_id=1, source_target_pairs={{0,26},{1,27},{2,24},{3,25},{4,30},{5,31},{6,28},{7,29},{8,2},{9,3... | collective-permute-start | bytes 528392 | tf_op jit(solution)/shard_map/ppermute | solution.py:59
  115.9 6.7 %collective-permute-start.31 = (bf16[16,5504]{1,0:T(8,128)(2,1)S(1)}, bf16[16,5504]{1,0:T(8,128)(2,1)S(1)}, u32[]{:S(2)}, u32[]{:S(2)}) collective-permute-start(bf16[16,5504]{1,0:T(8,128)(2,1)S(1)} %get-tuple-element.170), channel_id=1, source_target_pairs={{0,25},{1,24},{2,27},{3,26},{4,29},{5,28},{6,31},{7,30},{8,1},{9,0... | collective-permute-start | bytes 528392 | tf_op jit(solution)/shard_map/ppermute | solution.py:59
  115.9 9.0 %collective-permute-start.32 = (bf16[16,5504]{1,0:T(8,128)(2,1)S(1)}, bf16[16,5504]{1,0:T(8,128)(2,1)S(1)}, u32[]{:S(2)}, u32[]{:S(2)}) collective-permute-start(bf16[16,5504]{1,0:T(8,128)(2,1)S(1)} %get-tuple-element.171), channel_id=1, source_target_pairs={{0,24},{1,25},{2,26},{3,27},{4,28},{5,29},{6,30},{7,31},{8,0},{9,1... | collective-permute-start | bytes 528392 | tf_op jit(solution)/shard_map/ppermute | solution.py:59
  125.8 10.8 %collective-permute-start.33 = (bf16[16,5504]{1,0:T(8,128)(2,1)S(1)}, bf16[16,5504]{1,0:T(8,128)(2,1)S(1)}, u32[]{:S(2)}, u32[]{:S(2)}) collective-permute-start(bf16[16,5504]{1,0:T(8,128)(2,1)S(1)} %get-tuple-element.177), channel_id=1, source_target_pairs={{0,4},{1,5},{2,6},{3,7},{4,0},{5,1},{6,2},{7,3},{8,12},{9,13},{10,... | collective-permute-start | bytes 528392 | tf_op jit(solution)/shard_map/ppermute | solution.py:59
  125.9 10.8 %collective-permute-start.35 = (bf16[16,5504]{1,0:T(8,128)(2,1)S(1)}, bf16[16,5504]{1,0:T(8,128)(2,1)S(1)}, u32[]{:S(2)}, u32[]{:S(2)}) collective-permute-start(bf16[16,5504]{1,0:T(8,128)(2,1)S(1)} %get-tuple-element.178.refs_9_), channel_id=1, source_target_pairs={{0,1},{1,0},{2,3},{3,2},{4,5},{5,4},{6,7},{7,6},{8,9},{9,8},{10,11... | collective-permute-start | bytes 528392 | tf_op jit(solution)/shard_map/ppermute | solution.py:59
  127.0 10.8 %collective-permute-start.34 = (bf16[16,5504]{1,0:T(8,128)(2,1)S(1)}, bf16[16,5504]{1,0:T(8,128)(2,1)S(1)}, u32[]{:S(2)}, u32[]{:S(2)}) collective-permute-start(bf16[16,5504]{1,0:T(8,128)(2,1)S(1)} %get-tuple-element.178.refs_9_), channel_id=1, source_target_pairs={{0,2},{1,3},{2,0},{3,1},{4,6},{5,7},{6,4},{7,5},{8,10},{9,11},{10,... | collective-permute-start | bytes 528392 | tf_op jit(solution)/shard_map/ppermute | solution.py:59
  137.7 6.8 %collective-permute-start.37 = (bf16[16,5504]{1,0:T(8,128)(2,1)S(1)}, bf16[16,5504]{1,0:T(8,128)(2,1)S(1)}, u32[]{:S(2)}, u32[]{:S(2)}) collective-permute-start(bf16[16,5504]{1,0:T(8,128)(2,1)S(1)} %collective-permute-done.33.refs_9_), channel_id=1, source_target_pairs={{0,1},{1,0},{2,3},{3,2},{4,5},{5,4},{6,7},{7,6},{8,9},{9,8},{10,11... | collective-permute-start | bytes 528392 | tf_op jit(solution)/shard_map/ppermute | solution.py:59
  138.7 10.6 %collective-permute-start.36 = (bf16[16,5504]{1,0:T(8,128)(2,1)S(1)}, bf16[16,5504]{1,0:T(8,128)(2,1)S(1)}, u32[]{:S(2)}, u32[]{:S(2)}) collective-permute-start(bf16[16,5504]{1,0:T(8,128)(2,1)S(1)} %collective-permute-done.33.refs_9_), channel_id=1, source_target_pairs={{0,2},{1,3},{2,0},{3,1},{4,6},{5,7},{6,4},{7,5},{8,10},{9,11},{10,... | collective-permute-start | bytes 528392 | tf_op jit(solution)/shard_map/ppermute | solution.py:59
  139.6 14.1 %collective-permute-start.28 = (bf16[16,5504]{1,0:T(8,128)(2,1)S(1)}, bf16[16,5504]{1,0:T(8,128)(2,1)S(1)}, u32[]{:S(2)}, u32[]{:S(2)}) collective-permute-start(bf16[16,5504]{1,0:T(8,128)(2,1)S(1)} %get-tuple-element.161), channel_id=1, source_target_pairs={{0,2},{1,3},{2,0},{3,1},{4,6},{5,7},{6,4},{7,5},{8,10},{9,11},{10,... | collective-permute-start | bytes 528392 | tf_op jit(solution)/shard_map/ppermute | solution.py:59
  141.7 12.0 %collective-permute-start.29 = (bf16[16,5504]{1,0:T(8,128)(2,1)S(1)}, bf16[16,5504]{1,0:T(8,128)(2,1)S(1)}, u32[]{:S(2)}, u32[]{:S(2)}) collective-permute-start(bf16[16,5504]{1,0:T(8,128)(2,1)S(1)} %get-tuple-element.162), channel_id=1, source_target_pairs={{0,1},{1,0},{2,3},{3,2},{4,5},{5,4},{6,7},{7,6},{8,9},{9,8},{10,11... | collective-permute-start | bytes 528392 | tf_op jit(solution)/shard_map/ppermute | solution.py:59
  142.7 11.0 %collective-permute-start.27 = (bf16[16,5504]{1,0:T(8,128)(2,1)S(1)}, bf16[16,5504]{1,0:T(8,128)(2,1)S(1)}, u32[]{:S(2)}, u32[]{:S(2)}) collective-permute-start(bf16[16,5504]{1,0:T(8,128)(2,1)S(1)} %add_convert_fusion.1), channel_id=1, source_target_pairs={{0,4},{1,5},{2,6},{3,7},{4,0},{5,1},{6,2},{7,3},{8,12},{9,13},{10,... | collective-permute-start | bytes 528392 | tf_op jit(solution)/shard_map/ppermute | solution.py:59
  151.3 6.2 %collective-permute-start.39 = (bf16[16,5504]{1,0:T(8,128)(2,1)S(1)}, bf16[16,5504]{1,0:T(8,128)(2,1)S(1)}, u32[]{:S(2)}, u32[]{:S(2)}) collective-permute-start(bf16[16,5504]{1,0:T(8,128)(2,1)S(1)} %get-tuple-element.182), channel_id=1, source_target_pairs={{0,1},{1,0},{2,3},{3,2},{4,5},{5,4},{6,7},{7,6},{8,9},{9,8},{10,11... | collective-permute-start | bytes 528392 | tf_op jit(solution)/shard_map/ppermute | solution.py:59
  152.1 8.9 %collective-permute-start.38 = (bf16[16,5504]{1,0:T(8,128)(2,1)S(1)}, bf16[16,5504]{1,0:T(8,128)(2,1)S(1)}, u32[]{:S(2)}, u32[]{:S(2)}) collective-permute-start(bf16[16,5504]{1,0:T(8,128)(2,1)S(1)} %get-tuple-element.181.refs_11_), channel_id=1, source_target_pairs={{0,2},{1,3},{2,0},{3,1},{4,6},{5,7},{6,4},{7,5},{8,10},{9,11},{10,... | collective-permute-start | bytes 528392 | tf_op jit(solution)/shard_map/ppermute | solution.py:59
  155.7 7.1 %collective-permute-start.41 = (bf16[16,5504]{1,0:T(8,128)(2,1)S(1)}, bf16[16,5504]{1,0:T(8,128)(2,1)S(1)}, u32[]{:S(2)}, u32[]{:S(2)}) collective-permute-start(bf16[16,5504]{1,0:T(8,128)(2,1)S(1)} %get-tuple-element.189), channel_id=1, source_target_pairs={{0,2},{1,3},{2,0},{3,1},{4,6},{5,7},{6,4},{7,5},{8,10},{9,11},{10,... | collective-permute-start | bytes 528392 | tf_op jit(solution)/shard_map/ppermute | solution.py:59
  156.5 6.4 %collective-permute-start.42 = (bf16[16,5504]{1,0:T(8,128)(2,1)S(1)}, bf16[16,5504]{1,0:T(8,128)(2,1)S(1)}, u32[]{:S(2)}, u32[]{:S(2)}) collective-permute-start(bf16[16,5504]{1,0:T(8,128)(2,1)S(1)} %get-tuple-element.190), channel_id=1, source_target_pairs={{0,1},{1,0},{2,3},{3,2},{4,5},{5,4},{6,7},{7,6},{8,9},{9,8},{10,11... | collective-permute-start | bytes 528392 | tf_op jit(solution)/shard_map/ppermute | solution.py:59
  161.0 7.3 %collective-permute-start.40 = (bf16[16,5504]{1,0:T(8,128)(2,1)S(1)}, bf16[16,5504]{1,0:T(8,128)(2,1)S(1)}, u32[]{:S(2)}, u32[]{:S(2)}) collective-permute-start(bf16[16,5504]{1,0:T(8,128)(2,1)S(1)} %add_convert_fusion), channel_id=1, source_target_pairs={{0,4},{1,5},{2,6},{3,7},{4,0},{5,1},{6,2},{7,3},{8,12},{9,13},{10,... | collective-permute-start | bytes 528392 | tf_op jit(solution)/shard_map/ppermute | solution.py:59
  (1 other events, 2.3 us)

commit v2 on v1

--- a/solution.py
+++ b/solution.py
@@ -179,59 +179,67 @@
     return count * box.groups * ROWS, extra
 
 
-def unpack(box, refs, stack, tails, at=0):
-    count = 0
-    for ref in refs:
-        for p in range(ref.shape[0] // ROWS):
+def unpack(box, refs, stack, tails):
+    count = refs[0].shape[0] // ROWS
+    tall = stack.shape[0] // len(refs)
+    whole, extra = heights(box, count)
+    for which, ref in enumerate(refs):
+        for p in range(count):
             for g in range(box.groups):
+                at = which * tall + (p * box.groups + g) * ROWS
                 stack[at : at + ROWS, :] = ref[p * ROWS : (p + 1) * ROWS, box.group(g)]
-                at += ROWS
-            if box.extra:
-                tails[count * ROWS : (count + 1) * ROWS, :] = ref[
-                    p * ROWS : (p + 1) * ROWS, box.tail()
-                ]
-            count += 1
+        if box.extra:
+            tails[which * count * ROWS : (which + 1) * count * ROWS, :] = ref[:, box.tail()]
     if box.extra:
-        extra = heights(box, count)[1]
-        r = iota((extra, count * ROWS), 0)
-        c = iota((extra, count * ROWS), 1)
-        mine = (r // box.extra == c // ROWS) & (r % box.extra == c % ROWS // box.cuts)
+        r = iota((len(refs) * extra, tails.shape[0]), 0)
+        c = iota((len(refs) * extra, tails.shape[0]), 1)
+        mine, cut = place_of(box, count, r, c)
         for i in range(box.pieces):
             start, size = box.piece(i)
-            sel = jnp.where(mine & (c % ROWS % box.cuts == i), 1.0, 0.0).astype(BF)
-            stack[at : at + extra, start : start + size] = dot(sel, tails[:, :size]).astype(BF)
-
-
-def repack(box, rows, refs):
-    rows = rows.astype(BF)
-    at = 0
-    count = 0
-    for ref in refs:
-        for p in range(ref.shape[0] // ROWS):
+            sel = jnp.where(mine & (cut == i), 1.0, 0.0).astype(BF)
+            got = dot(sel, tails[:, :size]).astype(BF)
+            for which in range(len(refs)):
+                at = which * tall + whole
+                stack[at : at + extra, start : start + size] = got[
+                    which * extra : (which + 1) * extra
+                ]
+
+
+def place_of(box, count, row, tail):
+    extra = heights(box, count)[1]
+    inside, within = row % extra, tail % (count * ROWS)
+    mine = row // extra == tail // (count * ROWS)
+    mine &= (inside // box.extra == within // ROWS) & (inside < count * box.extra)
+    mine &= inside % box.extra == within % ROWS // box.cuts
+    return mine, within % ROWS % box.cuts
+
+
+def repack(box, values, refs):
+    count = refs[0].shape[0] // ROWS
+    whole, extra = heights(box, count)
+    values = [value.astype(BF) for value in values]
+    for value, ref in zip(values, refs):
+        for p in range(count):
             for g in range(box.groups):
-                ref[p * ROWS : (p + 1) * ROWS, box.group(g)] = rows[at : at + ROWS]
-                at += ROWS
-            count += 1
+                at = (p * box.groups + g) * ROWS
+                ref[p * ROWS : (p + 1) * ROWS, box.group(g)] = value[at : at + ROWS]
     if box.extra:
-        extra = heights(box, count)[1]
-        r = iota((count * ROWS, extra), 0)
-        c = iota((count * ROWS, extra), 1)
-        mine = (c // box.extra == r // ROWS) & (c % box.extra == r % ROWS // box.cuts)
-        total = jnp.zeros((count * ROWS, box.wide), F32)
+        lot = len(refs) * count * ROWS
+        rest = jnp.concatenate([value[whole:] for value in values], axis=0)
+        r = iota((lot, len(refs) * extra), 0)
+        c = iota((lot, len(refs) * extra), 1)
+        mine, cut = place_of(box, count, c, r)
+        total = jnp.zeros((lot, box.wide), F32)
         for i in range(box.pieces):
             start, size = box.piece(i)
-            sel = jnp.where(mine & (r % ROWS % box.cuts == i), 1.0, 0.0).astype(BF)
-            got = dot(sel, rows[at:, start : start + size])
+            sel = jnp.where(mine & (cut == i), 1.0, 0.0).astype(BF)
+            got = dot(sel, rest[:, start : start + size])
             if size < box.wide:
-                pad = jnp.zeros((count * ROWS, box.wide - size), F32)
-                got = jnp.concatenate([got, pad], axis=1)
+                got = jnp.concatenate([got, jnp.zeros((lot, box.wide - size), F32)], axis=1)
             total = total + got
         total = total.astype(BF)
-        count = 0
-        for ref in refs:
-            tall = ref.shape[0]
-            ref[:, box.tail()] = total[count : count + tall]
-            count += tall
+        for which, ref in enumerate(refs):
+            ref[:, box.tail()] = total[which * count * ROWS : (which + 1) * count * ROWS]
 
 
 def inv_rms(wide):
@@ -240,6 +248,31 @@
 
 def total_of(refs):
     return sum(ref[...].astype(F32) for ref in refs).astype(BF)
+
+
+def gather_kernel(rows, *refs):
+    arrays, (out, sems) = refs[:-2], refs[-2:]
+    copies = [
+        pltpu.make_async_copy(
+            ref.at[pl.ds(*rows)], out.at[pl.ds(at * rows[1], rows[1])], sems.at[at]
+        )
+        for at, ref in enumerate(arrays)
+    ]
+    for copy in copies:
+        copy.start()
+    for copy in copies:
+        copy.wait()
+
+
+def gather(rows, *arrays):
+    shape = (len(arrays) * rows[1], arrays[0].shape[1])
+    return pl.pallas_call(
+        functools.partial(gather_kernel, rows),
+        out_shape=jax.ShapeDtypeStruct(shape, arrays[0].dtype),
+        in_specs=[pl.BlockSpec(memory_space=pl.ANY)] * len(arrays),
+        out_specs=pl.BlockSpec(memory_space=pltpu.VMEM),
+        scratch_shapes=[pltpu.SemaphoreType.DMA((len(arrays),))],
+    )(*arrays)
 
 
 def start_kernel(box, experts, tokens, cot, gain, ids, mix, ahead, notes0, notes1, *boxes):
@@ -356,15 +389,13 @@
 
 def read_rows(box, rows, stack, tails):
     tall = stack.shape[0] // 3
-    for at, ref in enumerate(rows):
-        unpack(box, [ref], stack, tails, at * tall)
+    unpack(box, rows, stack, tails)
     return [stack[span, :] for span in spans(tall)]
 
 
 def write_rows(box, top, bottom, outs):
     tall = top.shape[0] // 2
-    for ref, value in zip(outs, (top[:tall], top[tall:] + bottom[:tall], bottom[tall:])):
-        repack(box, value, [ref])
+    repack(box, (top[:tall], top[tall:] + bottom[:tall], bottom[tall:]), outs)
 
 
 def forward_kernel(box, packs, saved, rows, outs, kept, stack, tails):
@@ -444,7 +475,7 @@
 
     scratch = [
         pltpu.VMEM((3 * tall, width), BF),
-        pltpu.VMEM((count * ROWS, max(box.wide, LANES)), BF),
+        pltpu.VMEM((3 * count * ROWS, max(box.wide, LANES)), BF),
     ]
     flops = sum(2 * 2 * tall * pack.size for pack in packs)
     results = call(body, results, *inputs, scratch=scratch, flops=flops, after=after)
@@ -500,8 +531,8 @@
 
     units = w_gate.shape[3]
     cut = -(-units * 7 // 12 // ROWS) * ROWS
-    top = jnp.concatenate([gate_w[:cut], up_w[:cut], down_w[:cut]], axis=0)
-    bottom = jnp.concatenate([gate_w[cut:], up_w[cut:], down_w[cut:]], axis=0)
+    top = gather((0, cut), gate_w, up_w, down_w)
+    bottom = gather((cut, units - cut), gate_w, up_w, down_w)
     packs = [top, shift(top, flip=1), bottom, shift(bottom, flip=2)]
 
     def rows_of(count):
@@ -570,12 +601,12 @@
         scratch=[picked],
     )
 
-    cross_g, own_z, own_x = fence(
-        (crossing_of(boxes_g), shift(own_g, flip=2), shift(own_g, flip=1))
+    cross_g, own_z, own_x, fin_own = fence(
+        (crossing_of(boxes_g), shift(own_g, flip=2), shift(own_g, flip=1), own_home(own_fin, 0))
     )
     cross_g, own_g = around(cross_g), [own_z, own_g, own_x]
     back = bind(expert_call, back_kernel, box, packs)
-    fin = fin_back + own_home(own_fin, 0)
+    fin = fin_back + fin_own
     cross_grad = back(cross_g, cross_kept0)[0]
     own_grad = back(own_g, own_kept0, after=cross_grad[:1] + tuple(fin))[0]
     got = home(sums(cross_grad), 0) + own_home(own_grad, 0)

time: 170 us -> 173 us (1.018)
  waiting for transfers between devices: 97.7 us -> 90.8 us
  starting transfers between devices: 43 us -> 49.9 us
  Pallas kernels: 23 us -> 27.8 us
    ppermute x43, waiting for transfers between devices: 97.7 us -> 90.8 us  [shift(): return lax.ppermute(value, ('section', 'expert'), pairs)]
    ppermute x43, starting transfers between devices: 43 us -> 49.9 us  [shift(): return lax.ppermute(value, ('section', 'expert'), pairs)]
    pallas_call x0 -> x2, Pallas kernels: none -> 4.97 us  [gather(): pl.pallas_call(functools.partial(gather_kernel, rows), out_shape=jax.Shap...]
    slice x6 -> x0, local copies, waits for them, and re-layouts: 4.47 us -> none  [the longest x3 2.32 us: local(): top = jnp.concatenate([gate_w[:cut], up_w[:cut], down_w[:cut]], axis=0)]
    unnamed x12 -> x20, local copies, waits for them, and re-layouts: 0.04 us -> 3.28 us
  transfers between devices with their start and end apart: 43 -> 43, of which waited for: 25 -> 25; matrix products, arithmetic and copies ran while one was open for 2% -> 0% of each run, Pallas kernels for 9% -> 10%
where the time goes in v2:
time: 173 us
  waiting for transfers between devices  90.8 us (52%)
  starting transfers between devices  49.9 us (29%)
  Pallas kernels  27.8 us (16%)
  local copies, waits for them, and re-layouts  3.31 us (2%)
    ppermute x43, waiting for transfers between devices, shift(): return lax.ppermute(value, ('section', 'expert'), pairs)  90.8 us
    ppermute x43, starting transfers between devices, shift(): return lax.ppermute(value, ('section', 'expert'), pairs)  49.9 us
    pallas_call x15, Pallas kernels, call(): pl.pallas_call(reading, out_shape=list(outs), in_specs=[vmem] * read + [p...  22.8 us
    pallas_call x2, Pallas kernels, gather(): pl.pallas_call(functools.partial(gather_kernel, rows), out_shape=jax.Shap...  4.97 us
  transfers between devices with their start and end apart: 43, of which 25 were waited for; matrix products, arithmetic and copies ran while one was open for 0% of the time, Pallas kernels for 10%

profile of v2, /device:TPU:0, one launch (start us, length us, event | category | flops | bytes accessed | tf_op | source)
XLA Modules:
  0.0 173.0 jit_solution(12228570343709364776)
XLA Ops:
  0.6 2.7 %shard_map.95.refs_5_.refs_0_ = bf16[336,2560]{1,0:T(8,128)(2,1)} custom-call(bf16[192,2560]{1,0:T(8,128)(2,1)} %bitcast.19, bf16[192,2560]{1,0:T(8,128)(2,1)} %bitcast.21, bf16[192,2560]{1,0:T(8,128)(2,1)} %bitcast.23), custom_call_target="tpu_custom_call" | custom-call | tf_op jit(solution)/shard_map/pallas_call | solution.py:269
  3.3 3.0 %collective-permute-start = (bf16[336,2560]{1,0:T(8,128)(2,1)}, bf16[336,2560]{1,0:T(8,128)(2,1)S(1)}, u32[]{:S(2)}, u32[]{:S(2)}) collective-permute-start(bf16[336,2560]{1,0:T(8,128)(2,1)} %shard_map.95.refs_5_.refs_0_), channel_id=1, source_target_pairs={{0,1},{1,0},{2,3},{3,2},{4,5},{5,4},{6,7},{7,6},{8,9},{9,8},{10,11... | collective-permute-start | bytes 5160968 | tf_op jit(solution)/shard_map/ppermute | solution.py:59
  6.4 2.3 %shard_map.96.refs_6_.refs_2_ = bf16[240,2560]{1,0:T(8,128)(2,1)} custom-call(bf16[192,2560]{1,0:T(8,128)(2,1)} %bitcast.20, bf16[192,2560]{1,0:T(8,128)(2,1)} %bitcast.22, bf16[192,2560]{1,0:T(8,128)(2,1)} %bitcast.24), custom_call_target="tpu_custom_call" | custom-call | tf_op jit(solution)/shard_map/pallas_call | solution.py:269
  8.7 1.6 collective-permute-start.1
  10.3 1.3 copy-done.1
  14.4 2.6 %collective-permute-start.2 = (bf16[32,5504]{1,0:T(8,128)(2,1)S(1)}, bf16[32,5504]{1,0:T(8,128)(2,1)S(1)}, u32[]{:S(2)}, u32[]{:S(2)}) collective-permute-start(bf16[32,5504]{1,0:T(8,128)(2,1)S(1)} %get-tuple-element.100), channel_id=1, source_target_pairs={{0,4},{1,5},{2,6},{3,7},{4,0},{5,1},{6,2},{7,3},{8,12},{9,13},{10,... | collective-permute-start | bytes 1056776 | tf_op jit(solution)/shard_map/ppermute | solution.py:59
  18.0 29.9 %collective-permute-done.4.refs_6_ = bf16[16,5504]{1,0:T(8,128)(2,1)S(1)} collective-permute-done((bf16[16,5504]{1,0:T(8,128)(2,1)S(1)}, bf16[16,5504]{1,0:T(8,128)(2,1)S(1)}, u32[]{:S(2)}, u32[]{:S(2)}) %collective-permute-start.4) | collective-permute-done | bytes 176160 | tf_op jit(solution)/shard_map/ppermute | solution.py:59
  49.8 1.6 collective-permute-start.5
  51.4 3.0 %collective-permute-done.6.refs_6_ = bf16[16,5504]{1,0:T(8,128)(2,1)S(1)} collective-permute-done((bf16[16,5504]{1,0:T(8,128)(2,1)S(1)}, bf16[16,5504]{1,0:T(8,128)(2,1)S(1)}, u32[]{:S(2)}, u32[]{:S(2)}) %collective-permute-start.6) | collective-permute-done | bytes 176160 | tf_op jit(solution)/shard_map/ppermute | solution.py:59
  55.2 2.5 %shard_map.98 = (bf16[16,5504]{1,0:T(8,128)(2,1)S(1)}, bf16[16,5504]{1,0:T(8,128)(2,1)S(1)}, bf16[16,5504]{1,0:T(8,128)(2,1)S(1)}, f32[96,224]{1,0:T(8,128)S(1)}...) custom-call(bf16[336,2560]{1,0:T(8,128)(2,1)S(1)} %copy-done, ...), custom_call_target="tpu_custom_call" | custom-call | flops 566231040 | bytes 7249920 | tf_op jit(solution)/shard_map/pallas_call | solution.py:71
  57.7 1.6 collective-permute-start.8
  59.3 1.1 collective-permute-start.9
  61.8 2.5 %shard_map.99 = (bf16[16,5504]{1,0:T(8,128)(2,1)S(1)}, bf16[16,5504]{1,0:T(8,128)(2,1)S(1)}, bf16[16,5504]{1,0:T(8,128)(2,1)S(1)}, f32[96,224]{1,0:T(8,128)S(1)}...) custom-call(bf16[336,2560]{1,0:T(8,128)(2,1)S(1)} %copy-done, ...), custom_call_target="tpu_custom_call" | custom-call | flops 566231040 | bytes 7249920 | tf_op jit(solution)/shard_map/pallas_call | solution.py:71
  65.0 1.7 collective-permute-done.9
  66.8 1.5 collective-permute-start.10
  68.3 2.5 %collective-permute-done.12.refs_6_ = bf16[32,5504]{1,0:T(8,128)(2,1)S(1)} collective-permute-done((bf16[32,5504]{1,0:T(8,128)(2,1)S(1)}, bf16[32,5504]{1,0:T(8,128)(2,1)S(1)}, u32[]{:S(2)}, u32[]{:S(2)}) %collective-permute-start.12) | collective-permute-done | bytes 352288 | tf_op jit(solution)/shard_map/ppermute | solution.py:59
  70.8 1.9 %collective-permute-start.14 = (bf16[16,5504]{1,0:T(8,128)(2,1)S(1)}, bf16[16,5504]{1,0:T(8,128)(2,1)S(1)}, u32[]{:S(2)}, u32[]{:S(2)}) collective-permute-start(bf16[16,5504]{1,0:T(8,128)(2,1)S(1)} %get-tuple-element.128), channel_id=1, source_target_pairs={{0,9},{1,8},{2,11},{3,10},{4,13},{5,12},{6,15},{7,14},{8,17},{9,16... | collective-permute-start | bytes 528392 | tf_op jit(solution)/shard_map/ppermute | solution.py:59
  72.8 6.4 %collective-permute-done.10.refs_4_ = bf16[16,5504]{1,0:T(8,128)(2,1)S(1)} collective-permute-done((bf16[16,5504]{1,0:T(8,128)(2,1)S(1)}, bf16[16,5504]{1,0:T(8,128)(2,1)S(1)}, u32[]{:S(2)}, u32[]{:S(2)}) %collective-permute-start.10) | collective-permute-done | bytes 176160 | tf_op jit(solution)/shard_map/ppermute | solution.py:59
  79.1 1.2 collective-permute-done.13.refs_5_
  80.3 1.1 collective-permute-done.15.refs_7_
  82.4 1.9 %collective-permute-start.16 = (bf16[16,5504]{1,0:T(8,128)(2,1)S(1)}, bf16[16,5504]{1,0:T(8,128)(2,1)S(1)}, u32[]{:S(2)}, u32[]{:S(2)}) collective-permute-start(bf16[16,5504]{1,0:T(8,128)(2,1)S(1)} %get-tuple-element.138), channel_id=1, source_target_pairs={{0,4},{1,5},{2,6},{3,7},{4,0},{5,1},{6,2},{7,3},{8,12},{9,13},{10,... | collective-permute-start | bytes 528392 | tf_op jit(solution)/shard_map/ppermute | solution.py:59
  84.9 2.5 %collective-permute-start.17 = (bf16[16,5504]{1,0:T(8,128)(2,1)S(1)}, bf16[16,5504]{1,0:T(8,128)(2,1)S(1)}, u32[]{:S(2)}, u32[]{:S(2)}) collective-permute-start(bf16[16,5504]{1,0:T(8,128)(2,1)S(1)} %get-tuple-element.139.refs_9_), channel_id=1, source_target_pairs={{0,2},{1,3},{2,0},{3,1},{4,6},{5,7},{6,4},{7,5},{8,10},{9,11},{10,... | collective-permute-start | bytes 528392 | tf_op jit(solution)/shard_map/ppermute | solution.py:59
  87.4 6.7 %collective-permute-done.16.refs_9_ = bf16[16,5504]{1,0:T(8,128)(2,1)S(1)} collective-permute-done((bf16[16,5504]{1,0:T(8,128)(2,1)S(1)}, bf16[16,5504]{1,0:T(8,128)(2,1)S(1)}, u32[]{:S(2)}, u32[]{:S(2)}) %collective-permute-start.16) | collective-permute-done | bytes 176160 | tf_op jit(solution)/shard_map/ppermute | solution.py:59
  94.8 1.0 collective-permute-start.21
  97.6 2.6 %shard_map.103 = (bf16[16,5504]{1,0:T(8,128)(2,1)S(1)}, bf16[16,5504]{1,0:T(8,128)(2,1)S(1)}, bf16[16,5504]{1,0:T(8,128)(2,1)S(1)}, f32[96,224]{1,0:T(8,128)S(1)...) custom-call(bf16[336,2560]{1,0:T(8,128)(2,1)S(1)} %copy-done, ...), custom_call_target="tpu_custom_call" | custom-call | flops 566231040 | bytes 7397376 | tf_op jit(solution)/shard_map/pallas_call | solution.py:71
  101.3 2.6 %shard_map.104 = (bf16[16,5504]{1,0:T(8,128)(2,1)S(1)}, bf16[16,5504]{1,0:T(8,128)(2,1)S(1)}, bf16[16,5504]{1,0:T(8,128)(2,1)S(1)}, f32[96,224]{1,0:T(8,128)S(1)...) custom-call(bf16[336,2560]{1,0:T(8,128)(2,1)S(1)} %copy-done, ...), custom_call_target="tpu_custom_call" | custom-call | flops 566231040 | bytes 7397376 | tf_op jit(solution)/shard_map/pallas_call | solution.py:71
  106.8 1.2 collective-permute-start.34
  109.9 1.0 collective-permute-start.26
  111.9 4.3 %collective-permute-start.28 = (bf16[16,5504]{1,0:T(8,128)(2,1)S(1)}, bf16[16,5504]{1,0:T(8,128)(2,1)S(1)}, u32[]{:S(2)}, u32[]{:S(2)}) collective-permute-start(bf16[16,5504]{1,0:T(8,128)(2,1)S(1)} %get-tuple-element.165.refs_11_), channel_id=1, source_target_pairs={{0,26},{1,27},{2,24},{3,25},{4,30},{5,31},{6,28},{7,29},{8,2},{9,3... | collective-permute-start | bytes 528392 | tf_op jit(solution)/shard_map/ppermute | solution.py:59
  116.1 5.5 %collective-permute-done.25 = bf16[16,5504]{1,0:T(8,128)(2,1)S(1)} collective-permute-done((bf16[16,5504]{1,0:T(8,128)(2,1)S(1)}, bf16[16,5504]{1,0:T(8,128)(2,1)S(1)}, u32[]{:S(2)}, u32[]{:S(2)}) %collective-permute-start.25) | collective-permute-done | bytes 176160 | tf_op jit(solution)/shard_map/ppermute | solution.py:59
  121.6 3.6 %collective-permute-start.30 = (bf16[16,5504]{1,0:T(8,128)(2,1)S(1)}, bf16[16,5504]{1,0:T(8,128)(2,1)S(1)}, u32[]{:S(2)}, u32[]{:S(2)}) collective-permute-start(bf16[16,5504]{1,0:T(8,128)(2,1)S(1)} %get-tuple-element.167), channel_id=1, source_target_pairs={{0,24},{1,25},{2,26},{3,27},{4,28},{5,29},{6,30},{7,31},{8,0},{9,1... | collective-permute-start | bytes 528392 | tf_op jit(solution)/shard_map/ppermute | solution.py:59
  125.4 2.8 %collective-permute-done.29.refs_4_ = bf16[16,5504]{1,0:T(8,128)(2,1)S(1)} collective-permute-done((bf16[16,5504]{1,0:T(8,128)(2,1)S(1)}, bf16[16,5504]{1,0:T(8,128)(2,1)S(1)}, u32[]{:S(2)}, u32[]{:S(2)}) %collective-permute-start.29) | collective-permute-done | bytes 176160 | tf_op jit(solution)/shard_map/ppermute | solution.py:59
  129.8 1.6 collective-permute-start.31
  132.2 2.5 %collective-permute-start.32 = (bf16[16,5504]{1,0:T(8,128)(2,1)S(1)}, bf16[16,5504]{1,0:T(8,128)(2,1)S(1)}, u32[]{:S(2)}, u32[]{:S(2)}) collective-permute-start(bf16[16,5504]{1,0:T(8,128)(2,1)S(1)} %get-tuple-element.169.refs_9_), channel_id=1, source_target_pairs={{0,2},{1,3},{2,0},{3,1},{4,6},{5,7},{6,4},{7,5},{8,10},{9,11},{10,... | collective-permute-start | bytes 528392 | tf_op jit(solution)/shard_map/ppermute | solution.py:59
  134.7 7.0 %collective-permute-done.31.refs_9_ = bf16[16,5504]{1,0:T(8,128)(2,1)S(1)} collective-permute-done((bf16[16,5504]{1,0:T(8,128)(2,1)S(1)}, bf16[16,5504]{1,0:T(8,128)(2,1)S(1)}, u32[]{:S(2)}, u32[]{:S(2)}) %collective-permute-start.31) | collective-permute-done | bytes 176160 | tf_op jit(solution)/shard_map/ppermute | solution.py:59
  141.7 1.8 %collective-permute-done.32.refs_8_ = bf16[16,5504]{1,0:T(8,128)(2,1)S(1)} collective-permute-done((bf16[16,5504]{1,0:T(8,128)(2,1)S(1)}, bf16[16,5504]{1,0:T(8,128)(2,1)S(1)}, u32[]{:S(2)}, u32[]{:S(2)}) %collective-permute-start.32) | collective-permute-done | bytes 176160 | tf_op jit(solution)/shard_map/ppermute | solution.py:59
  143.5 2.8 %collective-permute-start.27 = (bf16[16,5504]{1,0:T(8,128)(2,1)S(1)}, bf16[16,5504]{1,0:T(8,128)(2,1)S(1)}, u32[]{:S(2)}, u32[]{:S(2)}) collective-permute-start(bf16[16,5504]{1,0:T(8,128)(2,1)S(1)} %add_convert_fusion.1), channel_id=1, source_target_pairs={{0,4},{1,5},{2,6},{3,7},{4,0},{5,1},{6,2},{7,3},{8,12},{9,13},{10,... | collective-permute-start | bytes 528392 | tf_op jit(solution)/shard_map/ppermute | solution.py:59
  146.3 3.7 %collective-permute-done.37.refs_10_ = bf16[16,5504]{1,0:T(8,128)(2,1)S(1)} collective-permute-done((bf16[16,5504]{1,0:T(8,128)(2,1)S(1)}, bf16[16,5504]{1,0:T(8,128)(2,1)S(1)}, u32[]{:S(2)}, u32[]{:S(2)}) %collective-permute-start.37) | collective-permute-done | bytes 176160 | tf_op jit(solution)/shard_map/ppermute | solution.py:59
  150.0 2.9 %collective-permute-done.36.refs_8_ = bf16[16,5504]{1,0:T(8,128)(2,1)S(1)} collective-permute-done((bf16[16,5504]{1,0:T(8,128)(2,1)S(1)}, bf16[16,5504]{1,0:T(8,128)(2,1)S(1)}, u32[]{:S(2)}, u32[]{:S(2)}) %collective-permute-start.36) | collective-permute-done | bytes 176160 | tf_op jit(solution)/shard_map/ppermute | solution.py:59
  152.9 2.0 %shard_map.109 = (bf16[16,5504]{1,0:T(8,128)(2,1)S(1)}, bf16[16,5504]{1,0:T(8,128)(2,1)S(1)}, bf16[16,5504]{1,0:T(8,128)(2,1)S(1)}) custom-call(bf16[336,2560]{1,0:T(8,128)(2,1)S(1)} %copy-done, bf16[336,2560]{1,0:T(8,128)(2,1)S(1)} %collective-permute-done.refs_1_, bf16[240,2560]{1,0:T(8,128)(2,1)S(1)} %copy-done.2, ...), custom_call_target="tpu_custom_call" | custom-call | flops 566231040 | bytes 7249920 | tf_op jit(solution)/shard_map/pallas_call | solution.py:71
  154.8 1.8 %collective-permute-start.39 = (bf16[16,5504]{1,0:T(8,128)(2,1)S(1)}, bf16[16,5504]{1,0:T(8,128)(2,1)S(1)}, u32[]{:S(2)}, u32[]{:S(2)}) collective-permute-start(bf16[16,5504]{1,0:T(8,128)(2,1)S(1)} %get-tuple-element.188), channel_id=1, source_target_pairs={{0,1},{1,0},{2,3},{3,2},{4,5},{5,4},{6,7},{7,6},{8,9},{9,8},{10,11... | collective-permute-start | bytes 528392 | tf_op jit(solution)/shard_map/ppermute | solution.py:59
  156.6 2.0 %shard_map.110 = (bf16[16,5504]{1,0:T(8,128)(2,1)S(1)}, bf16[16,5504]{1,0:T(8,128)(2,1)S(1)}, bf16[16,5504]{1,0:T(8,128)(2,1)S(1)}) custom-call(bf16[336,2560]{1,0:T(8,128)(2,1)S(1)} %copy-done, bf16[336,2560]{1,0:T(8,128)(2,1)S(1)} %collective-permute-done.refs_1_, bf16[240,2560]{1,0:T(8,128)(2,1)S(1)} %copy-done.2, ...), custom_call_target="tpu_custom_call" | custom-call | flops 566231040 | bytes 7249920 | tf_op jit(solution)/shard_map/pallas_call | solution.py:71
  158.6 2.1 %collective-permute-start.41 = (bf16[16,5504]{1,0:T(8,128)(2,1)S(1)}, bf16[16,5504]{1,0:T(8,128)(2,1)S(1)}, u32[]{:S(2)}, u32[]{:S(2)}) collective-permute-start(bf16[16,5504]{1,0:T(8,128)(2,1)S(1)} %get-tuple-element.195), channel_id=1, source_target_pairs={{0,2},{1,3},{2,0},{3,1},{4,6},{5,7},{6,4},{7,5},{8,10},{9,11},{10,... | collective-permute-start | bytes 528392 | tf_op jit(solution)/shard_map/ppermute | solution.py:59
  161.0 3.4 %collective-permute-done.38 = bf16[16,5504]{1,0:T(8,128)(2,1)S(1)} collective-permute-done((bf16[16,5504]{1,0:T(8,128)(2,1)S(1)}, bf16[16,5504]{1,0:T(8,128)(2,1)S(1)}, u32[]{:S(2)}, u32[]{:S(2)}) %collective-permute-start.38) | collective-permute-done | bytes 176160 | tf_op jit(solution)/shard_map/ppermute | solution.py:59
  164.6 1.1 shard_map.108
  165.7 2.0 %collective-permute-done.41.refs_5_ = bf16[16,5504]{1,0:T(8,128)(2,1)S(1)} collective-permute-done((bf16[16,5504]{1,0:T(8,128)(2,1)S(1)}, bf16[16,5504]{1,0:T(8,128)(2,1)S(1)}, u32[]{:S(2)}, u32[]{:S(2)}) %collective-permute-start.41) | collective-permute-done | bytes 176160 | tf_op jit(solution)/shard_map/ppermute | solution.py:59
  167.7 4.0 %collective-permute-done.40.refs_4_ = bf16[16,5504]{1,0:T(8,128)(2,1)S(1)} collective-permute-done((bf16[16,5504]{1,0:T(8,128)(2,1)S(1)}, bf16[16,5504]{1,0:T(8,128)(2,1)S(1)}, u32[]{:S(2)}, u32[]{:S(2)}) %collective-permute-start.40) | collective-permute-done | bytes 176160 | tf_op jit(solution)/shard_map/ppermute | solution.py:59
  171.6 1.3 shard_map.111
  (81 shorter events, 22.5 us)
Async XLA Ops:
  3.3 7.0 %copy-start = (bf16[336,2560]{1,0:T(8,128)(2,1)S(1)}, bf16[336,2560]{1,0:T(8,128)(2,1)}, u32[]{:S(2)}) copy-start(bf16[336,2560]{1,0:T(8,128)(2,1)} %shard_map.95.refs_5_.refs_0_) | copy-start | bytes 5160964
  3.3 7.0 %copy-start.7 = (f32[1,2560]{1,0:T(1,128)S(1)}, f32[1,2560]{1,0:T(1,128)}, u32[]{:S(2)}) copy-start(f32[1,2560]{1,0:T(1,128)} %refs_3_.3) | copy-start | bytes 30724
  3.3 45.4 %collective-permute-start = (bf16[336,2560]{1,0:T(8,128)(2,1)}, bf16[336,2560]{1,0:T(8,128)(2,1)S(1)}, u32[]{:S(2)}, u32[]{:S(2)}) collective-permute-start(bf16[336,2560]{1,0:T(8,128)(2,1)} %shard_map.95.refs_5_.refs_0_), channel_id=1, source_target_pairs={{0,1},{1,0},{2,3},{3,2},{4,5},{5,4},{6,7},{7,6},{8,9},{9,8},{10,11... | collective-permute-start | bytes 5160968 | tf_op jit(solution)/shard_map/ppermute | solution.py:59
  8.7 40.1 %collective-permute-start.1 = (bf16[240,2560]{1,0:T(8,128)(2,1)}, bf16[240,2560]{1,0:T(8,128)(2,1)S(1)}, u32[]{:S(2)}, u32[]{:S(2)}) collective-permute-start(bf16[240,2560]{1,0:T(8,128)(2,1)} %shard_map.96.refs_6_.refs_2_), channel_id=1, source_target_pairs={{0,2},{1,3},{2,0},{3,1},{4,6},{5,7},{6,4},{7,5},{8,10},{9,11},{10,... | collective-permute-start | bytes 3686408 | tf_op jit(solution)/shard_map/ppermute | solution.py:59
  13.6 41.6 %copy-start.2 = (bf16[240,2560]{1,0:T(8,128)(2,1)S(1)}, bf16[240,2560]{1,0:T(8,128)(2,1)}, u32[]{:S(2)}) copy-start(bf16[240,2560]{1,0:T(8,128)(2,1)} %shard_map.96.refs_6_.refs_2_) | copy-start | bytes 3686404
  14.4 34.3 %collective-permute-start.2 = (bf16[32,5504]{1,0:T(8,128)(2,1)S(1)}, bf16[32,5504]{1,0:T(8,128)(2,1)S(1)}, u32[]{:S(2)}, u32[]{:S(2)}) collective-permute-start(bf16[32,5504]{1,0:T(8,128)(2,1)S(1)} %get-tuple-element.100), channel_id=1, source_target_pairs={{0,4},{1,5},{2,6},{3,7},{4,0},{5,1},{6,2},{7,3},{8,12},{9,13},{10,... | collective-permute-start | bytes 1056776 | tf_op jit(solution)/shard_map/ppermute | solution.py:59
  17.1 30.8 %collective-permute-start.4 = (bf16[16,5504]{1,0:T(8,128)(2,1)S(1)}, bf16[16,5504]{1,0:T(8,128)(2,1)S(1)}, u32[]{:S(2)}, u32[]{:S(2)}) collective-permute-start(bf16[16,5504]{1,0:T(8,128)(2,1)S(1)} %get-tuple-element.121.refs_5_), channel_id=1, source_target_pairs={{0,1},{1,0},{2,3},{3,2},{4,5},{5,4},{6,7},{7,6},{8,9},{9,8},{10,11... | collective-permute-start | bytes 528392 | tf_op jit(solution)/shard_map/ppermute | solution.py:59
  17.6 31.2 %collective-permute-start.3 = (bf16[16,5504]{1,0:T(8,128)(2,1)S(1)}, bf16[16,5504]{1,0:T(8,128)(2,1)S(1)}, u32[]{:S(2)}, u32[]{:S(2)}) collective-permute-start(bf16[16,5504]{1,0:T(8,128)(2,1)S(1)} %get-tuple-element.121.refs_5_), channel_id=1, source_target_pairs={{0,2},{1,3},{2,0},{3,1},{4,6},{5,7},{6,4},{7,5},{8,10},{9,11},{10,... | collective-permute-start | bytes 528392 | tf_op jit(solution)/shard_map/ppermute | solution.py:59
  48.8 5.5 %collective-permute-start.6 = (bf16[16,5504]{1,0:T(8,128)(2,1)S(1)}, bf16[16,5504]{1,0:T(8,128)(2,1)S(1)}, u32[]{:S(2)}, u32[]{:S(2)}) collective-permute-start(bf16[16,5504]{1,0:T(8,128)(2,1)S(1)} %get-tuple-element.109.refs_5_), channel_id=1, source_target_pairs={{0,1},{1,0},{2,3},{3,2},{4,5},{5,4},{6,7},{7,6},{8,9},{9,8},{10,11... | collective-permute-start | bytes 528392 | tf_op jit(solution)/shard_map/ppermute | solution.py:59
  49.8 5.5 %collective-permute-start.5 = (bf16[16,5504]{1,0:T(8,128)(2,1)S(1)}, bf16[16,5504]{1,0:T(8,128)(2,1)S(1)}, u32[]{:S(2)}, u32[]{:S(2)}) collective-permute-start(bf16[16,5504]{1,0:T(8,128)(2,1)S(1)} %get-tuple-element.109.refs_5_), channel_id=1, source_target_pairs={{0,2},{1,3},{2,0},{3,1},{4,6},{5,7},{6,4},{7,5},{8,10},{9,11},{10,... | collective-permute-start | bytes 528392 | tf_op jit(solution)/shard_map/ppermute | solution.py:59
  57.7 23.7 %copy-start.4 = (bf16[1,64,2560]{2,1,0:T(8,128)(2,1)S(1)}, bf16[1,64,2560]{2,1,0:T(8,128)(2,1)}, u32[]{:S(2)}) copy-start(bf16[1,64,2560]{2,1,0:T(8,128)(2,1)} %param.15) | copy-start | bytes 983044
  57.7 7.3 %collective-permute-start.8 = (bf16[16,5504]{1,0:T(8,128)(2,1)S(1)}, bf16[16,5504]{1,0:T(8,128)(2,1)S(1)}, u32[]{:S(2)}, u32[]{:S(2)}) collective-permute-start(bf16[16,5504]{1,0:T(8,128)(2,1)S(1)} %get-tuple-element.118.refs_7_), channel_id=1, source_target_pairs={{0,2},{1,3},{2,0},{3,1},{4,6},{5,7},{6,4},{7,5},{8,10},{9,11},{10,... | collective-permute-start | bytes 528392 | tf_op jit(solution)/shard_map/ppermute | solution.py:59
  59.3 7.4 %collective-permute-start.9 = (bf16[16,5504]{1,0:T(8,128)(2,1)S(1)}, bf16[16,5504]{1,0:T(8,128)(2,1)S(1)}, u32[]{:S(2)}, u32[]{:S(2)}) collective-permute-start(bf16[16,5504]{1,0:T(8,128)(2,1)S(1)} %get-tuple-element.119), channel_id=1, source_target_pairs={{0,1},{1,0},{2,3},{3,2},{4,5},{5,4},{6,7},{7,6},{8,9},{9,8},{10,11... | collective-permute-start | bytes 528392 | tf_op jit(solution)/shard_map/ppermute | solution.py:59
  60.5 10.3 %collective-permute-start.12 = (bf16[32,5504]{1,0:T(8,128)(2,1)S(1)}, bf16[32,5504]{1,0:T(8,128)(2,1)S(1)}, u32[]{:S(2)}, u32[]{:S(2)}) collective-permute-start(bf16[32,5504]{1,0:T(8,128)(2,1)S(1)} %pad_maximum_fusion.refs_5_), channel_id=1, source_target_pairs={{0,1},{1,0},{2,3},{3,2},{4,5},{5,4},{6,7},{7,6},{8,9},{9,8},{10,11... | collective-permute-start | bytes 1056776 | tf_op jit(solution)/shard_map/ppermute | solution.py:59
  61.4 9.5 %collective-permute-start.11 = (bf16[32,5504]{1,0:T(8,128)(2,1)S(1)}, bf16[32,5504]{1,0:T(8,128)(2,1)S(1)}, u32[]{:S(2)}, u32[]{:S(2)}) collective-permute-start(bf16[32,5504]{1,0:T(8,128)(2,1)S(1)} %pad_maximum_fusion.refs_5_), channel_id=1, source_target_pairs={{0,2},{1,3},{2,0},{3,1},{4,6},{5,7},{6,4},{7,5},{8,10},{9,11},{10,... | collective-permute-start | bytes 1056776 | tf_op jit(solution)/shard_map/ppermute | solution.py:59
  61.8 17.3 %collective-permute-start.7 = (bf16[80,2560]{1,0:T(8,128)(2,1)S(1)}, bf16[80,2560]{1,0:T(8,128)(2,1)S(1)}, u32[]{:S(2)}, u32[]{:S(2)}) collective-permute-start(bf16[80,2560]{1,0:T(8,128)(2,1)S(1)} %get-tuple-element.115), channel_id=1, source_target_pairs={{0,8},{1,9},{2,10},{3,11},{4,12},{5,13},{6,14},{7,15},{8,16},{9,17... | collective-permute-start | bytes 1228808 | tf_op jit(solution)/shard_map/ppermute | solution.py:59
  66.8 12.3 %collective-permute-start.10 = (bf16[16,5504]{1,0:T(8,128)(2,1)S(1)}, bf16[16,5504]{1,0:T(8,128)(2,1)S(1)}, u32[]{:S(2)}, u32[]{:S(2)}) collective-permute-start(bf16[16,5504]{1,0:T(8,128)(2,1)S(1)} %add_convert_fusion.3), channel_id=1, source_target_pairs={{0,12},{1,13},{2,14},{3,15},{4,8},{5,9},{6,10},{7,11},{8,20},{9,21... | collective-permute-start | bytes 528392 | tf_op jit(solution)/shard_map/ppermute | solution.py:59
  70.8 9.5 %collective-permute-start.13 = (bf16[16,5504]{1,0:T(8,128)(2,1)S(1)}, bf16[16,5504]{1,0:T(8,128)(2,1)S(1)}, u32[]{:S(2)}, u32[]{:S(2)}) collective-permute-start(bf16[16,5504]{1,0:T(8,128)(2,1)S(1)} %get-tuple-element.127), channel_id=1, source_target_pairs={{0,10},{1,11},{2,8},{3,9},{4,14},{5,15},{6,12},{7,13},{8,18},{9,19... | collective-permute-start | bytes 528392 | tf_op jit(solution)/shard_map/ppermute | solution.py:59
  70.8 9.5 %collective-permute-start.14 = (bf16[16,5504]{1,0:T(8,128)(2,1)S(1)}, bf16[16,5504]{1,0:T(8,128)(2,1)S(1)}, u32[]{:S(2)}, u32[]{:S(2)}) collective-permute-start(bf16[16,5504]{1,0:T(8,128)(2,1)S(1)} %get-tuple-element.128), channel_id=1, source_target_pairs={{0,9},{1,8},{2,11},{3,10},{4,13},{5,12},{6,15},{7,14},{8,17},{9,16... | collective-permute-start | bytes 528392 | tf_op jit(solution)/shard_map/ppermute | solution.py:59
  72.8 8.7 %collective-permute-start.15 = (bf16[16,5504]{1,0:T(8,128)(2,1)S(1)}, bf16[16,5504]{1,0:T(8,128)(2,1)S(1)}, u32[]{:S(2)}, u32[]{:S(2)}) collective-permute-start(bf16[16,5504]{1,0:T(8,128)(2,1)S(1)} %get-tuple-element.129), channel_id=1, source_target_pairs={{0,8},{1,9},{2,10},{3,11},{4,12},{5,13},{6,14},{7,15},{8,16},{9,17... | collective-permute-start | bytes 528392 | tf_op jit(solution)/shard_map/ppermute | solution.py:59
  82.3 12.5 %collective-permute-start.19 = (bf16[144,2560]{1,0:T(8,128)(2,1)S(1)}, bf16[144,2560]{1,0:T(8,128)(2,1)S(1)}, u32[]{:S(2)}, u32[]{:S(2)}) collective-permute-start(bf16[144,2560]{1,0:T(8,128)(2,1)S(1)} %get-tuple-element.140), channel_id=1, source_target_pairs={{0,24},{1,25},{2,26},{3,27},{4,28},{5,29},{6,30},{7,31},{8,0},{9,1... | collective-permute-start | bytes 2211848 | tf_op jit(solution)/shard_map/ppermute | solution.py:59
  82.4 11.7 %collective-permute-start.16 = (bf16[16,5504]{1,0:T(8,128)(2,1)S(1)}, bf16[16,5504]{1,0:T(8,128)(2,1)S(1)}, u32[]{:S(2)}, u32[]{:S(2)}) collective-permute-start(bf16[16,5504]{1,0:T(8,128)(2,1)S(1)} %get-tuple-element.138), channel_id=1, source_target_pairs={{0,4},{1,5},{2,6},{3,7},{4,0},{5,1},{6,2},{7,3},{8,12},{9,13},{10,... | collective-permute-start | bytes 528392 | tf_op jit(solution)/shard_map/ppermute | solution.py:59
  84.3 9.7 %collective-permute-start.18 = (bf16[16,5504]{1,0:T(8,128)(2,1)S(1)}, bf16[16,5504]{1,0:T(8,128)(2,1)S(1)}, u32[]{:S(2)}, u32[]{:S(2)}) collective-permute-start(bf16[16,5504]{1,0:T(8,128)(2,1)S(1)} %get-tuple-element.139.refs_9_), channel_id=1, source_target_pairs={{0,1},{1,0},{2,3},{3,2},{4,5},{5,4},{6,7},{7,6},{8,9},{9,8},{10,11... | collective-permute-start | bytes 528392 | tf_op jit(solution)/shard_map/ppermute | solution.py:59
  84.9 9.9 %collective-permute-start.17 = (bf16[16,5504]{1,0:T(8,128)(2,1)S(1)}, bf16[16,5504]{1,0:T(8,128)(2,1)S(1)}, u32[]{:S(2)}, u32[]{:S(2)}) collective-permute-start(bf16[16,5504]{1,0:T(8,128)(2,1)S(1)} %get-tuple-element.139.refs_9_), channel_id=1, source_target_pairs={{0,2},{1,3},{2,0},{3,1},{4,6},{5,7},{6,4},{7,5},{8,10},{9,11},{10,... | collective-permute-start | bytes 528392 | tf_op jit(solution)/shard_map/ppermute | solution.py:59
  94.8 5.5 %collective-permute-start.21 = (bf16[16,5504]{1,0:T(8,128)(2,1)S(1)}, bf16[16,5504]{1,0:T(8,128)(2,1)S(1)}, u32[]{:S(2)}, u32[]{:S(2)}) collective-permute-start(bf16[16,5504]{1,0:T(8,128)(2,1)S(1)} %collective-permute-done.16.refs_9_), channel_id=1, source_target_pairs={{0,1},{1,0},{2,3},{3,2},{4,5},{5,4},{6,7},{7,6},{8,9},{9,8},{10,11... | collective-permute-start | bytes 528392 | tf_op jit(solution)/shard_map/ppermute | solution.py:59
  95.9 5.5 %collective-permute-start.20 = (bf16[16,5504]{1,0:T(8,128)(2,1)S(1)}, bf16[16,5504]{1,0:T(8,128)(2,1)S(1)}, u32[]{:S(2)}, u32[]{:S(2)}) collective-permute-start(bf16[16,5504]{1,0:T(8,128)(2,1)S(1)} %collective-permute-done.16.refs_9_), channel_id=1, source_target_pairs={{0,2},{1,3},{2,0},{3,1},{4,6},{5,7},{6,4},{7,5},{8,10},{9,11},{10,... | collective-permute-start | bytes 528392 | tf_op jit(solution)/shard_map/ppermute | solution.py:59
  103.9 7.4 %collective-permute-start.22 = (bf16[16,5504]{1,0:T(8,128)(2,1)S(1)}, bf16[16,5504]{1,0:T(8,128)(2,1)S(1)}, u32[]{:S(2)}, u32[]{:S(2)}) collective-permute-start(bf16[16,5504]{1,0:T(8,128)(2,1)S(1)} %get-tuple-element.150), channel_id=1, source_target_pairs={{0,2},{1,3},{2,0},{3,1},{4,6},{5,7},{6,4},{7,5},{8,10},{9,11},{10,... | collective-permute-start | bytes 528392 | tf_op jit(solution)/shard_map/ppermute | solution.py:59
  104.9 6.4 %collective-permute-start.23 = (bf16[16,5504]{1,0:T(8,128)(2,1)S(1)}, bf16[16,5504]{1,0:T(8,128)(2,1)S(1)}, u32[]{:S(2)}, u32[]{:S(2)}) collective-permute-start(bf16[16,5504]{1,0:T(8,128)(2,1)S(1)} %get-tuple-element.151), channel_id=1, source_target_pairs={{0,1},{1,0},{2,3},{3,2},{4,5},{5,4},{6,7},{7,6},{8,9},{9,8},{10,11... | collective-permute-start | bytes 528392 | tf_op jit(solution)/shard_map/ppermute | solution.py:59
  106.8 27.9 %collective-permute-start.34 = (bf16[16,5504]{1,0:T(8,128)(2,1)S(1)}, bf16[16,5504]{1,0:T(8,128)(2,1)S(1)}, u32[]{:S(2)}, u32[]{:S(2)}) collective-permute-start(bf16[16,5504]{1,0:T(8,128)(2,1)S(1)} %get-tuple-element.174), channel_id=1, source_target_pairs={{0,2},{1,3},{2,0},{3,1},{4,6},{5,7},{6,4},{7,5},{8,10},{9,11},{10,... | collective-permute-start | bytes 528392 | tf_op jit(solution)/shard_map/ppermute | solution.py:59
  108.9 12.7 %collective-permute-start.25 = (bf16[16,5504]{1,0:T(8,128)(2,1)S(1)}, bf16[16,5504]{1,0:T(8,128)(2,1)S(1)}, u32[]{:S(2)}, u32[]{:S(2)}) collective-permute-start(bf16[16,5504]{1,0:T(8,128)(2,1)S(1)} %get-tuple-element.157), channel_id=1, source_target_pairs={{0,2},{1,3},{2,0},{3,1},{4,6},{5,7},{6,4},{7,5},{8,10},{9,11},{10,... | collective-permute-start | bytes 528392 | tf_op jit(solution)/shard_map/ppermute | solution.py:59
  109.9 11.8 %collective-permute-start.26 = (bf16[16,5504]{1,0:T(8,128)(2,1)S(1)}, bf16[16,5504]{1,0:T(8,128)(2,1)S(1)}, u32[]{:S(2)}, u32[]{:S(2)}) collective-permute-start(bf16[16,5504]{1,0:T(8,128)(2,1)S(1)} %get-tuple-element.158), channel_id=1, source_target_pairs={{0,1},{1,0},{2,3},{3,2},{4,5},{5,4},{6,7},{7,6},{8,9},{9,8},{10,11... | collective-permute-start | bytes 528392 | tf_op jit(solution)/shard_map/ppermute | solution.py:59
  111.4 13.9 %collective-permute-start.24 = (bf16[16,5504]{1,0:T(8,128)(2,1)S(1)}, bf16[16,5504]{1,0:T(8,128)(2,1)S(1)}, u32[]{:S(2)}, u32[]{:S(2)}) collective-permute-start(bf16[16,5504]{1,0:T(8,128)(2,1)S(1)} %add_convert_fusion.2), channel_id=1, source_target_pairs={{0,28},{1,29},{2,30},{3,31},{4,24},{5,25},{6,26},{7,27},{8,4},{9,5... | collective-permute-start | bytes 528392 | tf_op jit(solution)/shard_map/ppermute | solution.py:59
  111.9 13.5 %collective-permute-start.28 = (bf16[16,5504]{1,0:T(8,128)(2,1)S(1)}, bf16[16,5504]{1,0:T(8,128)(2,1)S(1)}, u32[]{:S(2)}, u32[]{:S(2)}) collective-permute-start(bf16[16,5504]{1,0:T(8,128)(2,1)S(1)} %get-tuple-element.165.refs_11_), channel_id=1, source_target_pairs={{0,26},{1,27},{2,24},{3,25},{4,30},{5,31},{6,28},{7,29},{8,2},{9,3... | collective-permute-start | bytes 528392 | tf_op jit(solution)/shard_map/ppermute | solution.py:59
  121.6 6.6 %collective-permute-start.29 = (bf16[16,5504]{1,0:T(8,128)(2,1)S(1)}, bf16[16,5504]{1,0:T(8,128)(2,1)S(1)}, u32[]{:S(2)}, u32[]{:S(2)}) collective-permute-start(bf16[16,5504]{1,0:T(8,128)(2,1)S(1)} %get-tuple-element.166), channel_id=1, source_target_pairs={{0,25},{1,24},{2,27},{3,26},{4,29},{5,28},{6,31},{7,30},{8,1},{9,0... | collective-permute-start | bytes 528392 | tf_op jit(solution)/shard_map/ppermute | solution.py:59
  121.6 7.2 %collective-permute-start.30 = (bf16[16,5504]{1,0:T(8,128)(2,1)S(1)}, bf16[16,5504]{1,0:T(8,128)(2,1)S(1)}, u32[]{:S(2)}, u32[]{:S(2)}) collective-permute-start(bf16[16,5504]{1,0:T(8,128)(2,1)S(1)} %get-tuple-element.167), channel_id=1, source_target_pairs={{0,24},{1,25},{2,26},{3,27},{4,28},{5,29},{6,30},{7,31},{8,0},{9,1... | collective-permute-start | bytes 528392 | tf_op jit(solution)/shard_map/ppermute | solution.py:59
  125.3 9.4 %collective-permute-start.35 = (bf16[16,5504]{1,0:T(8,128)(2,1)S(1)}, bf16[16,5504]{1,0:T(8,128)(2,1)S(1)}, u32[]{:S(2)}, u32[]{:S(2)}) collective-permute-start(bf16[16,5504]{1,0:T(8,128)(2,1)S(1)} %get-tuple-element.175), channel_id=1, source_target_pairs={{0,1},{1,0},{2,3},{3,2},{4,5},{5,4},{6,7},{7,6},{8,9},{9,8},{10,11... | collective-permute-start | bytes 528392 | tf_op jit(solution)/shard_map/ppermute | solution.py:59
  129.8 11.9 %collective-permute-start.31 = (bf16[16,5504]{1,0:T(8,128)(2,1)S(1)}, bf16[16,5504]{1,0:T(8,128)(2,1)S(1)}, u32[]{:S(2)}, u32[]{:S(2)}) collective-permute-start(bf16[16,5504]{1,0:T(8,128)(2,1)S(1)} %get-tuple-element.168), channel_id=1, source_target_pairs={{0,4},{1,5},{2,6},{3,7},{4,0},{5,1},{6,2},{7,3},{8,12},{9,13},{10,... | collective-permute-start | bytes 528392 | tf_op jit(solution)/shard_map/ppermute | solution.py:59
  131.4 10.3 %collective-permute-start.33 = (bf16[16,5504]{1,0:T(8,128)(2,1)S(1)}, bf16[16,5504]{1,0:T(8,128)(2,1)S(1)}, u32[]{:S(2)}, u32[]{:S(2)}) collective-permute-start(bf16[16,5504]{1,0:T(8,128)(2,1)S(1)} %get-tuple-element.169.refs_9_), channel_id=1, source_target_pairs={{0,1},{1,0},{2,3},{3,2},{4,5},{5,4},{6,7},{7,6},{8,9},{9,8},{10,11... | collective-permute-start | bytes 528392 | tf_op jit(solution)/shard_map/ppermute | solution.py:59
  132.2 11.3 %collective-permute-start.32 = (bf16[16,5504]{1,0:T(8,128)(2,1)S(1)}, bf16[16,5504]{1,0:T(8,128)(2,1)S(1)}, u32[]{:S(2)}, u32[]{:S(2)}) collective-permute-start(bf16[16,5504]{1,0:T(8,128)(2,1)S(1)} %get-tuple-element.169.refs_9_), channel_id=1, source_target_pairs={{0,2},{1,3},{2,0},{3,1},{4,6},{5,7},{6,4},{7,5},{8,10},{9,11},{10,... | collective-permute-start | bytes 528392 | tf_op jit(solution)/shard_map/ppermute | solution.py:59
  143.5 6.5 %collective-permute-start.37 = (bf16[16,5504]{1,0:T(8,128)(2,1)S(1)}, bf16[16,5504]{1,0:T(8,128)(2,1)S(1)}, u32[]{:S(2)}, u32[]{:S(2)}) collective-permute-start(bf16[16,5504]{1,0:T(8,128)(2,1)S(1)} %collective-permute-done.31.refs_9_), channel_id=1, source_target_pairs={{0,1},{1,0},{2,3},{3,2},{4,5},{5,4},{6,7},{7,6},{8,9},{9,8},{10,11... | collective-permute-start | bytes 528392 | tf_op jit(solution)/shard_map/ppermute | solution.py:59
  143.5 9.4 %collective-permute-start.36 = (bf16[16,5504]{1,0:T(8,128)(2,1)S(1)}, bf16[16,5504]{1,0:T(8,128)(2,1)S(1)}, u32[]{:S(2)}, u32[]{:S(2)}) collective-permute-start(bf16[16,5504]{1,0:T(8,128)(2,1)S(1)} %collective-permute-done.31.refs_9_), channel_id=1, source_target_pairs={{0,2},{1,3},{2,0},{3,1},{4,6},{5,7},{6,4},{7,5},{8,10},{9,11},{10,... | collective-permute-start | bytes 528392 | tf_op jit(solution)/shard_map/ppermute | solution.py:59
  143.5 13.2 %collective-permute-start.27 = (bf16[16,5504]{1,0:T(8,128)(2,1)S(1)}, bf16[16,5504]{1,0:T(8,128)(2,1)S(1)}, u32[]{:S(2)}, u32[]{:S(2)}) collective-permute-start(bf16[16,5504]{1,0:T(8,128)(2,1)S(1)} %add_convert_fusion.1), channel_id=1, source_target_pairs={{0,4},{1,5},{2,6},{3,7},{4,0},{5,1},{6,2},{7,3},{8,12},{9,13},{10,... | collective-permute-start | bytes 528392 | tf_op jit(solution)/shard_map/ppermute | solution.py:59
  154.8 6.2 %collective-permute-start.39 = (bf16[16,5504]{1,0:T(8,128)(2,1)S(1)}, bf16[16,5504]{1,0:T(8,128)(2,1)S(1)}, u32[]{:S(2)}, u32[]{:S(2)}) collective-permute-start(bf16[16,5504]{1,0:T(8,128)(2,1)S(1)} %get-tuple-element.188), channel_id=1, source_target_pairs={{0,1},{1,0},{2,3},{3,2},{4,5},{5,4},{6,7},{7,6},{8,9},{9,8},{10,11... | collective-permute-start | bytes 528392 | tf_op jit(solution)/shard_map/ppermute | solution.py:59
  156.6 7.8 %collective-permute-start.38 = (bf16[16,5504]{1,0:T(8,128)(2,1)S(1)}, bf16[16,5504]{1,0:T(8,128)(2,1)S(1)}, u32[]{:S(2)}, u32[]{:S(2)}) collective-permute-start(bf16[16,5504]{1,0:T(8,128)(2,1)S(1)} %get-tuple-element.187.refs_11_), channel_id=1, source_target_pairs={{0,2},{1,3},{2,0},{3,1},{4,6},{5,7},{6,4},{7,5},{8,10},{9,11},{10,... | collective-permute-start | bytes 528392 | tf_op jit(solution)/shard_map/ppermute | solution.py:59
  158.6 13.0 %copy-start.6 = (bf16[1,64,2560]{2,1,0:T(8,128)(2,1)S(1)}, bf16[1,64,2560]{2,1,0:T(8,128)(2,1)}, u32[]{:S(2)}) copy-start(bf16[1,64,2560]{2,1,0:T(8,128)(2,1)} %param.8) | copy-start | bytes 983044
  158.6 9.0 %collective-permute-start.41 = (bf16[16,5504]{1,0:T(8,128)(2,1)S(1)}, bf16[16,5504]{1,0:T(8,128)(2,1)S(1)}, u32[]{:S(2)}, u32[]{:S(2)}) collective-permute-start(bf16[16,5504]{1,0:T(8,128)(2,1)S(1)} %get-tuple-element.195), channel_id=1, source_target_pairs={{0,2},{1,3},{2,0},{3,1},{4,6},{5,7},{6,4},{7,5},{8,10},{9,11},{10,... | collective-permute-start | bytes 528392 | tf_op jit(solution)/shard_map/ppermute | solution.py:59
  160.7 6.9 %collective-permute-start.42 = (bf16[16,5504]{1,0:T(8,128)(2,1)S(1)}, bf16[16,5504]{1,0:T(8,128)(2,1)S(1)}, u32[]{:S(2)}, u32[]{:S(2)}) collective-permute-start(bf16[16,5504]{1,0:T(8,128)(2,1)S(1)} %get-tuple-element.196), channel_id=1, source_target_pairs={{0,1},{1,0},{2,3},{3,2},{4,5},{5,4},{6,7},{7,6},{8,9},{9,8},{10,11... | collective-permute-start | bytes 528392 | tf_op jit(solution)/shard_map/ppermute | solution.py:59
  164.5 7.2 %collective-permute-start.40 = (bf16[16,5504]{1,0:T(8,128)(2,1)S(1)}, bf16[16,5504]{1,0:T(8,128)(2,1)S(1)}, u32[]{:S(2)}, u32[]{:S(2)}) collective-permute-start(bf16[16,5504]{1,0:T(8,128)(2,1)S(1)} %add_convert_fusion), channel_id=1, source_target_pairs={{0,4},{1,5},{2,6},{3,7},{4,0},{5,1},{6,2},{7,3},{8,12},{9,13},{10,... | collective-permute-start | bytes 528392 | tf_op jit(solution)/shard_map/ppermute | solution.py:59
  (5 other events, 17.2 us)

commit v3 on v1

--- a/solution.py
+++ b/solution.py
@@ -262,7 +262,7 @@
 
 
 def combine(box, notes, n, own, back, picked):
-    sums = [total_of(own)] + [ref[...] for ref in back]
+    sums = [total_of(own)] + [ref[...].astype(BF) for ref in back]
     pick_rows(box, slots_in(notes, n), sums, n, picked)
     return mix_in(notes, n) * picked[...]
 
@@ -578,7 +578,8 @@
     fin = fin_back + own_home(own_fin, 0)
     cross_grad = back(cross_g, cross_kept0)[0]
     own_grad = back(own_g, own_kept0, after=cross_grad[:1] + tuple(fin))[0]
-    got = home(sums(cross_grad), 0) + own_home(own_grad, 0)
+    got, _ = give_back(cross_grad, own_grad, 0)
+    got[: experts - 1] = [sums_home.astype(F32) for sums_home in got[: experts - 1]]
     (g0,) = call(
         bind(last_kernel, box, experts),
         [rows_of(n)],

time: 170 us -> 170 us (level)
  starting transfers between devices: 43 us -> 48.5 us
  waiting for transfers between devices: 97.7 us -> 92.4 us
    ppermute x43, starting transfers between devices: 43 us -> 48.5 us  [shift(): return lax.ppermute(value, ('section', 'expert'), pairs)]
    ppermute x43, waiting for transfers between devices: 97.7 us -> 92.4 us  [shift(): return lax.ppermute(value, ('section', 'expert'), pairs)]
  transfers between devices with their start and end apart: 43 -> 43, of which waited for: 25 -> 25; matrix products, arithmetic and copies ran while one was open for 2% -> 1% of each run, Pallas kernels for 9% -> 9%
where the time goes in v3:
time: 170 us
  waiting for transfers between devices  92.4 us (54%)
  starting transfers between devices  48.5 us (29%)
  Pallas kernels  23 us (14%)
  local copies, waits for them, and re-layouts  4.53 us (3%)
    ppermute x43, waiting for transfers between devices, shift(): return lax.ppermute(value, ('section', 'expert'), pairs)  92.4 us
    ppermute x43, starting transfers between devices, shift(): return lax.ppermute(value, ('section', 'expert'), pairs)  48.5 us
    pallas_call x15, Pallas kernels, call(): pl.pallas_call(reading, out_shape=list(outs), in_specs=[vmem] * read + [p...  23 us
  transfers between devices with their start and end apart: 43, of which 25 were waited for; matrix products, arithmetic and copies ran while one was open for 1% of the time, Pallas kernels for 9%

profile of v3, /device:TPU:0, one launch (start us, length us, event | category | flops | bytes accessed | tf_op | source)
XLA Modules:
  0.0 169.8 jit_solution(16358026608234878201)
XLA Ops:
  0.6 1.2 slice.40
  1.8 1.1 slice.41
  3.1 3.0 %collective-permute-start = (bf16[336,2560]{1,0:T(8,128)(2,1)S(1)}, bf16[336,2560]{1,0:T(8,128)(2,1)S(1)}, u32[]{:S(2)}, u32[]{:S(2)}) collective-permute-start(bf16[336,2560]{1,0:T(8,128)(2,1)S(1)} %pad_maximum_fusion.refs_5_.refs_0_), channel_id=1, source_target_pairs={{0,1},{1,0},{2,3},{3,2},{4,5},{5,4},{6,7},{7,6},{8,9},{9,8},{10,11... | collective-permute-start | bytes 5160968 | tf_op jit(solution)/shard_map/ppermute | solution.py:59
  6.1 1.0 slice.42
  7.2 1.1 slice.43
  8.4 1.6 collective-permute-start.1
  10.9 2.6 %collective-permute-start.2 = (bf16[32,5504]{1,0:T(8,128)(2,1)S(1)}, bf16[32,5504]{1,0:T(8,128)(2,1)S(1)}, u32[]{:S(2)}, u32[]{:S(2)}) collective-permute-start(bf16[32,5504]{1,0:T(8,128)(2,1)S(1)} %get-tuple-element.100), channel_id=1, source_target_pairs={{0,4},{1,5},{2,6},{3,7},{4,0},{5,1},{6,2},{7,3},{8,12},{9,13},{10,... | collective-permute-start | bytes 1056776 | tf_op jit(solution)/shard_map/ppermute | solution.py:59
  14.5 32.9 %collective-permute-done.4.refs_6_ = bf16[16,5504]{1,0:T(8,128)(2,1)S(1)} collective-permute-done((bf16[16,5504]{1,0:T(8,128)(2,1)S(1)}, bf16[16,5504]{1,0:T(8,128)(2,1)S(1)}, u32[]{:S(2)}, u32[]{:S(2)}) %collective-permute-start.4) | collective-permute-done | bytes 176160 | tf_op jit(solution)/shard_map/ppermute | solution.py:59
  49.3 1.6 collective-permute-start.5
  50.9 2.9 %collective-permute-done.6.refs_6_ = bf16[16,5504]{1,0:T(8,128)(2,1)S(1)} collective-permute-done((bf16[16,5504]{1,0:T(8,128)(2,1)S(1)}, bf16[16,5504]{1,0:T(8,128)(2,1)S(1)}, u32[]{:S(2)}, u32[]{:S(2)}) %collective-permute-start.6) | collective-permute-done | bytes 176160 | tf_op jit(solution)/shard_map/ppermute | solution.py:59
  54.8 2.5 %shard_map.96 = (bf16[16,5504]{1,0:T(8,128)(2,1)S(1)}, bf16[16,5504]{1,0:T(8,128)(2,1)S(1)}, bf16[16,5504]{1,0:T(8,128)(2,1)S(1)}, f32[96,224]{1,0:T(8,128)S(1)}...) custom-call(bf16[336,2560]{1,0:T(8,128)(2,1)S(1)} %pad_maximum_fusion.refs_5_.refs_0_, ...), custom_call_target="tpu_custom_call" | custom-call | flops 566231040 | bytes 7249920 | tf_op jit(solution)/shard_map/pallas_call | solution.py:71
  57.2 1.6 collective-permute-start.8
  58.9 1.1 collective-permute-start.9
  61.3 2.5 %shard_map.97 = (bf16[16,5504]{1,0:T(8,128)(2,1)S(1)}, bf16[16,5504]{1,0:T(8,128)(2,1)S(1)}, bf16[16,5504]{1,0:T(8,128)(2,1)S(1)}, f32[96,224]{1,0:T(8,128)S(1)}...) custom-call(bf16[336,2560]{1,0:T(8,128)(2,1)S(1)} %pad_maximum_fusion.refs_5_.refs_0_, ...), custom_call_target="tpu_custom_call" | custom-call | flops 566231040 | bytes 7249920 | tf_op jit(solution)/shard_map/pallas_call | solution.py:71
  64.5 1.7 %collective-permute-done.9 = bf16[16,5504]{1,0:T(8,128)(2,1)S(1)} collective-permute-done((bf16[16,5504]{1,0:T(8,128)(2,1)S(1)}, bf16[16,5504]{1,0:T(8,128)(2,1)S(1)}, u32[]{:S(2)}, u32[]{:S(2)}) %collective-permute-start.9) | collective-permute-done | bytes 176160 | tf_op jit(solution)/shard_map/ppermute | solution.py:59
  66.3 1.5 collective-permute-start.10
  67.8 2.5 %collective-permute-done.12.refs_6_ = bf16[32,5504]{1,0:T(8,128)(2,1)S(1)} collective-permute-done((bf16[32,5504]{1,0:T(8,128)(2,1)S(1)}, bf16[32,5504]{1,0:T(8,128)(2,1)S(1)}, u32[]{:S(2)}, u32[]{:S(2)}) %collective-permute-start.12) | collective-permute-done | bytes 352288 | tf_op jit(solution)/shard_map/ppermute | solution.py:59
  70.3 1.9 %collective-permute-start.14 = (bf16[16,5504]{1,0:T(8,128)(2,1)S(1)}, bf16[16,5504]{1,0:T(8,128)(2,1)S(1)}, u32[]{:S(2)}, u32[]{:S(2)}) collective-permute-start(bf16[16,5504]{1,0:T(8,128)(2,1)S(1)} %get-tuple-element.128), channel_id=1, source_target_pairs={{0,9},{1,8},{2,11},{3,10},{4,13},{5,12},{6,15},{7,14},{8,17},{9,16... | collective-permute-start | bytes 528392 | tf_op jit(solution)/shard_map/ppermute | solution.py:59
  72.3 6.4 %collective-permute-done.10.refs_4_ = bf16[16,5504]{1,0:T(8,128)(2,1)S(1)} collective-permute-done((bf16[16,5504]{1,0:T(8,128)(2,1)S(1)}, bf16[16,5504]{1,0:T(8,128)(2,1)S(1)}, u32[]{:S(2)}, u32[]{:S(2)}) %collective-permute-start.10) | collective-permute-done | bytes 176160 | tf_op jit(solution)/shard_map/ppermute | solution.py:59
  78.7 1.2 collective-permute-done.13.refs_5_
  79.8 1.1 collective-permute-done.15.refs_7_
  81.9 1.9 %collective-permute-start.16 = (bf16[16,5504]{1,0:T(8,128)(2,1)S(1)}, bf16[16,5504]{1,0:T(8,128)(2,1)S(1)}, u32[]{:S(2)}, u32[]{:S(2)}) collective-permute-start(bf16[16,5504]{1,0:T(8,128)(2,1)S(1)} %get-tuple-element.138), channel_id=1, source_target_pairs={{0,4},{1,5},{2,6},{3,7},{4,0},{5,1},{6,2},{7,3},{8,12},{9,13},{10,... | collective-permute-start | bytes 528392 | tf_op jit(solution)/shard_map/ppermute | solution.py:59
  84.4 2.5 %collective-permute-start.17 = (bf16[16,5504]{1,0:T(8,128)(2,1)S(1)}, bf16[16,5504]{1,0:T(8,128)(2,1)S(1)}, u32[]{:S(2)}, u32[]{:S(2)}) collective-permute-start(bf16[16,5504]{1,0:T(8,128)(2,1)S(1)} %get-tuple-element.139.refs_9_), channel_id=1, source_target_pairs={{0,2},{1,3},{2,0},{3,1},{4,6},{5,7},{6,4},{7,5},{8,10},{9,11},{10,... | collective-permute-start | bytes 528392 | tf_op jit(solution)/shard_map/ppermute | solution.py:59
  86.9 6.7 %collective-permute-done.16.refs_9_ = bf16[16,5504]{1,0:T(8,128)(2,1)S(1)} collective-permute-done((bf16[16,5504]{1,0:T(8,128)(2,1)S(1)}, bf16[16,5504]{1,0:T(8,128)(2,1)S(1)}, u32[]{:S(2)}, u32[]{:S(2)}) %collective-permute-start.16) | collective-permute-done | bytes 176160 | tf_op jit(solution)/shard_map/ppermute | solution.py:59
  97.1 2.6 %shard_map.101 = (bf16[16,5504]{1,0:T(8,128)(2,1)S(1)}, bf16[16,5504]{1,0:T(8,128)(2,1)S(1)}, bf16[16,5504]{1,0:T(8,128)(2,1)S(1)}, f32[96,224]{1,0:T(8,128)S(1)...) custom-call(bf16[336,2560]{1,0:T(8,128)(2,1)S(1)} %pad_maximum_fusion.refs_5_.refs_0_, ...), custom_call_target="tpu_custom_call" | custom-call | flops 566231040 | bytes 7397376 | tf_op jit(solution)/shard_map/pallas_call | solution.py:71
  100.8 2.6 %shard_map.102 = (bf16[16,5504]{1,0:T(8,128)(2,1)S(1)}, bf16[16,5504]{1,0:T(8,128)(2,1)S(1)}, bf16[16,5504]{1,0:T(8,128)(2,1)S(1)}, f32[96,224]{1,0:T(8,128)S(1)...) custom-call(bf16[336,2560]{1,0:T(8,128)(2,1)S(1)} %pad_maximum_fusion.refs_5_.refs_0_, ...), custom_call_target="tpu_custom_call" | custom-call | flops 566231040 | bytes 7397376 | tf_op jit(solution)/shard_map/pallas_call | solution.py:71
  103.4 1.0 collective-permute-start.22
  106.4 1.1 collective-permute-start.25
  108.4 2.3 %collective-permute-done.22 = bf16[16,5504]{1,0:T(8,128)(2,1)S(1)} collective-permute-done((bf16[16,5504]{1,0:T(8,128)(2,1)S(1)}, bf16[16,5504]{1,0:T(8,128)(2,1)S(1)}, u32[]{:S(2)}, u32[]{:S(2)}) %collective-permute-start.22) | collective-permute-done | bytes 176160 | tf_op jit(solution)/shard_map/ppermute | solution.py:59
  111.4 4.5 %collective-permute-start.30 = (bf16[16,5504]{1,0:T(8,128)(2,1)S(1)}, bf16[16,5504]{1,0:T(8,128)(2,1)S(1)}, u32[]{:S(2)}, u32[]{:S(2)}) collective-permute-start(bf16[16,5504]{1,0:T(8,128)(2,1)S(1)} %get-tuple-element.172.refs_11_), channel_id=1, source_target_pairs={{0,26},{1,27},{2,24},{3,25},{4,30},{5,31},{6,28},{7,29},{8,2},{9,3... | collective-permute-start | bytes 528392 | tf_op jit(solution)/shard_map/ppermute | solution.py:59
  116.3 6.3 %collective-permute-done.24.refs_2_ = bf16[16,5504]{1,0:T(8,128)(2,1)S(1)} collective-permute-done((bf16[16,5504]{1,0:T(8,128)(2,1)S(1)}, bf16[16,5504]{1,0:T(8,128)(2,1)S(1)}, u32[]{:S(2)}, u32[]{:S(2)}) %collective-permute-start.24) | collective-permute-done | bytes 176160 | tf_op jit(solution)/shard_map/ppermute | solution.py:59
  122.6 2.3 %collective-permute-done.32.refs_5_ = bf16[16,5504]{1,0:T(8,128)(2,1)S(1)} collective-permute-done((bf16[16,5504]{1,0:T(8,128)(2,1)S(1)}, bf16[16,5504]{1,0:T(8,128)(2,1)S(1)}, u32[]{:S(2)}, u32[]{:S(2)}) %collective-permute-start.32) | collective-permute-done | bytes 176160 | tf_op jit(solution)/shard_map/ppermute | solution.py:59
  125.9 1.1 collective-permute-start.35
  127.0 1.4 collective-permute-start.34
  128.4 8.3 %collective-permute-done.33.refs_9_ = bf16[16,5504]{1,0:T(8,128)(2,1)S(1)} collective-permute-done((bf16[16,5504]{1,0:T(8,128)(2,1)S(1)}, bf16[16,5504]{1,0:T(8,128)(2,1)S(1)}, u32[]{:S(2)}, u32[]{:S(2)}) %collective-permute-start.33) | collective-permute-done | bytes 176160 | tf_op jit(solution)/shard_map/ppermute | solution.py:59
  137.7 1.0 collective-permute-start.37
  139.6 2.1 %collective-permute-start.28 = (bf16[16,5504]{1,0:T(8,128)(2,1)S(1)}, bf16[16,5504]{1,0:T(8,128)(2,1)S(1)}, u32[]{:S(2)}, u32[]{:S(2)}) collective-permute-start(bf16[16,5504]{1,0:T(8,128)(2,1)S(1)} %get-tuple-element.164), channel_id=1, source_target_pairs={{0,2},{1,3},{2,0},{3,1},{4,6},{5,7},{6,4},{7,5},{8,10},{9,11},{10,... | collective-permute-start | bytes 528392 | tf_op jit(solution)/shard_map/ppermute | solution.py:59
  143.1 1.3 collective-permute-done.37.refs_10_
  144.4 5.0 %collective-permute-done.36.refs_8_ = bf16[16,5504]{1,0:T(8,128)(2,1)S(1)} collective-permute-done((bf16[16,5504]{1,0:T(8,128)(2,1)S(1)}, bf16[16,5504]{1,0:T(8,128)(2,1)S(1)}, u32[]{:S(2)}, u32[]{:S(2)}) %collective-permute-start.36) | collective-permute-done | bytes 176160 | tf_op jit(solution)/shard_map/ppermute | solution.py:59
  149.4 2.0 %shard_map.107 = (bf16[16,5504]{1,0:T(8,128)(2,1)S(1)}, bf16[16,5504]{1,0:T(8,128)(2,1)S(1)}, bf16[16,5504]{1,0:T(8,128)(2,1)S(1)}) custom-call(bf16[336,2560]{1,0:T(8,128)(2,1)S(1)} %pad_maximum_fusion.refs_5_.refs_0_, bf16[336,2560]{1,0:T(8,128)(2,1)S(1)} %collective-permute-done.refs_1_, bf16[240,2560]{1,0:T(8,128)(2,1)S(1)} %pad_maximum_fusion.1.refs_6_.refs_2_, ...), custom_call_target="tpu_custom_call" | custom-call | flops 566231040 | bytes 7249920 | tf_op jit(solution)/shard_map/pallas_call | solution.py:71
  152.1 1.5 collective-permute-done.28.refs_3_.refs_13_
  153.7 2.0 %shard_map.108 = (bf16[16,5504]{1,0:T(8,128)(2,1)S(1)}, bf16[16,5504]{1,0:T(8,128)(2,1)S(1)}, bf16[16,5504]{1,0:T(8,128)(2,1)S(1)}) custom-call(bf16[336,2560]{1,0:T(8,128)(2,1)S(1)} %pad_maximum_fusion.refs_5_.refs_0_, bf16[336,2560]{1,0:T(8,128)(2,1)S(1)} %collective-permute-done.refs_1_, bf16[240,2560]{1,0:T(8,128)(2,1)S(1)} %pad_maximum_fusion.1.refs_6_.refs_2_, ...), custom_call_target="tpu_custom_call" | custom-call | flops 566231040 | bytes 7249920 | tf_op jit(solution)/shard_map/pallas_call | solution.py:71
  155.7 1.2 collective-permute-done.39
  158.1 2.1 %collective-permute-start.41 = (bf16[16,5504]{1,0:T(8,128)(2,1)S(1)}, bf16[16,5504]{1,0:T(8,128)(2,1)S(1)}, u32[]{:S(2)}, u32[]{:S(2)}) collective-permute-start(bf16[16,5504]{1,0:T(8,128)(2,1)S(1)} %get-tuple-element.195), channel_id=1, source_target_pairs={{0,2},{1,3},{2,0},{3,1},{4,6},{5,7},{6,4},{7,5},{8,10},{9,11},{10,... | collective-permute-start | bytes 528392 | tf_op jit(solution)/shard_map/ppermute | solution.py:59
  160.2 4.9 %collective-permute-start.42 = (bf16[16,5504]{1,0:T(8,128)(2,1)S(1)}, bf16[16,5504]{1,0:T(8,128)(2,1)S(1)}, u32[]{:S(2)}, u32[]{:S(2)}) collective-permute-start(bf16[16,5504]{1,0:T(8,128)(2,1)S(1)} %get-tuple-element.196), channel_id=1, source_target_pairs={{0,1},{1,0},{2,3},{3,2},{4,5},{5,4},{6,7},{7,6},{8,9},{9,8},{10,11... | collective-permute-start | bytes 528392 | tf_op jit(solution)/shard_map/ppermute | solution.py:59
  165.1 1.1 shard_map.105
  166.2 2.3 %collective-permute-done.42.refs_6_ = bf16[16,5504]{1,0:T(8,128)(2,1)S(1)} collective-permute-done((bf16[16,5504]{1,0:T(8,128)(2,1)S(1)}, bf16[16,5504]{1,0:T(8,128)(2,1)S(1)}, u32[]{:S(2)}, u32[]{:S(2)}) %collective-permute-start.42) | collective-permute-done | bytes 176160 | tf_op jit(solution)/shard_map/ppermute | solution.py:59
  168.5 1.3 shard_map.109
  (80 shorter events, 23.3 us)
Async XLA Ops:
  3.1 45.2 %collective-permute-start = (bf16[336,2560]{1,0:T(8,128)(2,1)S(1)}, bf16[336,2560]{1,0:T(8,128)(2,1)S(1)}, u32[]{:S(2)}, u32[]{:S(2)}) collective-permute-start(bf16[336,2560]{1,0:T(8,128)(2,1)S(1)} %pad_maximum_fusion.refs_5_.refs_0_), channel_id=1, source_target_pairs={{0,1},{1,0},{2,3},{3,2},{4,5},{5,4},{6,7},{7,6},{8,9},{9,8},{10,11... | collective-permute-start | bytes 5160968 | tf_op jit(solution)/shard_map/ppermute | solution.py:59
  7.2 2.9 %copy-start = (bf16[1,64,2560]{2,1,0:T(8,128)(2,1)S(1)}, bf16[1,64,2560]{2,1,0:T(8,128)(2,1)}, u32[]{:S(2)}) copy-start(bf16[1,64,2560]{2,1,0:T(8,128)(2,1)} %param.15) | copy-start | bytes 983044
  7.2 2.9 %copy-start.1 = (bf16[1,64,2560]{2,1,0:T(8,128)(2,1)S(1)}, bf16[1,64,2560]{2,1,0:T(8,128)(2,1)}, u32[]{:S(2)}) copy-start(bf16[1,64,2560]{2,1,0:T(8,128)(2,1)} %param.8) | copy-start | bytes 983044
  7.2 2.9 %copy-start.2 = (f32[1,2560]{1,0:T(1,128)S(1)}, f32[1,2560]{1,0:T(1,128)}, u32[]{:S(2)}) copy-start(f32[1,2560]{1,0:T(1,128)} %refs_3_.3) | copy-start | bytes 30724
  7.2 2.9 %copy-start.3 = (s32[1,2,64,1]{2,3,1,0:T(1,128)S(1)}, s32[1,2,64,1]{2,3,1,0:T(1,128)}, u32[]{:S(2)}) copy-start(s32[1,2,64,1]{2,3,1,0:T(1,128)} %param.13) | copy-start | bytes 1540
  7.2 2.8 %copy-start.4 = (f32[1,2,64,1]{2,3,1,0:T(1,128)S(1)}, f32[1,2,64,1]{2,3,1,0:T(1,128)}, u32[]{:S(2)}) copy-start(f32[1,2,64,1]{2,3,1,0:T(1,128)} %param.14) | copy-start | bytes 1540
  8.4 39.9 %collective-permute-start.1 = (bf16[240,2560]{1,0:T(8,128)(2,1)S(1)}, bf16[240,2560]{1,0:T(8,128)(2,1)S(1)}, u32[]{:S(2)}, u32[]{:S(2)}) collective-permute-start(bf16[240,2560]{1,0:T(8,128)(2,1)S(1)} %pad_maximum_fusion.1.refs_6_.refs_2_), channel_id=1, source_target_pairs={{0,2},{1,3},{2,0},{3,1},{4,6},{5,7},{6,4},{7,5},{8,10},{9,11},{10,... | collective-permute-start | bytes 3686408 | tf_op jit(solution)/shard_map/ppermute | solution.py:59
  10.9 37.4 %collective-permute-start.2 = (bf16[32,5504]{1,0:T(8,128)(2,1)S(1)}, bf16[32,5504]{1,0:T(8,128)(2,1)S(1)}, u32[]{:S(2)}, u32[]{:S(2)}) collective-permute-start(bf16[32,5504]{1,0:T(8,128)(2,1)S(1)} %get-tuple-element.100), channel_id=1, source_target_pairs={{0,4},{1,5},{2,6},{3,7},{4,0},{5,1},{6,2},{7,3},{8,12},{9,13},{10,... | collective-permute-start | bytes 1056776 | tf_op jit(solution)/shard_map/ppermute | solution.py:59
  13.6 33.9 %collective-permute-start.4 = (bf16[16,5504]{1,0:T(8,128)(2,1)S(1)}, bf16[16,5504]{1,0:T(8,128)(2,1)S(1)}, u32[]{:S(2)}, u32[]{:S(2)}) collective-permute-start(bf16[16,5504]{1,0:T(8,128)(2,1)S(1)} %get-tuple-element.121.refs_5_), channel_id=1, source_target_pairs={{0,1},{1,0},{2,3},{3,2},{4,5},{5,4},{6,7},{7,6},{8,9},{9,8},{10,11... | collective-permute-start | bytes 528392 | tf_op jit(solution)/shard_map/ppermute | solution.py:59
  14.1 34.2 %collective-permute-start.3 = (bf16[16,5504]{1,0:T(8,128)(2,1)S(1)}, bf16[16,5504]{1,0:T(8,128)(2,1)S(1)}, u32[]{:S(2)}, u32[]{:S(2)}) collective-permute-start(bf16[16,5504]{1,0:T(8,128)(2,1)S(1)} %get-tuple-element.121.refs_5_), channel_id=1, source_target_pairs={{0,2},{1,3},{2,0},{3,1},{4,6},{5,7},{6,4},{7,5},{8,10},{9,11},{10,... | collective-permute-start | bytes 528392 | tf_op jit(solution)/shard_map/ppermute | solution.py:59
  48.3 5.5 %collective-permute-start.6 = (bf16[16,5504]{1,0:T(8,128)(2,1)S(1)}, bf16[16,5504]{1,0:T(8,128)(2,1)S(1)}, u32[]{:S(2)}, u32[]{:S(2)}) collective-permute-start(bf16[16,5504]{1,0:T(8,128)(2,1)S(1)} %get-tuple-element.109.refs_5_), channel_id=1, source_target_pairs={{0,1},{1,0},{2,3},{3,2},{4,5},{5,4},{6,7},{7,6},{8,9},{9,8},{10,11... | collective-permute-start | bytes 528392 | tf_op jit(solution)/shard_map/ppermute | solution.py:59
  49.3 5.5 %collective-permute-start.5 = (bf16[16,5504]{1,0:T(8,128)(2,1)S(1)}, bf16[16,5504]{1,0:T(8,128)(2,1)S(1)}, u32[]{:S(2)}, u32[]{:S(2)}) collective-permute-start(bf16[16,5504]{1,0:T(8,128)(2,1)S(1)} %get-tuple-element.109.refs_5_), channel_id=1, source_target_pairs={{0,2},{1,3},{2,0},{3,1},{4,6},{5,7},{6,4},{7,5},{8,10},{9,11},{10,... | collective-permute-start | bytes 528392 | tf_op jit(solution)/shard_map/ppermute | solution.py:59
  57.2 7.3 %collective-permute-start.8 = (bf16[16,5504]{1,0:T(8,128)(2,1)S(1)}, bf16[16,5504]{1,0:T(8,128)(2,1)S(1)}, u32[]{:S(2)}, u32[]{:S(2)}) collective-permute-start(bf16[16,5504]{1,0:T(8,128)(2,1)S(1)} %get-tuple-element.118.refs_7_), channel_id=1, source_target_pairs={{0,2},{1,3},{2,0},{3,1},{4,6},{5,7},{6,4},{7,5},{8,10},{9,11},{10,... | collective-permute-start | bytes 528392 | tf_op jit(solution)/shard_map/ppermute | solution.py:59
  58.9 7.4 %collective-permute-start.9 = (bf16[16,5504]{1,0:T(8,128)(2,1)S(1)}, bf16[16,5504]{1,0:T(8,128)(2,1)S(1)}, u32[]{:S(2)}, u32[]{:S(2)}) collective-permute-start(bf16[16,5504]{1,0:T(8,128)(2,1)S(1)} %get-tuple-element.119), channel_id=1, source_target_pairs={{0,1},{1,0},{2,3},{3,2},{4,5},{5,4},{6,7},{7,6},{8,9},{9,8},{10,11... | collective-permute-start | bytes 528392 | tf_op jit(solution)/shard_map/ppermute | solution.py:59
  60.0 10.3 %collective-permute-start.12 = (bf16[32,5504]{1,0:T(8,128)(2,1)S(1)}, bf16[32,5504]{1,0:T(8,128)(2,1)S(1)}, u32[]{:S(2)}, u32[]{:S(2)}) collective-permute-start(bf16[32,5504]{1,0:T(8,128)(2,1)S(1)} %pad_maximum_fusion.2.refs_5_), channel_id=1, source_target_pairs={{0,1},{1,0},{2,3},{3,2},{4,5},{5,4},{6,7},{7,6},{8,9},{9,8},{10,11... | collective-permute-start | bytes 1056776 | tf_op jit(solution)/shard_map/ppermute | solution.py:59
  60.9 9.4 %collective-permute-start.11 = (bf16[32,5504]{1,0:T(8,128)(2,1)S(1)}, bf16[32,5504]{1,0:T(8,128)(2,1)S(1)}, u32[]{:S(2)}, u32[]{:S(2)}) collective-permute-start(bf16[32,5504]{1,0:T(8,128)(2,1)S(1)} %pad_maximum_fusion.2.refs_5_), channel_id=1, source_target_pairs={{0,2},{1,3},{2,0},{3,1},{4,6},{5,7},{6,4},{7,5},{8,10},{9,11},{10,... | collective-permute-start | bytes 1056776 | tf_op jit(solution)/shard_map/ppermute | solution.py:59
  61.3 17.3 %collective-permute-start.7 = (bf16[80,2560]{1,0:T(8,128)(2,1)S(1)}, bf16[80,2560]{1,0:T(8,128)(2,1)S(1)}, u32[]{:S(2)}, u32[]{:S(2)}) collective-permute-start(bf16[80,2560]{1,0:T(8,128)(2,1)S(1)} %get-tuple-element.115), channel_id=1, source_target_pairs={{0,8},{1,9},{2,10},{3,11},{4,12},{5,13},{6,14},{7,15},{8,16},{9,17... | collective-permute-start | bytes 1228808 | tf_op jit(solution)/shard_map/ppermute | solution.py:59
  66.3 12.3 %collective-permute-start.10 = (bf16[16,5504]{1,0:T(8,128)(2,1)S(1)}, bf16[16,5504]{1,0:T(8,128)(2,1)S(1)}, u32[]{:S(2)}, u32[]{:S(2)}) collective-permute-start(bf16[16,5504]{1,0:T(8,128)(2,1)S(1)} %add_convert_fusion.3), channel_id=1, source_target_pairs={{0,12},{1,13},{2,14},{3,15},{4,8},{5,9},{6,10},{7,11},{8,20},{9,21... | collective-permute-start | bytes 528392 | tf_op jit(solution)/shard_map/ppermute | solution.py:59
  70.3 9.5 %collective-permute-start.13 = (bf16[16,5504]{1,0:T(8,128)(2,1)S(1)}, bf16[16,5504]{1,0:T(8,128)(2,1)S(1)}, u32[]{:S(2)}, u32[]{:S(2)}) collective-permute-start(bf16[16,5504]{1,0:T(8,128)(2,1)S(1)} %get-tuple-element.127), channel_id=1, source_target_pairs={{0,10},{1,11},{2,8},{3,9},{4,14},{5,15},{6,12},{7,13},{8,18},{9,19... | collective-permute-start | bytes 528392 | tf_op jit(solution)/shard_map/ppermute | solution.py:59
  70.3 9.5 %collective-permute-start.14 = (bf16[16,5504]{1,0:T(8,128)(2,1)S(1)}, bf16[16,5504]{1,0:T(8,128)(2,1)S(1)}, u32[]{:S(2)}, u32[]{:S(2)}) collective-permute-start(bf16[16,5504]{1,0:T(8,128)(2,1)S(1)} %get-tuple-element.128), channel_id=1, source_target_pairs={{0,9},{1,8},{2,11},{3,10},{4,13},{5,12},{6,15},{7,14},{8,17},{9,16... | collective-permute-start | bytes 528392 | tf_op jit(solution)/shard_map/ppermute | solution.py:59
  72.3 8.7 %collective-permute-start.15 = (bf16[16,5504]{1,0:T(8,128)(2,1)S(1)}, bf16[16,5504]{1,0:T(8,128)(2,1)S(1)}, u32[]{:S(2)}, u32[]{:S(2)}) collective-permute-start(bf16[16,5504]{1,0:T(8,128)(2,1)S(1)} %get-tuple-element.129), channel_id=1, source_target_pairs={{0,8},{1,9},{2,10},{3,11},{4,12},{5,13},{6,14},{7,15},{8,16},{9,17... | collective-permute-start | bytes 528392 | tf_op jit(solution)/shard_map/ppermute | solution.py:59
  81.9 12.5 %collective-permute-start.19 = (bf16[144,2560]{1,0:T(8,128)(2,1)S(1)}, bf16[144,2560]{1,0:T(8,128)(2,1)S(1)}, u32[]{:S(2)}, u32[]{:S(2)}) collective-permute-start(bf16[144,2560]{1,0:T(8,128)(2,1)S(1)} %get-tuple-element.140), channel_id=1, source_target_pairs={{0,24},{1,25},{2,26},{3,27},{4,28},{5,29},{6,30},{7,31},{8,0},{9,1... | collective-permute-start | bytes 2211848 | tf_op jit(solution)/shard_map/ppermute | solution.py:59
  81.9 11.7 %collective-permute-start.16 = (bf16[16,5504]{1,0:T(8,128)(2,1)S(1)}, bf16[16,5504]{1,0:T(8,128)(2,1)S(1)}, u32[]{:S(2)}, u32[]{:S(2)}) collective-permute-start(bf16[16,5504]{1,0:T(8,128)(2,1)S(1)} %get-tuple-element.138), channel_id=1, source_target_pairs={{0,4},{1,5},{2,6},{3,7},{4,0},{5,1},{6,2},{7,3},{8,12},{9,13},{10,... | collective-permute-start | bytes 528392 | tf_op jit(solution)/shard_map/ppermute | solution.py:59
  83.8 9.7 %collective-permute-start.18 = (bf16[16,5504]{1,0:T(8,128)(2,1)S(1)}, bf16[16,5504]{1,0:T(8,128)(2,1)S(1)}, u32[]{:S(2)}, u32[]{:S(2)}) collective-permute-start(bf16[16,5504]{1,0:T(8,128)(2,1)S(1)} %get-tuple-element.139.refs_9_), channel_id=1, source_target_pairs={{0,1},{1,0},{2,3},{3,2},{4,5},{5,4},{6,7},{7,6},{8,9},{9,8},{10,11... | collective-permute-start | bytes 528392 | tf_op jit(solution)/shard_map/ppermute | solution.py:59
  84.4 10.0 %collective-permute-start.17 = (bf16[16,5504]{1,0:T(8,128)(2,1)S(1)}, bf16[16,5504]{1,0:T(8,128)(2,1)S(1)}, u32[]{:S(2)}, u32[]{:S(2)}) collective-permute-start(bf16[16,5504]{1,0:T(8,128)(2,1)S(1)} %get-tuple-element.139.refs_9_), channel_id=1, source_target_pairs={{0,2},{1,3},{2,0},{3,1},{4,6},{5,7},{6,4},{7,5},{8,10},{9,11},{10,... | collective-permute-start | bytes 528392 | tf_op jit(solution)/shard_map/ppermute | solution.py:59
  94.3 5.5 %collective-permute-start.21 = (bf16[16,5504]{1,0:T(8,128)(2,1)S(1)}, bf16[16,5504]{1,0:T(8,128)(2,1)S(1)}, u32[]{:S(2)}, u32[]{:S(2)}) collective-permute-start(bf16[16,5504]{1,0:T(8,128)(2,1)S(1)} %collective-permute-done.16.refs_9_), channel_id=1, source_target_pairs={{0,1},{1,0},{2,3},{3,2},{4,5},{5,4},{6,7},{7,6},{8,9},{9,8},{10,11... | collective-permute-start | bytes 528392 | tf_op jit(solution)/shard_map/ppermute | solution.py:59
  95.3 5.5 %collective-permute-start.20 = (bf16[16,5504]{1,0:T(8,128)(2,1)S(1)}, bf16[16,5504]{1,0:T(8,128)(2,1)S(1)}, u32[]{:S(2)}, u32[]{:S(2)}) collective-permute-start(bf16[16,5504]{1,0:T(8,128)(2,1)S(1)} %collective-permute-done.16.refs_9_), channel_id=1, source_target_pairs={{0,2},{1,3},{2,0},{3,1},{4,6},{5,7},{6,4},{7,5},{8,10},{9,11},{10,... | collective-permute-start | bytes 528392 | tf_op jit(solution)/shard_map/ppermute | solution.py:59
  103.4 7.3 %collective-permute-start.22 = (bf16[16,5504]{1,0:T(8,128)(2,1)S(1)}, bf16[16,5504]{1,0:T(8,128)(2,1)S(1)}, u32[]{:S(2)}, u32[]{:S(2)}) collective-permute-start(bf16[16,5504]{1,0:T(8,128)(2,1)S(1)} %get-tuple-element.150), channel_id=1, source_target_pairs={{0,2},{1,3},{2,0},{3,1},{4,6},{5,7},{6,4},{7,5},{8,10},{9,11},{10,... | collective-permute-start | bytes 528392 | tf_op jit(solution)/shard_map/ppermute | solution.py:59
  104.5 6.7 %collective-permute-start.23 = (bf16[16,5504]{1,0:T(8,128)(2,1)S(1)}, bf16[16,5504]{1,0:T(8,128)(2,1)S(1)}, u32[]{:S(2)}, u32[]{:S(2)}) collective-permute-start(bf16[16,5504]{1,0:T(8,128)(2,1)S(1)} %get-tuple-element.151), channel_id=1, source_target_pairs={{0,1},{1,0},{2,3},{3,2},{4,5},{5,4},{6,7},{7,6},{8,9},{9,8},{10,11... | collective-permute-start | bytes 528392 | tf_op jit(solution)/shard_map/ppermute | solution.py:59
  106.4 9.5 %collective-permute-start.25 = (bf16[16,5504]{1,0:T(8,128)(2,1)S(1)}, bf16[16,5504]{1,0:T(8,128)(2,1)S(1)}, u32[]{:S(2)}, u32[]{:S(2)}) collective-permute-start(bf16[16,5504]{1,0:T(8,128)(2,1)S(1)} %get-tuple-element.157), channel_id=1, source_target_pairs={{0,2},{1,3},{2,0},{3,1},{4,6},{5,7},{6,4},{7,5},{8,10},{9,11},{10,... | collective-permute-start | bytes 528392 | tf_op jit(solution)/shard_map/ppermute | solution.py:59
  107.4 8.8 %collective-permute-start.26 = (bf16[16,5504]{1,0:T(8,128)(2,1)S(1)}, bf16[16,5504]{1,0:T(8,128)(2,1)S(1)}, u32[]{:S(2)}, u32[]{:S(2)}) collective-permute-start(bf16[16,5504]{1,0:T(8,128)(2,1)S(1)} %get-tuple-element.158), channel_id=1, source_target_pairs={{0,1},{1,0},{2,3},{3,2},{4,5},{5,4},{6,7},{7,6},{8,9},{9,8},{10,11... | collective-permute-start | bytes 528392 | tf_op jit(solution)/shard_map/ppermute | solution.py:59
  111.3 11.3 %collective-permute-start.24 = (bf16[16,5504]{1,0:T(8,128)(2,1)S(1)}, bf16[16,5504]{1,0:T(8,128)(2,1)S(1)}, u32[]{:S(2)}, u32[]{:S(2)}) collective-permute-start(bf16[16,5504]{1,0:T(8,128)(2,1)S(1)} %add_convert_fusion.2), channel_id=1, source_target_pairs={{0,28},{1,29},{2,30},{3,31},{4,24},{5,25},{6,26},{7,27},{8,4},{9,5... | collective-permute-start | bytes 528392 | tf_op jit(solution)/shard_map/ppermute | solution.py:59
  111.4 11.2 %collective-permute-start.30 = (bf16[16,5504]{1,0:T(8,128)(2,1)S(1)}, bf16[16,5504]{1,0:T(8,128)(2,1)S(1)}, u32[]{:S(2)}, u32[]{:S(2)}) collective-permute-start(bf16[16,5504]{1,0:T(8,128)(2,1)S(1)} %get-tuple-element.172.refs_11_), channel_id=1, source_target_pairs={{0,26},{1,27},{2,24},{3,25},{4,30},{5,31},{6,28},{7,29},{8,2},{9,3... | collective-permute-start | bytes 528392 | tf_op jit(solution)/shard_map/ppermute | solution.py:59
  115.9 6.7 %collective-permute-start.31 = (bf16[16,5504]{1,0:T(8,128)(2,1)S(1)}, bf16[16,5504]{1,0:T(8,128)(2,1)S(1)}, u32[]{:S(2)}, u32[]{:S(2)}) collective-permute-start(bf16[16,5504]{1,0:T(8,128)(2,1)S(1)} %get-tuple-element.173), channel_id=1, source_target_pairs={{0,25},{1,24},{2,27},{3,26},{4,29},{5,28},{6,31},{7,30},{8,1},{9,0... | collective-permute-start | bytes 528392 | tf_op jit(solution)/shard_map/ppermute | solution.py:59
  115.9 8.9 %collective-permute-start.32 = (bf16[16,5504]{1,0:T(8,128)(2,1)S(1)}, bf16[16,5504]{1,0:T(8,128)(2,1)S(1)}, u32[]{:S(2)}, u32[]{:S(2)}) collective-permute-start(bf16[16,5504]{1,0:T(8,128)(2,1)S(1)} %get-tuple-element.174), channel_id=1, source_target_pairs={{0,24},{1,25},{2,26},{3,27},{4,28},{5,29},{6,30},{7,31},{8,0},{9,1... | collective-permute-start | bytes 528392 | tf_op jit(solution)/shard_map/ppermute | solution.py:59
  125.8 10.9 %collective-permute-start.33 = (bf16[16,5504]{1,0:T(8,128)(2,1)S(1)}, bf16[16,5504]{1,0:T(8,128)(2,1)S(1)}, u32[]{:S(2)}, u32[]{:S(2)}) collective-permute-start(bf16[16,5504]{1,0:T(8,128)(2,1)S(1)} %get-tuple-element.180), channel_id=1, source_target_pairs={{0,4},{1,5},{2,6},{3,7},{4,0},{5,1},{6,2},{7,3},{8,12},{9,13},{10,... | collective-permute-start | bytes 528392 | tf_op jit(solution)/shard_map/ppermute | solution.py:59
  125.9 10.9 %collective-permute-start.35 = (bf16[16,5504]{1,0:T(8,128)(2,1)S(1)}, bf16[16,5504]{1,0:T(8,128)(2,1)S(1)}, u32[]{:S(2)}, u32[]{:S(2)}) collective-permute-start(bf16[16,5504]{1,0:T(8,128)(2,1)S(1)} %get-tuple-element.181.refs_9_), channel_id=1, source_target_pairs={{0,1},{1,0},{2,3},{3,2},{4,5},{5,4},{6,7},{7,6},{8,9},{9,8},{10,11... | collective-permute-start | bytes 528392 | tf_op jit(solution)/shard_map/ppermute | solution.py:59
  127.0 10.8 %collective-permute-start.34 = (bf16[16,5504]{1,0:T(8,128)(2,1)S(1)}, bf16[16,5504]{1,0:T(8,128)(2,1)S(1)}, u32[]{:S(2)}, u32[]{:S(2)}) collective-permute-start(bf16[16,5504]{1,0:T(8,128)(2,1)S(1)} %get-tuple-element.181.refs_9_), channel_id=1, source_target_pairs={{0,2},{1,3},{2,0},{3,1},{4,6},{5,7},{6,4},{7,5},{8,10},{9,11},{10,... | collective-permute-start | bytes 528392 | tf_op jit(solution)/shard_map/ppermute | solution.py:59
  137.7 6.7 %collective-permute-start.37 = (bf16[16,5504]{1,0:T(8,128)(2,1)S(1)}, bf16[16,5504]{1,0:T(8,128)(2,1)S(1)}, u32[]{:S(2)}, u32[]{:S(2)}) collective-permute-start(bf16[16,5504]{1,0:T(8,128)(2,1)S(1)} %collective-permute-done.33.refs_9_), channel_id=1, source_target_pairs={{0,1},{1,0},{2,3},{3,2},{4,5},{5,4},{6,7},{7,6},{8,9},{9,8},{10,11... | collective-permute-start | bytes 528392 | tf_op jit(solution)/shard_map/ppermute | solution.py:59
  138.7 10.7 %collective-permute-start.36 = (bf16[16,5504]{1,0:T(8,128)(2,1)S(1)}, bf16[16,5504]{1,0:T(8,128)(2,1)S(1)}, u32[]{:S(2)}, u32[]{:S(2)}) collective-permute-start(bf16[16,5504]{1,0:T(8,128)(2,1)S(1)} %collective-permute-done.33.refs_9_), channel_id=1, source_target_pairs={{0,2},{1,3},{2,0},{3,1},{4,6},{5,7},{6,4},{7,5},{8,10},{9,11},{10,... | collective-permute-start | bytes 528392 | tf_op jit(solution)/shard_map/ppermute | solution.py:59
  139.6 14.1 %collective-permute-start.28 = (bf16[16,5504]{1,0:T(8,128)(2,1)S(1)}, bf16[16,5504]{1,0:T(8,128)(2,1)S(1)}, u32[]{:S(2)}, u32[]{:S(2)}) collective-permute-start(bf16[16,5504]{1,0:T(8,128)(2,1)S(1)} %get-tuple-element.164), channel_id=1, source_target_pairs={{0,2},{1,3},{2,0},{3,1},{4,6},{5,7},{6,4},{7,5},{8,10},{9,11},{10,... | collective-permute-start | bytes 528392 | tf_op jit(solution)/shard_map/ppermute | solution.py:59
  141.7 12.0 %collective-permute-start.29 = (bf16[16,5504]{1,0:T(8,128)(2,1)S(1)}, bf16[16,5504]{1,0:T(8,128)(2,1)S(1)}, u32[]{:S(2)}, u32[]{:S(2)}) collective-permute-start(bf16[16,5504]{1,0:T(8,128)(2,1)S(1)} %get-tuple-element.165), channel_id=1, source_target_pairs={{0,1},{1,0},{2,3},{3,2},{4,5},{5,4},{6,7},{7,6},{8,9},{9,8},{10,11... | collective-permute-start | bytes 528392 | tf_op jit(solution)/shard_map/ppermute | solution.py:59
  142.7 11.0 %collective-permute-start.27 = (bf16[16,5504]{1,0:T(8,128)(2,1)S(1)}, bf16[16,5504]{1,0:T(8,128)(2,1)S(1)}, u32[]{:S(2)}, u32[]{:S(2)}) collective-permute-start(bf16[16,5504]{1,0:T(8,128)(2,1)S(1)} %add_convert_fusion.1), channel_id=1, source_target_pairs={{0,4},{1,5},{2,6},{3,7},{4,0},{5,1},{6,2},{7,3},{8,12},{9,13},{10,... | collective-permute-start | bytes 528392 | tf_op jit(solution)/shard_map/ppermute | solution.py:59
  151.4 5.5 %collective-permute-start.39 = (bf16[16,5504]{1,0:T(8,128)(2,1)S(1)}, bf16[16,5504]{1,0:T(8,128)(2,1)S(1)}, u32[]{:S(2)}, u32[]{:S(2)}) collective-permute-start(bf16[16,5504]{1,0:T(8,128)(2,1)S(1)} %get-tuple-element.185), channel_id=1, source_target_pairs={{0,1},{1,0},{2,3},{3,2},{4,5},{5,4},{6,7},{7,6},{8,9},{9,8},{10,11... | collective-permute-start | bytes 528392 | tf_op jit(solution)/shard_map/ppermute | solution.py:59
  152.1 5.5 %collective-permute-start.38 = (bf16[16,5504]{1,0:T(8,128)(2,1)S(1)}, bf16[16,5504]{1,0:T(8,128)(2,1)S(1)}, u32[]{:S(2)}, u32[]{:S(2)}) collective-permute-start(bf16[16,5504]{1,0:T(8,128)(2,1)S(1)} %get-tuple-element.184.refs_11_), channel_id=1, source_target_pairs={{0,2},{1,3},{2,0},{3,1},{4,6},{5,7},{6,4},{7,5},{8,10},{9,11},{10,... | collective-permute-start | bytes 528392 | tf_op jit(solution)/shard_map/ppermute | solution.py:59
  157.7 8.5 %collective-permute-start.40 = (bf16[16,5504]{1,0:T(8,128)(2,1)S(1)}, bf16[16,5504]{1,0:T(8,128)(2,1)S(1)}, u32[]{:S(2)}, u32[]{:S(2)}) collective-permute-start(bf16[16,5504]{1,0:T(8,128)(2,1)S(1)} %add_convert_fusion), channel_id=1, source_target_pairs={{0,4},{1,5},{2,6},{3,7},{4,0},{5,1},{6,2},{7,3},{8,12},{9,13},{10,... | collective-permute-start | bytes 528392 | tf_op jit(solution)/shard_map/ppermute | solution.py:59
  158.1 8.1 %collective-permute-start.41 = (bf16[16,5504]{1,0:T(8,128)(2,1)S(1)}, bf16[16,5504]{1,0:T(8,128)(2,1)S(1)}, u32[]{:S(2)}, u32[]{:S(2)}) collective-permute-start(bf16[16,5504]{1,0:T(8,128)(2,1)S(1)} %get-tuple-element.195), channel_id=1, source_target_pairs={{0,2},{1,3},{2,0},{3,1},{4,6},{5,7},{6,4},{7,5},{8,10},{9,11},{10,... | collective-permute-start | bytes 528392 | tf_op jit(solution)/shard_map/ppermute | solution.py:59
  160.2 8.3 %collective-permute-start.42 = (bf16[16,5504]{1,0:T(8,128)(2,1)S(1)}, bf16[16,5504]{1,0:T(8,128)(2,1)S(1)}, u32[]{:S(2)}, u32[]{:S(2)}) collective-permute-start(bf16[16,5504]{1,0:T(8,128)(2,1)S(1)} %get-tuple-element.196), channel_id=1, source_target_pairs={{0,1},{1,0},{2,3},{3,2},{4,5},{5,4},{6,7},{7,6},{8,9},{9,8},{10,11... | collective-permute-start | bytes 528392 | tf_op jit(solution)/shard_map/ppermute | solution.py:59
  (1 other events, 2.3 us)

commit v4 on v3

--- a/solution.py
+++ b/solution.py
@@ -570,14 +570,15 @@
         scratch=[picked],
     )
 
-    cross_g, own_z, own_x = fence(
-        (crossing_of(boxes_g), shift(own_g, flip=2), shift(own_g, flip=1))
+    cross_g, own_z, own_x, fin_back = fence(
+        (crossing_of(boxes_g), shift(own_g, flip=2), shift(own_g, flip=1), fin_back)
     )
     cross_g, own_g = around(cross_g), [own_z, own_g, own_x]
     back = bind(expert_call, back_kernel, box, packs)
-    fin = fin_back + own_home(own_fin, 0)
-    cross_grad = back(cross_g, cross_kept0)[0]
-    own_grad = back(own_g, own_kept0, after=cross_grad[:1] + tuple(fin))[0]
+    fin_own = own_home(own_fin, 0)
+    fin = fin_back + fin_own
+    own_grad = back(own_g, own_kept0, after=fin_own)[0]
+    cross_grad = back(cross_g, cross_kept0, after=own_grad[:1])[0]
     got, _ = give_back(cross_grad, own_grad, 0)
     got[: experts - 1] = [sums_home.astype(F32) for sums_home in got[: experts - 1]]
     (g0,) = call(

time: 170 us -> 170 us (level)
  waiting for transfers between devices: 92.4 us -> 95.1 us
  starting transfers between devices: 48.5 us -> 45.9 us
    ppermute x43, waiting for transfers between devices: 92.4 us -> 95.1 us  [shift(): return lax.ppermute(value, ('section', 'expert'), pairs)]
    ppermute x43, starting transfers between devices: 48.5 us -> 45.9 us  [shift(): return lax.ppermute(value, ('section', 'expert'), pairs)]
  transfers between devices with their start and end apart: 43 -> 43, of which waited for: 25 -> 25; matrix products, arithmetic and copies ran while one was open for 1% -> 1% of each run, Pallas kernels for 9% -> 7%
where the time goes in v4:
time: 170 us
  waiting for transfers between devices  95.1 us (56%)
  starting transfers between devices  45.9 us (27%)
  Pallas kernels  23 us (14%)
  local copies, waits for them, and re-layouts  4.53 us (3%)
    ppermute x43, waiting for transfers between devices, shift(): return lax.ppermute(value, ('section', 'expert'), pairs)  95.1 us
    ppermute x43, starting transfers between devices, shift(): return lax.ppermute(value, ('section', 'expert'), pairs)  45.9 us
    pallas_call x15, Pallas kernels, call(): pl.pallas_call(reading, out_shape=list(outs), in_specs=[vmem] * read + [p...  23 us
  transfers between devices with their start and end apart: 43, of which 25 were waited for; matrix products, arithmetic and copies ran while one was open for 1% of the time, Pallas kernels for 7%

profile of v4, /device:TPU:0, one launch (start us, length us, event | category | flops | bytes accessed | tf_op | source)
XLA Modules:
  0.0 170.0 jit_solution(16683910746969626603)
XLA Ops:
  0.6 1.2 slice.40
  1.8 1.1 slice.41
  3.1 3.0 %collective-permute-start = (bf16[336,2560]{1,0:T(8,128)(2,1)S(1)}, bf16[336,2560]{1,0:T(8,128)(2,1)S(1)}, u32[]{:S(2)}, u32[]{:S(2)}) collective-permute-start(bf16[336,2560]{1,0:T(8,128)(2,1)S(1)} %pad_maximum_fusion.refs_5_.refs_0_), channel_id=1, source_target_pairs={{0,1},{1,0},{2,3},{3,2},{4,5},{5,4},{6,7},{7,6},{8,9},{9,8},{10,11... | collective-permute-start | bytes 5160968 | tf_op jit(solution)/shard_map/ppermute | solution.py:59
  6.1 1.0 slice.42
  7.2 1.1 slice.43
  8.4 1.6 collective-permute-start.1
  10.9 2.6 %collective-permute-start.2 = (bf16[32,5504]{1,0:T(8,128)(2,1)S(1)}, bf16[32,5504]{1,0:T(8,128)(2,1)S(1)}, u32[]{:S(2)}, u32[]{:S(2)}) collective-permute-start(bf16[32,5504]{1,0:T(8,128)(2,1)S(1)} %get-tuple-element.101), channel_id=1, source_target_pairs={{0,4},{1,5},{2,6},{3,7},{4,0},{5,1},{6,2},{7,3},{8,12},{9,13},{10,... | collective-permute-start | bytes 1056776 | tf_op jit(solution)/shard_map/ppermute | solution.py:59
  14.6 32.9 %collective-permute-done.4.refs_6_ = bf16[16,5504]{1,0:T(8,128)(2,1)S(1)} collective-permute-done((bf16[16,5504]{1,0:T(8,128)(2,1)S(1)}, bf16[16,5504]{1,0:T(8,128)(2,1)S(1)}, u32[]{:S(2)}, u32[]{:S(2)}) %collective-permute-start.4) | collective-permute-done | bytes 176160 | tf_op jit(solution)/shard_map/ppermute | solution.py:59
  49.3 1.6 collective-permute-start.5
  50.9 2.9 %collective-permute-done.6.refs_6_ = bf16[16,5504]{1,0:T(8,128)(2,1)S(1)} collective-permute-done((bf16[16,5504]{1,0:T(8,128)(2,1)S(1)}, bf16[16,5504]{1,0:T(8,128)(2,1)S(1)}, u32[]{:S(2)}, u32[]{:S(2)}) %collective-permute-start.6) | collective-permute-done | bytes 176160 | tf_op jit(solution)/shard_map/ppermute | solution.py:59
  54.8 2.5 %shard_map.96 = (bf16[16,5504]{1,0:T(8,128)(2,1)S(1)}, bf16[16,5504]{1,0:T(8,128)(2,1)S(1)}, bf16[16,5504]{1,0:T(8,128)(2,1)S(1)}, f32[96,224]{1,0:T(8,128)S(1)}...) custom-call(bf16[336,2560]{1,0:T(8,128)(2,1)S(1)} %pad_maximum_fusion.refs_5_.refs_0_, ...), custom_call_target="tpu_custom_call" | custom-call | flops 566231040 | bytes 7249920 | tf_op jit(solution)/shard_map/pallas_call | solution.py:71
  57.2 1.6 collective-permute-start.8
  58.9 1.1 collective-permute-start.9
  61.3 2.5 %shard_map.97 = (bf16[16,5504]{1,0:T(8,128)(2,1)S(1)}, bf16[16,5504]{1,0:T(8,128)(2,1)S(1)}, bf16[16,5504]{1,0:T(8,128)(2,1)S(1)}, f32[96,224]{1,0:T(8,128)S(1)}...) custom-call(bf16[336,2560]{1,0:T(8,128)(2,1)S(1)} %pad_maximum_fusion.refs_5_.refs_0_, ...), custom_call_target="tpu_custom_call" | custom-call | flops 566231040 | bytes 7249920 | tf_op jit(solution)/shard_map/pallas_call | solution.py:71
  64.5 1.7 %collective-permute-done.9 = bf16[16,5504]{1,0:T(8,128)(2,1)S(1)} collective-permute-done((bf16[16,5504]{1,0:T(8,128)(2,1)S(1)}, bf16[16,5504]{1,0:T(8,128)(2,1)S(1)}, u32[]{:S(2)}, u32[]{:S(2)}) %collective-permute-start.9) | collective-permute-done | bytes 176160 | tf_op jit(solution)/shard_map/ppermute | solution.py:59
  66.3 1.5 collective-permute-start.10
  67.8 2.5 %collective-permute-done.12.refs_6_ = bf16[32,5504]{1,0:T(8,128)(2,1)S(1)} collective-permute-done((bf16[32,5504]{1,0:T(8,128)(2,1)S(1)}, bf16[32,5504]{1,0:T(8,128)(2,1)S(1)}, u32[]{:S(2)}, u32[]{:S(2)}) %collective-permute-start.12) | collective-permute-done | bytes 352288 | tf_op jit(solution)/shard_map/ppermute | solution.py:59
  70.3 1.9 %collective-permute-start.14 = (bf16[16,5504]{1,0:T(8,128)(2,1)S(1)}, bf16[16,5504]{1,0:T(8,128)(2,1)S(1)}, u32[]{:S(2)}, u32[]{:S(2)}) collective-permute-start(bf16[16,5504]{1,0:T(8,128)(2,1)S(1)} %get-tuple-element.129), channel_id=1, source_target_pairs={{0,9},{1,8},{2,11},{3,10},{4,13},{5,12},{6,15},{7,14},{8,17},{9,16... | collective-permute-start | bytes 528392 | tf_op jit(solution)/shard_map/ppermute | solution.py:59
  72.3 6.4 %collective-permute-done.10.refs_4_ = bf16[16,5504]{1,0:T(8,128)(2,1)S(1)} collective-permute-done((bf16[16,5504]{1,0:T(8,128)(2,1)S(1)}, bf16[16,5504]{1,0:T(8,128)(2,1)S(1)}, u32[]{:S(2)}, u32[]{:S(2)}) %collective-permute-start.10) | collective-permute-done | bytes 176160 | tf_op jit(solution)/shard_map/ppermute | solution.py:59
  78.7 1.2 collective-permute-done.13.refs_5_
  79.8 1.1 collective-permute-done.15.refs_7_
  81.9 1.9 %collective-permute-start.16 = (bf16[16,5504]{1,0:T(8,128)(2,1)S(1)}, bf16[16,5504]{1,0:T(8,128)(2,1)S(1)}, u32[]{:S(2)}, u32[]{:S(2)}) collective-permute-start(bf16[16,5504]{1,0:T(8,128)(2,1)S(1)} %get-tuple-element.132), channel_id=1, source_target_pairs={{0,4},{1,5},{2,6},{3,7},{4,0},{5,1},{6,2},{7,3},{8,12},{9,13},{10,... | collective-permute-start | bytes 528392 | tf_op jit(solution)/shard_map/ppermute | solution.py:59
  84.4 2.5 %collective-permute-start.17 = (bf16[16,5504]{1,0:T(8,128)(2,1)S(1)}, bf16[16,5504]{1,0:T(8,128)(2,1)S(1)}, u32[]{:S(2)}, u32[]{:S(2)}) collective-permute-start(bf16[16,5504]{1,0:T(8,128)(2,1)S(1)} %get-tuple-element.133.refs_9_), channel_id=1, source_target_pairs={{0,2},{1,3},{2,0},{3,1},{4,6},{5,7},{6,4},{7,5},{8,10},{9,11},{10,... | collective-permute-start | bytes 528392 | tf_op jit(solution)/shard_map/ppermute | solution.py:59
  86.9 6.7 %collective-permute-done.16.refs_9_ = bf16[16,5504]{1,0:T(8,128)(2,1)S(1)} collective-permute-done((bf16[16,5504]{1,0:T(8,128)(2,1)S(1)}, bf16[16,5504]{1,0:T(8,128)(2,1)S(1)}, u32[]{:S(2)}, u32[]{:S(2)}) %collective-permute-start.16) | collective-permute-done | bytes 176160 | tf_op jit(solution)/shard_map/ppermute | solution.py:59
  97.1 2.6 %shard_map.101 = (bf16[16,5504]{1,0:T(8,128)(2,1)S(1)}, bf16[16,5504]{1,0:T(8,128)(2,1)S(1)}, bf16[16,5504]{1,0:T(8,128)(2,1)S(1)}, f32[96,224]{1,0:T(8,128)S(1)...) custom-call(bf16[336,2560]{1,0:T(8,128)(2,1)S(1)} %pad_maximum_fusion.refs_5_.refs_0_, ...), custom_call_target="tpu_custom_call" | custom-call | flops 566231040 | bytes 7397376 | tf_op jit(solution)/shard_map/pallas_call | solution.py:71
  99.8 1.0 collective-permute-done.20.refs_8_
  100.8 2.7 %shard_map.102 = (bf16[16,5504]{1,0:T(8,128)(2,1)S(1)}, bf16[16,5504]{1,0:T(8,128)(2,1)S(1)}, bf16[16,5504]{1,0:T(8,128)(2,1)S(1)}, f32[96,224]{1,0:T(8,128)S(1)...) custom-call(bf16[336,2560]{1,0:T(8,128)(2,1)S(1)} %pad_maximum_fusion.refs_5_.refs_0_, ...), custom_call_target="tpu_custom_call" | custom-call | flops 566231040 | bytes 7397376 | tf_op jit(solution)/shard_map/pallas_call | solution.py:71
  103.5 1.0 collective-permute-start.22
  106.4 1.1 collective-permute-start.25
  108.4 2.3 %collective-permute-done.22 = bf16[16,5504]{1,0:T(8,128)(2,1)S(1)} collective-permute-done((bf16[16,5504]{1,0:T(8,128)(2,1)S(1)}, bf16[16,5504]{1,0:T(8,128)(2,1)S(1)}, u32[]{:S(2)}, u32[]{:S(2)}) %collective-permute-start.22) | collective-permute-done | bytes 176160 | tf_op jit(solution)/shard_map/ppermute | solution.py:59
  111.4 4.5 %collective-permute-start.27 = (bf16[16,5504]{1,0:T(8,128)(2,1)S(1)}, bf16[16,5504]{1,0:T(8,128)(2,1)S(1)}, u32[]{:S(2)}, u32[]{:S(2)}) collective-permute-start(bf16[16,5504]{1,0:T(8,128)(2,1)S(1)} %get-tuple-element.165.refs_11_), channel_id=1, source_target_pairs={{0,26},{1,27},{2,24},{3,25},{4,30},{5,31},{6,28},{7,29},{8,2},{9,3... | collective-permute-start | bytes 528392 | tf_op jit(solution)/shard_map/ppermute | solution.py:59
  116.3 6.3 %collective-permute-done.24.refs_2_ = bf16[16,5504]{1,0:T(8,128)(2,1)S(1)} collective-permute-done((bf16[16,5504]{1,0:T(8,128)(2,1)S(1)}, bf16[16,5504]{1,0:T(8,128)(2,1)S(1)}, u32[]{:S(2)}, u32[]{:S(2)}) %collective-permute-start.24) | collective-permute-done | bytes 176160 | tf_op jit(solution)/shard_map/ppermute | solution.py:59
  122.6 2.2 %collective-permute-done.29.refs_5_ = bf16[16,5504]{1,0:T(8,128)(2,1)S(1)} collective-permute-done((bf16[16,5504]{1,0:T(8,128)(2,1)S(1)}, bf16[16,5504]{1,0:T(8,128)(2,1)S(1)}, u32[]{:S(2)}, u32[]{:S(2)}) %collective-permute-start.29) | collective-permute-done | bytes 176160 | tf_op jit(solution)/shard_map/ppermute | solution.py:59
  125.9 1.1 collective-permute-start.32
  127.0 1.5 collective-permute-start.31
  128.4 1.4 collective-permute-start.33
  130.7 2.1 %collective-permute-start.34 = (bf16[16,5504]{1,0:T(8,128)(2,1)S(1)}, bf16[16,5504]{1,0:T(8,128)(2,1)S(1)}, u32[]{:S(2)}, u32[]{:S(2)}) collective-permute-start(bf16[16,5504]{1,0:T(8,128)(2,1)S(1)} %get-tuple-element.176), channel_id=1, source_target_pairs={{0,2},{1,3},{2,0},{3,1},{4,6},{5,7},{6,4},{7,5},{8,10},{9,11},{10,... | collective-permute-start | bytes 528392 | tf_op jit(solution)/shard_map/ppermute | solution.py:59
  132.7 4.0 %collective-permute-done.30.refs_9_ = bf16[16,5504]{1,0:T(8,128)(2,1)S(1)} collective-permute-done((bf16[16,5504]{1,0:T(8,128)(2,1)S(1)}, bf16[16,5504]{1,0:T(8,128)(2,1)S(1)}, u32[]{:S(2)}, u32[]{:S(2)}) %collective-permute-start.30) | collective-permute-done | bytes 176160 | tf_op jit(solution)/shard_map/ppermute | solution.py:59
  138.1 6.2 %collective-permute-done.33.refs_2_ = bf16[16,5504]{1,0:T(8,128)(2,1)S(1)} collective-permute-done((bf16[16,5504]{1,0:T(8,128)(2,1)S(1)}, bf16[16,5504]{1,0:T(8,128)(2,1)S(1)}, u32[]{:S(2)}, u32[]{:S(2)}) %collective-permute-start.33) | collective-permute-done | bytes 176160 | tf_op jit(solution)/shard_map/ppermute | solution.py:59
  145.3 2.0 %shard_map.107 = (bf16[16,5504]{1,0:T(8,128)(2,1)S(1)}, bf16[16,5504]{1,0:T(8,128)(2,1)S(1)}, bf16[16,5504]{1,0:T(8,128)(2,1)S(1)}) custom-call(bf16[336,2560]{1,0:T(8,128)(2,1)S(1)} %pad_maximum_fusion.refs_5_.refs_0_, bf16[336,2560]{1,0:T(8,128)(2,1)S(1)} %collective-permute-done.refs_1_, bf16[240,2560]{1,0:T(8,128)(2,1)S(1)} %pad_maximum_fusion.1.refs_6_.refs_2_, ...), custom_call_target="tpu_custom_call" | custom-call | flops 566231040 | bytes 7249920 | tf_op jit(solution)/shard_map/pallas_call | solution.py:71
  147.3 3.5 %collective-permute-done.37.refs_10_ = bf16[16,5504]{1,0:T(8,128)(2,1)S(1)} collective-permute-done((bf16[16,5504]{1,0:T(8,128)(2,1)S(1)}, bf16[16,5504]{1,0:T(8,128)(2,1)S(1)}, u32[]{:S(2)}, u32[]{:S(2)}) %collective-permute-start.37) | collective-permute-done | bytes 176160 | tf_op jit(solution)/shard_map/ppermute | solution.py:59
  151.4 2.0 %shard_map.108 = (bf16[16,5504]{1,0:T(8,128)(2,1)S(1)}, bf16[16,5504]{1,0:T(8,128)(2,1)S(1)}, bf16[16,5504]{1,0:T(8,128)(2,1)S(1)}) custom-call(bf16[336,2560]{1,0:T(8,128)(2,1)S(1)} %pad_maximum_fusion.refs_5_.refs_0_, bf16[336,2560]{1,0:T(8,128)(2,1)S(1)} %collective-permute-done.refs_1_, bf16[240,2560]{1,0:T(8,128)(2,1)S(1)} %pad_maximum_fusion.1.refs_6_.refs_2_, ...), custom_call_target="tpu_custom_call" | custom-call | flops 566231040 | bytes 7249920 | tf_op jit(solution)/shard_map/pallas_call | solution.py:71
  153.7 1.1 collective-permute-start.39
  154.8 4.1 %collective-permute-done.38 = bf16[16,5504]{1,0:T(8,128)(2,1)S(1)} collective-permute-done((bf16[16,5504]{1,0:T(8,128)(2,1)S(1)}, bf16[16,5504]{1,0:T(8,128)(2,1)S(1)}, u32[]{:S(2)}, u32[]{:S(2)}) %collective-permute-start.38) | collective-permute-done | bytes 176160 | tf_op jit(solution)/shard_map/ppermute | solution.py:59
  159.3 2.6 %collective-permute-start.40 = (bf16[16,5504]{1,0:T(8,128)(2,1)S(1)}, bf16[16,5504]{1,0:T(8,128)(2,1)S(1)}, u32[]{:S(2)}, u32[]{:S(2)}) collective-permute-start(bf16[16,5504]{1,0:T(8,128)(2,1)S(1)} %add_convert_fusion), channel_id=1, source_target_pairs={{0,4},{1,5},{2,6},{3,7},{4,0},{5,1},{6,2},{7,3},{8,12},{9,13},{10,... | collective-permute-start | bytes 528392 | tf_op jit(solution)/shard_map/ppermute | solution.py:59
  162.6 1.1 shard_map.106
  163.7 4.9 %collective-permute-done.40 = bf16[16,5504]{1,0:T(8,128)(2,1)S(1)} collective-permute-done((bf16[16,5504]{1,0:T(8,128)(2,1)S(1)}, bf16[16,5504]{1,0:T(8,128)(2,1)S(1)}, u32[]{:S(2)}, u32[]{:S(2)}) %collective-permute-start.40) | collective-permute-done | bytes 176160 | tf_op jit(solution)/shard_map/ppermute | solution.py:59
  168.6 1.3 shard_map.109
  (80 shorter events, 22.4 us)
Async XLA Ops:
  3.1 45.2 %collective-permute-start = (bf16[336,2560]{1,0:T(8,128)(2,1)S(1)}, bf16[336,2560]{1,0:T(8,128)(2,1)S(1)}, u32[]{:S(2)}, u32[]{:S(2)}) collective-permute-start(bf16[336,2560]{1,0:T(8,128)(2,1)S(1)} %pad_maximum_fusion.refs_5_.refs_0_), channel_id=1, source_target_pairs={{0,1},{1,0},{2,3},{3,2},{4,5},{5,4},{6,7},{7,6},{8,9},{9,8},{10,11... | collective-permute-start | bytes 5160968 | tf_op jit(solution)/shard_map/ppermute | solution.py:59
  7.2 2.9 %copy-start = (bf16[1,64,2560]{2,1,0:T(8,128)(2,1)S(1)}, bf16[1,64,2560]{2,1,0:T(8,128)(2,1)}, u32[]{:S(2)}) copy-start(bf16[1,64,2560]{2,1,0:T(8,128)(2,1)} %param.15) | copy-start | bytes 983044
  7.2 2.9 %copy-start.1 = (bf16[1,64,2560]{2,1,0:T(8,128)(2,1)S(1)}, bf16[1,64,2560]{2,1,0:T(8,128)(2,1)}, u32[]{:S(2)}) copy-start(bf16[1,64,2560]{2,1,0:T(8,128)(2,1)} %param.8) | copy-start | bytes 983044
  7.2 2.9 %copy-start.2 = (f32[1,2560]{1,0:T(1,128)S(1)}, f32[1,2560]{1,0:T(1,128)}, u32[]{:S(2)}) copy-start(f32[1,2560]{1,0:T(1,128)} %refs_3_.3) | copy-start | bytes 30724
  7.2 2.9 %copy-start.3 = (s32[1,2,64,1]{2,3,1,0:T(1,128)S(1)}, s32[1,2,64,1]{2,3,1,0:T(1,128)}, u32[]{:S(2)}) copy-start(s32[1,2,64,1]{2,3,1,0:T(1,128)} %param.13) | copy-start | bytes 1540
  7.2 2.8 %copy-start.4 = (f32[1,2,64,1]{2,3,1,0:T(1,128)S(1)}, f32[1,2,64,1]{2,3,1,0:T(1,128)}, u32[]{:S(2)}) copy-start(f32[1,2,64,1]{2,3,1,0:T(1,128)} %param.14) | copy-start | bytes 1540
  8.4 39.9 %collective-permute-start.1 = (bf16[240,2560]{1,0:T(8,128)(2,1)S(1)}, bf16[240,2560]{1,0:T(8,128)(2,1)S(1)}, u32[]{:S(2)}, u32[]{:S(2)}) collective-permute-start(bf16[240,2560]{1,0:T(8,128)(2,1)S(1)} %pad_maximum_fusion.1.refs_6_.refs_2_), channel_id=1, source_target_pairs={{0,2},{1,3},{2,0},{3,1},{4,6},{5,7},{6,4},{7,5},{8,10},{9,11},{10,... | collective-permute-start | bytes 3686408 | tf_op jit(solution)/shard_map/ppermute | solution.py:59
  10.9 37.3 %collective-permute-start.2 = (bf16[32,5504]{1,0:T(8,128)(2,1)S(1)}, bf16[32,5504]{1,0:T(8,128)(2,1)S(1)}, u32[]{:S(2)}, u32[]{:S(2)}) collective-permute-start(bf16[32,5504]{1,0:T(8,128)(2,1)S(1)} %get-tuple-element.101), channel_id=1, source_target_pairs={{0,4},{1,5},{2,6},{3,7},{4,0},{5,1},{6,2},{7,3},{8,12},{9,13},{10,... | collective-permute-start | bytes 1056776 | tf_op jit(solution)/shard_map/ppermute | solution.py:59
  13.6 33.9 %collective-permute-start.4 = (bf16[16,5504]{1,0:T(8,128)(2,1)S(1)}, bf16[16,5504]{1,0:T(8,128)(2,1)S(1)}, u32[]{:S(2)}, u32[]{:S(2)}) collective-permute-start(bf16[16,5504]{1,0:T(8,128)(2,1)S(1)} %get-tuple-element.122.refs_5_), channel_id=1, source_target_pairs={{0,1},{1,0},{2,3},{3,2},{4,5},{5,4},{6,7},{7,6},{8,9},{9,8},{10,11... | collective-permute-start | bytes 528392 | tf_op jit(solution)/shard_map/ppermute | solution.py:59
  14.1 34.2 %collective-permute-start.3 = (bf16[16,5504]{1,0:T(8,128)(2,1)S(1)}, bf16[16,5504]{1,0:T(8,128)(2,1)S(1)}, u32[]{:S(2)}, u32[]{:S(2)}) collective-permute-start(bf16[16,5504]{1,0:T(8,128)(2,1)S(1)} %get-tuple-element.122.refs_5_), channel_id=1, source_target_pairs={{0,2},{1,3},{2,0},{3,1},{4,6},{5,7},{6,4},{7,5},{8,10},{9,11},{10,... | collective-permute-start | bytes 528392 | tf_op jit(solution)/shard_map/ppermute | solution.py:59
  48.3 5.5 %collective-permute-start.6 = (bf16[16,5504]{1,0:T(8,128)(2,1)S(1)}, bf16[16,5504]{1,0:T(8,128)(2,1)S(1)}, u32[]{:S(2)}, u32[]{:S(2)}) collective-permute-start(bf16[16,5504]{1,0:T(8,128)(2,1)S(1)} %get-tuple-element.110.refs_5_), channel_id=1, source_target_pairs={{0,1},{1,0},{2,3},{3,2},{4,5},{5,4},{6,7},{7,6},{8,9},{9,8},{10,11... | collective-permute-start | bytes 528392 | tf_op jit(solution)/shard_map/ppermute | solution.py:59
  49.3 5.5 %collective-permute-start.5 = (bf16[16,5504]{1,0:T(8,128)(2,1)S(1)}, bf16[16,5504]{1,0:T(8,128)(2,1)S(1)}, u32[]{:S(2)}, u32[]{:S(2)}) collective-permute-start(bf16[16,5504]{1,0:T(8,128)(2,1)S(1)} %get-tuple-element.110.refs_5_), channel_id=1, source_target_pairs={{0,2},{1,3},{2,0},{3,1},{4,6},{5,7},{6,4},{7,5},{8,10},{9,11},{10,... | collective-permute-start | bytes 528392 | tf_op jit(solution)/shard_map/ppermute | solution.py:59
  57.2 7.3 %collective-permute-start.8 = (bf16[16,5504]{1,0:T(8,128)(2,1)S(1)}, bf16[16,5504]{1,0:T(8,128)(2,1)S(1)}, u32[]{:S(2)}, u32[]{:S(2)}) collective-permute-start(bf16[16,5504]{1,0:T(8,128)(2,1)S(1)} %get-tuple-element.119.refs_7_), channel_id=1, source_target_pairs={{0,2},{1,3},{2,0},{3,1},{4,6},{5,7},{6,4},{7,5},{8,10},{9,11},{10,... | collective-permute-start | bytes 528392 | tf_op jit(solution)/shard_map/ppermute | solution.py:59
  58.9 7.4 %collective-permute-start.9 = (bf16[16,5504]{1,0:T(8,128)(2,1)S(1)}, bf16[16,5504]{1,0:T(8,128)(2,1)S(1)}, u32[]{:S(2)}, u32[]{:S(2)}) collective-permute-start(bf16[16,5504]{1,0:T(8,128)(2,1)S(1)} %get-tuple-element.120), channel_id=1, source_target_pairs={{0,1},{1,0},{2,3},{3,2},{4,5},{5,4},{6,7},{7,6},{8,9},{9,8},{10,11... | collective-permute-start | bytes 528392 | tf_op jit(solution)/shard_map/ppermute | solution.py:59
  60.0 10.3 %collective-permute-start.12 = (bf16[32,5504]{1,0:T(8,128)(2,1)S(1)}, bf16[32,5504]{1,0:T(8,128)(2,1)S(1)}, u32[]{:S(2)}, u32[]{:S(2)}) collective-permute-start(bf16[32,5504]{1,0:T(8,128)(2,1)S(1)} %pad_maximum_fusion.2.refs_5_), channel_id=1, source_target_pairs={{0,1},{1,0},{2,3},{3,2},{4,5},{5,4},{6,7},{7,6},{8,9},{9,8},{10,11... | collective-permute-start | bytes 1056776 | tf_op jit(solution)/shard_map/ppermute | solution.py:59
  60.9 9.4 %collective-permute-start.11 = (bf16[32,5504]{1,0:T(8,128)(2,1)S(1)}, bf16[32,5504]{1,0:T(8,128)(2,1)S(1)}, u32[]{:S(2)}, u32[]{:S(2)}) collective-permute-start(bf16[32,5504]{1,0:T(8,128)(2,1)S(1)} %pad_maximum_fusion.2.refs_5_), channel_id=1, source_target_pairs={{0,2},{1,3},{2,0},{3,1},{4,6},{5,7},{6,4},{7,5},{8,10},{9,11},{10,... | collective-permute-start | bytes 1056776 | tf_op jit(solution)/shard_map/ppermute | solution.py:59
  61.3 17.3 %collective-permute-start.7 = (bf16[80,2560]{1,0:T(8,128)(2,1)S(1)}, bf16[80,2560]{1,0:T(8,128)(2,1)S(1)}, u32[]{:S(2)}, u32[]{:S(2)}) collective-permute-start(bf16[80,2560]{1,0:T(8,128)(2,1)S(1)} %get-tuple-element.116), channel_id=1, source_target_pairs={{0,8},{1,9},{2,10},{3,11},{4,12},{5,13},{6,14},{7,15},{8,16},{9,17... | collective-permute-start | bytes 1228808 | tf_op jit(solution)/shard_map/ppermute | solution.py:59
  66.3 12.3 %collective-permute-start.10 = (bf16[16,5504]{1,0:T(8,128)(2,1)S(1)}, bf16[16,5504]{1,0:T(8,128)(2,1)S(1)}, u32[]{:S(2)}, u32[]{:S(2)}) collective-permute-start(bf16[16,5504]{1,0:T(8,128)(2,1)S(1)} %add_convert_fusion.3), channel_id=1, source_target_pairs={{0,12},{1,13},{2,14},{3,15},{4,8},{5,9},{6,10},{7,11},{8,20},{9,21... | collective-permute-start | bytes 528392 | tf_op jit(solution)/shard_map/ppermute | solution.py:59
  70.3 9.5 %collective-permute-start.13 = (bf16[16,5504]{1,0:T(8,128)(2,1)S(1)}, bf16[16,5504]{1,0:T(8,128)(2,1)S(1)}, u32[]{:S(2)}, u32[]{:S(2)}) collective-permute-start(bf16[16,5504]{1,0:T(8,128)(2,1)S(1)} %get-tuple-element.128), channel_id=1, source_target_pairs={{0,10},{1,11},{2,8},{3,9},{4,14},{5,15},{6,12},{7,13},{8,18},{9,19... | collective-permute-start | bytes 528392 | tf_op jit(solution)/shard_map/ppermute | solution.py:59
  70.3 9.5 %collective-permute-start.14 = (bf16[16,5504]{1,0:T(8,128)(2,1)S(1)}, bf16[16,5504]{1,0:T(8,128)(2,1)S(1)}, u32[]{:S(2)}, u32[]{:S(2)}) collective-permute-start(bf16[16,5504]{1,0:T(8,128)(2,1)S(1)} %get-tuple-element.129), channel_id=1, source_target_pairs={{0,9},{1,8},{2,11},{3,10},{4,13},{5,12},{6,15},{7,14},{8,17},{9,16... | collective-permute-start | bytes 528392 | tf_op jit(solution)/shard_map/ppermute | solution.py:59
  72.3 8.7 %collective-permute-start.15 = (bf16[16,5504]{1,0:T(8,128)(2,1)S(1)}, bf16[16,5504]{1,0:T(8,128)(2,1)S(1)}, u32[]{:S(2)}, u32[]{:S(2)}) collective-permute-start(bf16[16,5504]{1,0:T(8,128)(2,1)S(1)} %get-tuple-element.130), channel_id=1, source_target_pairs={{0,8},{1,9},{2,10},{3,11},{4,12},{5,13},{6,14},{7,15},{8,16},{9,17... | collective-permute-start | bytes 528392 | tf_op jit(solution)/shard_map/ppermute | solution.py:59
  81.9 12.5 %collective-permute-start.19 = (bf16[144,2560]{1,0:T(8,128)(2,1)S(1)}, bf16[144,2560]{1,0:T(8,128)(2,1)S(1)}, u32[]{:S(2)}, u32[]{:S(2)}) collective-permute-start(bf16[144,2560]{1,0:T(8,128)(2,1)S(1)} %get-tuple-element.134), channel_id=1, source_target_pairs={{0,24},{1,25},{2,26},{3,27},{4,28},{5,29},{6,30},{7,31},{8,0},{9,1... | collective-permute-start | bytes 2211848 | tf_op jit(solution)/shard_map/ppermute | solution.py:59
  81.9 11.7 %collective-permute-start.16 = (bf16[16,5504]{1,0:T(8,128)(2,1)S(1)}, bf16[16,5504]{1,0:T(8,128)(2,1)S(1)}, u32[]{:S(2)}, u32[]{:S(2)}) collective-permute-start(bf16[16,5504]{1,0:T(8,128)(2,1)S(1)} %get-tuple-element.132), channel_id=1, source_target_pairs={{0,4},{1,5},{2,6},{3,7},{4,0},{5,1},{6,2},{7,3},{8,12},{9,13},{10,... | collective-permute-start | bytes 528392 | tf_op jit(solution)/shard_map/ppermute | solution.py:59
  83.8 9.7 %collective-permute-start.18 = (bf16[16,5504]{1,0:T(8,128)(2,1)S(1)}, bf16[16,5504]{1,0:T(8,128)(2,1)S(1)}, u32[]{:S(2)}, u32[]{:S(2)}) collective-permute-start(bf16[16,5504]{1,0:T(8,128)(2,1)S(1)} %get-tuple-element.133.refs_9_), channel_id=1, source_target_pairs={{0,1},{1,0},{2,3},{3,2},{4,5},{5,4},{6,7},{7,6},{8,9},{9,8},{10,11... | collective-permute-start | bytes 528392 | tf_op jit(solution)/shard_map/ppermute | solution.py:59
  84.4 9.9 %collective-permute-start.17 = (bf16[16,5504]{1,0:T(8,128)(2,1)S(1)}, bf16[16,5504]{1,0:T(8,128)(2,1)S(1)}, u32[]{:S(2)}, u32[]{:S(2)}) collective-permute-start(bf16[16,5504]{1,0:T(8,128)(2,1)S(1)} %get-tuple-element.133.refs_9_), channel_id=1, source_target_pairs={{0,2},{1,3},{2,0},{3,1},{4,6},{5,7},{6,4},{7,5},{8,10},{9,11},{10,... | collective-permute-start | bytes 528392 | tf_op jit(solution)/shard_map/ppermute | solution.py:59
  94.3 5.4 %collective-permute-start.21 = (bf16[16,5504]{1,0:T(8,128)(2,1)S(1)}, bf16[16,5504]{1,0:T(8,128)(2,1)S(1)}, u32[]{:S(2)}, u32[]{:S(2)}) collective-permute-start(bf16[16,5504]{1,0:T(8,128)(2,1)S(1)} %collective-permute-done.16.refs_9_), channel_id=1, source_target_pairs={{0,1},{1,0},{2,3},{3,2},{4,5},{5,4},{6,7},{7,6},{8,9},{9,8},{10,11... | collective-permute-start | bytes 528392 | tf_op jit(solution)/shard_map/ppermute | solution.py:59
  95.4 5.5 %collective-permute-start.20 = (bf16[16,5504]{1,0:T(8,128)(2,1)S(1)}, bf16[16,5504]{1,0:T(8,128)(2,1)S(1)}, u32[]{:S(2)}, u32[]{:S(2)}) collective-permute-start(bf16[16,5504]{1,0:T(8,128)(2,1)S(1)} %collective-permute-done.16.refs_9_), channel_id=1, source_target_pairs={{0,2},{1,3},{2,0},{3,1},{4,6},{5,7},{6,4},{7,5},{8,10},{9,11},{10,... | collective-permute-start | bytes 528392 | tf_op jit(solution)/shard_map/ppermute | solution.py:59
  103.5 7.2 %collective-permute-start.22 = (bf16[16,5504]{1,0:T(8,128)(2,1)S(1)}, bf16[16,5504]{1,0:T(8,128)(2,1)S(1)}, u32[]{:S(2)}, u32[]{:S(2)}) collective-permute-start(bf16[16,5504]{1,0:T(8,128)(2,1)S(1)} %get-tuple-element.153), channel_id=1, source_target_pairs={{0,2},{1,3},{2,0},{3,1},{4,6},{5,7},{6,4},{7,5},{8,10},{9,11},{10,... | collective-permute-start | bytes 528392 | tf_op jit(solution)/shard_map/ppermute | solution.py:59
  104.5 6.7 %collective-permute-start.23 = (bf16[16,5504]{1,0:T(8,128)(2,1)S(1)}, bf16[16,5504]{1,0:T(8,128)(2,1)S(1)}, u32[]{:S(2)}, u32[]{:S(2)}) collective-permute-start(bf16[16,5504]{1,0:T(8,128)(2,1)S(1)} %get-tuple-element.154), channel_id=1, source_target_pairs={{0,1},{1,0},{2,3},{3,2},{4,5},{5,4},{6,7},{7,6},{8,9},{9,8},{10,11... | collective-permute-start | bytes 528392 | tf_op jit(solution)/shard_map/ppermute | solution.py:59
  106.4 9.5 %collective-permute-start.25 = (bf16[16,5504]{1,0:T(8,128)(2,1)S(1)}, bf16[16,5504]{1,0:T(8,128)(2,1)S(1)}, u32[]{:S(2)}, u32[]{:S(2)}) collective-permute-start(bf16[16,5504]{1,0:T(8,128)(2,1)S(1)} %get-tuple-element.160), channel_id=1, source_target_pairs={{0,2},{1,3},{2,0},{3,1},{4,6},{5,7},{6,4},{7,5},{8,10},{9,11},{10,... | collective-permute-start | bytes 528392 | tf_op jit(solution)/shard_map/ppermute | solution.py:59
  107.4 8.8 %collective-permute-start.26 = (bf16[16,5504]{1,0:T(8,128)(2,1)S(1)}, bf16[16,5504]{1,0:T(8,128)(2,1)S(1)}, u32[]{:S(2)}, u32[]{:S(2)}) collective-permute-start(bf16[16,5504]{1,0:T(8,128)(2,1)S(1)} %get-tuple-element.161), channel_id=1, source_target_pairs={{0,1},{1,0},{2,3},{3,2},{4,5},{5,4},{6,7},{7,6},{8,9},{9,8},{10,11... | collective-permute-start | bytes 528392 | tf_op jit(solution)/shard_map/ppermute | solution.py:59
  111.3 11.3 %collective-permute-start.24 = (bf16[16,5504]{1,0:T(8,128)(2,1)S(1)}, bf16[16,5504]{1,0:T(8,128)(2,1)S(1)}, u32[]{:S(2)}, u32[]{:S(2)}) collective-permute-start(bf16[16,5504]{1,0:T(8,128)(2,1)S(1)} %add_convert_fusion.2), channel_id=1, source_target_pairs={{0,28},{1,29},{2,30},{3,31},{4,24},{5,25},{6,26},{7,27},{8,4},{9,5... | collective-permute-start | bytes 528392 | tf_op jit(solution)/shard_map/ppermute | solution.py:59
  111.4 11.2 %collective-permute-start.27 = (bf16[16,5504]{1,0:T(8,128)(2,1)S(1)}, bf16[16,5504]{1,0:T(8,128)(2,1)S(1)}, u32[]{:S(2)}, u32[]{:S(2)}) collective-permute-start(bf16[16,5504]{1,0:T(8,128)(2,1)S(1)} %get-tuple-element.165.refs_11_), channel_id=1, source_target_pairs={{0,26},{1,27},{2,24},{3,25},{4,30},{5,31},{6,28},{7,29},{8,2},{9,3... | collective-permute-start | bytes 528392 | tf_op jit(solution)/shard_map/ppermute | solution.py:59
  115.9 6.7 %collective-permute-start.28 = (bf16[16,5504]{1,0:T(8,128)(2,1)S(1)}, bf16[16,5504]{1,0:T(8,128)(2,1)S(1)}, u32[]{:S(2)}, u32[]{:S(2)}) collective-permute-start(bf16[16,5504]{1,0:T(8,128)(2,1)S(1)} %get-tuple-element.166), channel_id=1, source_target_pairs={{0,25},{1,24},{2,27},{3,26},{4,29},{5,28},{6,31},{7,30},{8,1},{9,0... | collective-permute-start | bytes 528392 | tf_op jit(solution)/shard_map/ppermute | solution.py:59
  115.9 8.9 %collective-permute-start.29 = (bf16[16,5504]{1,0:T(8,128)(2,1)S(1)}, bf16[16,5504]{1,0:T(8,128)(2,1)S(1)}, u32[]{:S(2)}, u32[]{:S(2)}) collective-permute-start(bf16[16,5504]{1,0:T(8,128)(2,1)S(1)} %get-tuple-element.167), channel_id=1, source_target_pairs={{0,24},{1,25},{2,26},{3,27},{4,28},{5,29},{6,30},{7,31},{8,0},{9,1... | collective-permute-start | bytes 528392 | tf_op jit(solution)/shard_map/ppermute | solution.py:59
  125.8 10.9 %collective-permute-start.30 = (bf16[16,5504]{1,0:T(8,128)(2,1)S(1)}, bf16[16,5504]{1,0:T(8,128)(2,1)S(1)}, u32[]{:S(2)}, u32[]{:S(2)}) collective-permute-start(bf16[16,5504]{1,0:T(8,128)(2,1)S(1)} %get-tuple-element.168), channel_id=1, source_target_pairs={{0,4},{1,5},{2,6},{3,7},{4,0},{5,1},{6,2},{7,3},{8,12},{9,13},{10,... | collective-permute-start | bytes 528392 | tf_op jit(solution)/shard_map/ppermute | solution.py:59
  125.9 11.8 %collective-permute-start.32 = (bf16[16,5504]{1,0:T(8,128)(2,1)S(1)}, bf16[16,5504]{1,0:T(8,128)(2,1)S(1)}, u32[]{:S(2)}, u32[]{:S(2)}) collective-permute-start(bf16[16,5504]{1,0:T(8,128)(2,1)S(1)} %get-tuple-element.169.refs_9_), channel_id=1, source_target_pairs={{0,1},{1,0},{2,3},{3,2},{4,5},{5,4},{6,7},{7,6},{8,9},{9,8},{10,11... | collective-permute-start | bytes 528392 | tf_op jit(solution)/shard_map/ppermute | solution.py:59
  127.0 11.2 %collective-permute-start.31 = (bf16[16,5504]{1,0:T(8,128)(2,1)S(1)}, bf16[16,5504]{1,0:T(8,128)(2,1)S(1)}, u32[]{:S(2)}, u32[]{:S(2)}) collective-permute-start(bf16[16,5504]{1,0:T(8,128)(2,1)S(1)} %get-tuple-element.169.refs_9_), channel_id=1, source_target_pairs={{0,2},{1,3},{2,0},{3,1},{4,6},{5,7},{6,4},{7,5},{8,10},{9,11},{10,... | collective-permute-start | bytes 528392 | tf_op jit(solution)/shard_map/ppermute | solution.py:59
  128.4 15.9 %collective-permute-start.33 = (bf16[16,5504]{1,0:T(8,128)(2,1)S(1)}, bf16[16,5504]{1,0:T(8,128)(2,1)S(1)}, u32[]{:S(2)}, u32[]{:S(2)}) collective-permute-start(bf16[16,5504]{1,0:T(8,128)(2,1)S(1)} %add_convert_fusion.1), channel_id=1, source_target_pairs={{0,4},{1,5},{2,6},{3,7},{4,0},{5,1},{6,2},{7,3},{8,12},{9,13},{10,... | collective-permute-start | bytes 528392 | tf_op jit(solution)/shard_map/ppermute | solution.py:59
  130.7 14.6 %collective-permute-start.34 = (bf16[16,5504]{1,0:T(8,128)(2,1)S(1)}, bf16[16,5504]{1,0:T(8,128)(2,1)S(1)}, u32[]{:S(2)}, u32[]{:S(2)}) collective-permute-start(bf16[16,5504]{1,0:T(8,128)(2,1)S(1)} %get-tuple-element.176), channel_id=1, source_target_pairs={{0,2},{1,3},{2,0},{3,1},{4,6},{5,7},{6,4},{7,5},{8,10},{9,11},{10,... | collective-permute-start | bytes 528392 | tf_op jit(solution)/shard_map/ppermute | solution.py:59
  136.7 8.6 %collective-permute-start.35 = (bf16[16,5504]{1,0:T(8,128)(2,1)S(1)}, bf16[16,5504]{1,0:T(8,128)(2,1)S(1)}, u32[]{:S(2)}, u32[]{:S(2)}) collective-permute-start(bf16[16,5504]{1,0:T(8,128)(2,1)S(1)} %get-tuple-element.177), channel_id=1, source_target_pairs={{0,1},{1,0},{2,3},{3,2},{4,5},{5,4},{6,7},{7,6},{8,9},{9,8},{10,11... | collective-permute-start | bytes 528392 | tf_op jit(solution)/shard_map/ppermute | solution.py:59
  144.3 6.4 %collective-permute-start.37 = (bf16[16,5504]{1,0:T(8,128)(2,1)S(1)}, bf16[16,5504]{1,0:T(8,128)(2,1)S(1)}, u32[]{:S(2)}, u32[]{:S(2)}) collective-permute-start(bf16[16,5504]{1,0:T(8,128)(2,1)S(1)} %collective-permute-done.30.refs_9_), channel_id=1, source_target_pairs={{0,1},{1,0},{2,3},{3,2},{4,5},{5,4},{6,7},{7,6},{8,9},{9,8},{10,11... | collective-permute-start | bytes 528392 | tf_op jit(solution)/shard_map/ppermute | solution.py:59
  145.2 6.1 %collective-permute-start.36 = (bf16[16,5504]{1,0:T(8,128)(2,1)S(1)}, bf16[16,5504]{1,0:T(8,128)(2,1)S(1)}, u32[]{:S(2)}, u32[]{:S(2)}) collective-permute-start(bf16[16,5504]{1,0:T(8,128)(2,1)S(1)} %collective-permute-done.30.refs_9_), channel_id=1, source_target_pairs={{0,2},{1,3},{2,0},{3,1},{4,6},{5,7},{6,4},{7,5},{8,10},{9,11},{10,... | collective-permute-start | bytes 528392 | tf_op jit(solution)/shard_map/ppermute | solution.py:59
  153.4 5.5 %collective-permute-start.38 = (bf16[16,5504]{1,0:T(8,128)(2,1)S(1)}, bf16[16,5504]{1,0:T(8,128)(2,1)S(1)}, u32[]{:S(2)}, u32[]{:S(2)}) collective-permute-start(bf16[16,5504]{1,0:T(8,128)(2,1)S(1)} %get-tuple-element.193), channel_id=1, source_target_pairs={{0,2},{1,3},{2,0},{3,1},{4,6},{5,7},{6,4},{7,5},{8,10},{9,11},{10,... | collective-permute-start | bytes 528392 | tf_op jit(solution)/shard_map/ppermute | solution.py:59
  153.7 5.5 %collective-permute-start.39 = (bf16[16,5504]{1,0:T(8,128)(2,1)S(1)}, bf16[16,5504]{1,0:T(8,128)(2,1)S(1)}, u32[]{:S(2)}, u32[]{:S(2)}) collective-permute-start(bf16[16,5504]{1,0:T(8,128)(2,1)S(1)} %get-tuple-element.194), channel_id=1, source_target_pairs={{0,1},{1,0},{2,3},{3,2},{4,5},{5,4},{6,7},{7,6},{8,9},{9,8},{10,11... | collective-permute-start | bytes 528392 | tf_op jit(solution)/shard_map/ppermute | solution.py:59
  159.3 9.3 %collective-permute-start.40 = (bf16[16,5504]{1,0:T(8,128)(2,1)S(1)}, bf16[16,5504]{1,0:T(8,128)(2,1)S(1)}, u32[]{:S(2)}, u32[]{:S(2)}) collective-permute-start(bf16[16,5504]{1,0:T(8,128)(2,1)S(1)} %add_convert_fusion), channel_id=1, source_target_pairs={{0,4},{1,5},{2,6},{3,7},{4,0},{5,1},{6,2},{7,3},{8,12},{9,13},{10,... | collective-permute-start | bytes 528392 | tf_op jit(solution)/shard_map/ppermute | solution.py:59
  161.8 6.8 %collective-permute-start.41 = (bf16[16,5504]{1,0:T(8,128)(2,1)S(1)}, bf16[16,5504]{1,0:T(8,128)(2,1)S(1)}, u32[]{:S(2)}, u32[]{:S(2)}) collective-permute-start(bf16[16,5504]{1,0:T(8,128)(2,1)S(1)} %get-tuple-element.197.refs_11_), channel_id=1, source_target_pairs={{0,2},{1,3},{2,0},{3,1},{4,6},{5,7},{6,4},{7,5},{8,10},{9,11},{10,... | collective-permute-start | bytes 528392 | tf_op jit(solution)/shard_map/ppermute | solution.py:59
  162.1 6.6 %collective-permute-start.42 = (bf16[16,5504]{1,0:T(8,128)(2,1)S(1)}, bf16[16,5504]{1,0:T(8,128)(2,1)S(1)}, u32[]{:S(2)}, u32[]{:S(2)}) collective-permute-start(bf16[16,5504]{1,0:T(8,128)(2,1)S(1)} %get-tuple-element.198), channel_id=1, source_target_pairs={{0,1},{1,0},{2,3},{3,2},{4,5},{5,4},{6,7},{7,6},{8,9},{9,8},{10,11... | collective-permute-start | bytes 528392 | tf_op jit(solution)/shard_map/ppermute | solution.py:59
  (1 other events, 2.3 us)
